TPU v7x, 128 devices: a whole 4x4x4 slice. The times are simulated.
128 devices in a mesh: dp: 8 (over x, z_lo), seq: 8 (over y, core), tensor: 2 (over z_hi).
Axes of the slice: x: 4, y: 4, z: 4 (z_hi: 2, z_lo: 2; z = z_hi * 2 + z_lo), core: 2. Of those that a mesh axis runs over, the one named last changes fastest.
Arguments:
- tokens: bfloat16 [8, 2048, 1024], P('dp', 'seq'), may hold values from -6 to 6
- cotangent: bfloat16 [8, 2048, 1024], P('dp', 'seq'), may hold values from -6 to 6
- positions: int32 [8, 2048], P('dp', 'seq'), may hold values from 0 to 2047, as said below
- segments: int32 [8, 2048], P('dp', 'seq'), may hold values from 0 to 3, as said below
- attention_gain: bfloat16 [1024], replicated, may hold values from 0.5 to 1.5
- query_weight: bfloat16 [1024, 2048], P(None, 'tensor'), may hold values from -0.1875 to 0.1875
- key_weight: bfloat16 [1024, 1024], P(None, 'tensor'), may hold values from -0.1875 to 0.1875
- value_weight: bfloat16 [1024, 1024], P(None, 'tensor'), may hold values from -0.1875 to 0.1875
- query_gain: bfloat16 [128], replicated, may hold values from 0.796875 to 1.796875
- key_gain: bfloat16 [128], replicated, may hold values from 0.796875 to 1.796875
- out_weight: bfloat16 [2048, 1024], P('tensor'), may hold values from -0.75 to 0.75
- mlp_gain: bfloat16 [1024], replicated, may hold values from 0.5 to 1.5
- gate_weight: bfloat16 [1024, 3072], P(None, 'tensor'), may hold values from -0.1875 to 0.1875
- up_weight: bfloat16 [1024, 3072], P(None, 'tensor'), may hold values from -0.1875 to 0.1875
- down_weight: bfloat16 [3072, 1024], P('tensor'), may hold values from -0.109375 to 0.109375
Outputs:
- output: bfloat16 [8, 2048, 1024], P('dp', 'seq')
- input_grad: bfloat16 [8, 2048, 1024], P('dp', 'seq')
- grad_query: float32 [1024, 2048], P(('dp', 'seq'), 'tensor')
- grad_key: float32 [1024, 1024], P(('dp', 'seq'), 'tensor')
- grad_value: float32 [1024, 1024], P(('dp', 'seq'), 'tensor')
- grad_out: float32 [2048, 1024], P('tensor', ('dp', 'seq'))
- grad_gate: float32 [1024, 3072], P(('dp', 'seq'), 'tensor')
- grad_up: float32 [1024, 3072], P(('dp', 'seq'), 'tensor')
- grad_down: float32 [3072, 1024], P('tensor', ('dp', 'seq'))
- grad_attention_gain: float32 [1024], P(('dp', 'seq'))
- grad_mlp_gain: float32 [1024], P(('dp', 'seq'))
- grad_query_gain: float32 [128], P(('dp', 'seq'))
- grad_key_gain: float32 [128], P(('dp', 'seq'))
Inputs may be any that keep to these rules, and one draw needn't show every extreme that they name: In each sequence the positions are a permutation of 0 to 2047; the rows of the device at index j of seq are two runs of 128 consecutive positions, the runs numbered c and 2 n - 1 - c of the sequence's 2 n runs, with n the devices of seq and c depending on j. `segments`: document numbers never fall along increasing positions and rise by at most one from one position to the next; every sequence holds four documents.
All inputs are finite; a program needn't handle non-finite values.
Results may differ from a plain program's by a relative error of at most 0.03.
Values may be sent and summed in bfloat16 or wider, within the bound.
A program may use at most 128 MiB of HBM per device.

v0:
```python
import math

import jax
import jax.numpy as jnp
from jax import lax
from jax.sharding import PartitionSpec as P

EPS = 1e-06
ROPE_BASE = 1000000.0
NEGATIVE = -1e30


def mean_rms(entries):
    return lax.rsqrt(jnp.mean(entries * entries, axis=-1, keepdims=True) + EPS)


def norm_back(entries, gain_vec, gradient):
    inverse = mean_rms(entries)
    scaled = gradient * gain_vec
    gain_grad = jnp.sum((gradient * entries * inverse).reshape(-1, entries.shape[-1]), axis=0)
    entries_grad = inverse * scaled - entries * inverse**3 * jnp.mean(
        scaled * entries, axis=-1, keepdims=True
    )
    return (entries_grad, gain_grad)


def rope_tables(token_place, head_dim):
    half_dim = head_dim // 2
    inverse = 1.0 / ROPE_BASE ** (jnp.arange(half_dim, dtype=jnp.float32) * 2.0 / head_dim)
    angles = token_place.astype(jnp.float32)[:, None] * inverse[None, :]
    return (jnp.cos(angles), jnp.sin(angles))


def rotate(entries, cosine_table, sine_table):
    half_dim = entries.shape[-1] // 2
    front_half = entries[..., :half_dim]
    back_half = entries[..., half_dim:]
    cosine = cosine_table[:, None, :]
    sine = sine_table[:, None, :]
    return jnp.concatenate(
        [front_half * cosine - back_half * sine, back_half * cosine + front_half * sine], axis=-1
    )


def unrotate(gradient, cosine_table, sine_table):
    half_dim = gradient.shape[-1] // 2
    front_half = gradient[..., :half_dim]
    back_half = gradient[..., half_dim:]
    cosine = cosine_table[:, None, :]
    sine = sine_table[:, None, :]
    return jnp.concatenate(
        [front_half * cosine + back_half * sine, back_half * cosine - front_half * sine], axis=-1
    )


def dense(left, right):
    return jnp.dot(left, right, preferred_element_type=jnp.float32)


def shards(
    tokens,
    cotangent,
    positions,
    segments,
    attention_gain,
    query_weight,
    key_weight,
    value_weight,
    query_gain,
    key_gain,
    out_weight,
    mlp_gain,
    gate_weight,
    up_weight,
    down_weight,
):
    head_dim = query_gain.shape[0]
    local_rows = tokens.shape[1]
    key_heads = key_weight.shape[1] // head_dim
    query_heads = query_weight.shape[1] // head_dim
    groups = query_heads // key_heads
    block_rows = min(512, local_rows)
    block_count = local_rows // block_rows
    score_scale = 1.0 / math.sqrt(head_dim)
    attention_gain = attention_gain.astype(jnp.float32)
    mlp_gain = mlp_gain.astype(jnp.float32)
    query_gain = query_gain.astype(jnp.float32)
    key_gain = key_gain.astype(jnp.float32)
    inputs = tokens[0].astype(jnp.float32)
    token_place = positions[0]
    segment = segments[0]
    cosine_table, sine_table = rope_tables(token_place, head_dim)
    normed = (inputs * mean_rms(inputs) * attention_gain).astype(jnp.bfloat16)
    query_raw = dense(normed, query_weight).reshape(local_rows, query_heads, head_dim)
    key_raw = dense(normed, key_weight).reshape(local_rows, key_heads, head_dim)
    value_low = (
        dense(normed, value_weight).astype(jnp.bfloat16).reshape(local_rows, key_heads, head_dim)
    )
    query_low = rotate(
        query_raw * mean_rms(query_raw) * query_gain, cosine_table, sine_table
    ).astype(jnp.bfloat16)
    key_low = rotate(key_raw * mean_rms(key_raw) * key_gain, cosine_table, sine_table).astype(
        jnp.bfloat16
    )
    key_local = key_low.transpose(1, 0, 2)
    value_local = value_low.transpose(1, 0, 2)
    key_all, value_all, place_all, segment_all = (
        lax.all_gather(key_local, "seq", axis=1, tiled=True),
        lax.all_gather(value_local, "seq", axis=1, tiled=True),
        lax.all_gather(token_place, "seq", axis=0, tiled=True),
        lax.all_gather(segment, "seq", axis=0, tiled=True),
    )
    query_blocks = query_low.reshape(
        block_count, block_rows, key_heads, groups, head_dim
    ).transpose(2, 0, 3, 1, 4)
    place_blocks = token_place.reshape(block_count, block_rows)
    segment_blocks = segment.reshape(block_count, block_rows)

    def block_mask(query_place, query_segment, key_place, key_segment):
        return (key_place[None, :] <= query_place[:, None]) & (
            key_segment[None, :] == query_segment[:, None]
        )

    def forward_head(element):
        query_head, key_head, value_head = element

        def forward_block(pieces):
            query_block, query_place, query_segment = pieces
            scores = (
                jnp.einsum("gbd,td->gbt", query_block, key_head, preferred_element_type=jnp.float32)
                * score_scale
            )
            allowed = block_mask(query_place, query_segment, place_all, segment_all)[None]
            scores = jnp.where(allowed, scores, NEGATIVE)
            largest = jnp.max(scores, axis=-1, keepdims=True)
            exponent = jnp.exp(scores - largest)
            row_total = jnp.sum(exponent, axis=-1, keepdims=True)
            attend = (exponent / row_total).astype(jnp.bfloat16)
            attended = jnp.einsum(
                "gbt,td->gbd", attend, value_head, preferred_element_type=jnp.float32
            )
            return (attended, largest[..., 0] + jnp.log(row_total[..., 0]))

        return lax.map(forward_block, (query_head, place_blocks, segment_blocks))

    attended, log_total = lax.map(forward_head, (query_blocks, key_all, value_all))
    attended_low = (
        attended.transpose(1, 3, 0, 2, 4)
        .reshape(local_rows, query_heads * head_dim)
        .astype(jnp.bfloat16)
    )
    attention_out = lax.psum(dense(attended_low, out_weight), "tensor")
    middle = inputs + attention_out
    normed_mlp = (middle * mean_rms(middle) * mlp_gain).astype(jnp.bfloat16)
    gate_value = dense(normed_mlp, gate_weight)
    up_value = dense(normed_mlp, up_weight)
    sigmoid_gate = jax.nn.sigmoid(gate_value)
    activated = (gate_value * sigmoid_gate * up_value).astype(jnp.bfloat16)
    mlp_out = lax.psum(dense(activated, down_weight).astype(jnp.bfloat16), "tensor").astype(
        jnp.float32
    )
    output = (middle + mlp_out).astype(jnp.bfloat16)[None]
    upstream = cotangent[0]
    grad_down = dense(activated.T, upstream)
    grad_act = dense(upstream, down_weight.T)
    gate_grad_low = (
        grad_act * up_value * sigmoid_gate * (1.0 + gate_value * (1.0 - sigmoid_gate))
    ).astype(jnp.bfloat16)
    up_grad_low = (grad_act * gate_value * sigmoid_gate).astype(jnp.bfloat16)
    grad_gate = dense(normed_mlp.T, gate_grad_low)
    grad_up = dense(normed_mlp.T, up_grad_low)
    mlp_partial = dense(gate_grad_low, gate_weight.T) + dense(up_grad_low, up_weight.T)
    mlp_normed_grad = lax.psum(mlp_partial.astype(jnp.bfloat16), "tensor").astype(jnp.float32)
    middle_part, mlp_gain_grad = norm_back(middle, mlp_gain, mlp_normed_grad)
    grad_middle = upstream.astype(jnp.float32) + middle_part
    middle_low = grad_middle.astype(jnp.bfloat16)
    grad_out = dense(attended_low.T, middle_low)
    attended_grad_low = dense(middle_low, out_weight.T).astype(jnp.bfloat16)
    grad_blocks = attended_grad_low.reshape(
        block_count, block_rows, key_heads, groups, head_dim
    ).transpose(2, 0, 3, 1, 4)
    key_use, value_use, place_use, segment_use = (key_all, value_all, place_all, segment_all)

    def backward_head(element):
        query_head, grad_head, total_head, key_head, value_head = element

        def backward_block(carried, pieces):
            key_sum, value_sum = carried
            query_block, grad_block, total_block, query_place, query_segment = pieces
            scores = (
                jnp.einsum("gbd,td->gbt", query_block, key_head, preferred_element_type=jnp.float32)
                * score_scale
            )
            allowed = block_mask(query_place, query_segment, place_use, segment_use)[None]
            attend = jnp.where(allowed, jnp.exp(scores - total_block[..., None]), 0.0)
            attend_low = attend.astype(jnp.bfloat16)
            grad_attend = jnp.einsum(
                "gbd,td->gbt", grad_block, value_head, preferred_element_type=jnp.float32
            )
            inner_sum = jnp.sum(attend * grad_attend, axis=-1, keepdims=True)
            scores_grad = (attend * (grad_attend - inner_sum)).astype(jnp.bfloat16)
            query_grad = (
                jnp.einsum("gbt,td->gbd", scores_grad, key_head, preferred_element_type=jnp.float32)
                * score_scale
            )
            key_sum = (
                key_sum
                + jnp.einsum(
                    "gbt,gbd->td", scores_grad, query_block, preferred_element_type=jnp.float32
                )
                * score_scale
            )
            value_sum = value_sum + jnp.einsum(
                "gbt,gbd->td", attend_low, grad_block, preferred_element_type=jnp.float32
            )
            return ((key_sum, value_sum), query_grad)

        initial = jnp.zeros(key_head.shape, jnp.float32)
        sums, query_grad = lax.scan(
            backward_block,
            (initial, initial),
            (query_head, grad_head, total_head, place_blocks, segment_blocks),
        )
        return (query_grad, sums[0], sums[1])

    query_grad_blocks, key_grad_all, value_grad_all = lax.map(
        backward_head, (query_blocks, grad_blocks, log_total, key_use, value_use)
    )
    key_grad, value_grad = (
        lax.psum_scatter(
            key_grad_all.astype(jnp.bfloat16), "seq", scatter_dimension=1, tiled=True
        ).astype(jnp.float32),
        lax.psum_scatter(
            value_grad_all.astype(jnp.bfloat16), "seq", scatter_dimension=1, tiled=True
        ).astype(jnp.float32),
    )
    query_rot_grad = query_grad_blocks.transpose(1, 3, 0, 2, 4).reshape(
        local_rows, query_heads, head_dim
    )
    query_raw_grad, query_gain_part = norm_back(
        query_raw, query_gain, unrotate(query_rot_grad, cosine_table, sine_table)
    )
    key_raw_grad, key_gain_part = norm_back(
        key_raw, key_gain, unrotate(key_grad.transpose(1, 0, 2), cosine_table, sine_table)
    )
    query_grad_low = query_raw_grad.reshape(local_rows, query_heads * head_dim).astype(jnp.bfloat16)
    key_grad_low = key_raw_grad.reshape(local_rows, key_heads * head_dim).astype(jnp.bfloat16)
    value_grad_low = (
        value_grad.transpose(1, 0, 2).reshape(local_rows, key_heads * head_dim).astype(jnp.bfloat16)
    )
    grad_query = dense(normed.T, query_grad_low)
    grad_key = dense(normed.T, key_grad_low)
    grad_value = dense(normed.T, value_grad_low)
    attention_partial = (
        dense(query_grad_low, query_weight.T)
        + dense(key_grad_low, key_weight.T)
        + dense(value_grad_low, value_weight.T)
    )
    normed_grad, query_gain_grad, key_gain_grad = (
        lax.psum(attention_partial.astype(jnp.bfloat16), "tensor").astype(jnp.float32),
        lax.psum(query_gain_part.astype(jnp.bfloat16), "tensor").astype(jnp.float32),
        lax.psum(key_gain_part.astype(jnp.bfloat16), "tensor").astype(jnp.float32),
    )
    input_part, attention_gain_grad = norm_back(inputs, attention_gain, normed_grad)
    input_grad = (grad_middle + input_part).astype(jnp.bfloat16)[None]
    gradients = (
        grad_query,
        grad_key,
        grad_value,
        grad_out,
        grad_gate,
        grad_up,
        grad_down,
        attention_gain_grad,
        mlp_gain_grad,
        query_gain_grad,
        key_gain_grad,
    )
    shares = (
        lax.psum_scatter(gradients[0], ("dp", "seq"), scatter_dimension=0, tiled=True),
        lax.psum_scatter(gradients[1], ("dp", "seq"), scatter_dimension=0, tiled=True),
        lax.psum_scatter(gradients[2], ("dp", "seq"), scatter_dimension=0, tiled=True),
        lax.psum_scatter(gradients[3], ("dp", "seq"), scatter_dimension=1, tiled=True),
        lax.psum_scatter(gradients[4], ("dp", "seq"), scatter_dimension=0, tiled=True),
        lax.psum_scatter(gradients[5], ("dp", "seq"), scatter_dimension=0, tiled=True),
        lax.psum_scatter(gradients[6], ("dp", "seq"), scatter_dimension=1, tiled=True),
        lax.psum_scatter(gradients[7], ("dp", "seq"), scatter_dimension=0, tiled=True),
        lax.psum_scatter(gradients[8], ("dp", "seq"), scatter_dimension=0, tiled=True),
        lax.psum_scatter(gradients[9], ("dp", "seq"), scatter_dimension=0, tiled=True),
        lax.psum_scatter(gradients[10], ("dp", "seq"), scatter_dimension=0, tiled=True),
    )
    return (
        output,
        input_grad,
        shares[0],
        shares[1],
        shares[2],
        shares[3],
        shares[4],
        shares[5],
        shares[6],
        shares[7],
        shares[8],
        shares[9],
        shares[10],
    )


def solution(mesh):
    return jax.shard_map(
        shards,
        mesh=mesh,
        in_specs=(
            P("dp", "seq", None),
            P("dp", "seq", None),
            P("dp", "seq"),
            P("dp", "seq"),
            P(),
            P(None, "tensor"),
            P(None, "tensor"),
            P(None, "tensor"),
            P(),
            P(),
            P("tensor", None),
            P(),
            P(None, "tensor"),
            P(None, "tensor"),
            P("tensor", None),
        ),
        out_specs=(
            P("dp", "seq", None),
            P("dp", "seq", None),
            P(("dp", "seq"), "tensor"),
            P(("dp", "seq"), "tensor"),
            P(("dp", "seq"), "tensor"),
            P("tensor", ("dp", "seq")),
            P(("dp", "seq"), "tensor"),
            P(("dp", "seq"), "tensor"),
            P("tensor", ("dp", "seq")),
            P(("dp", "seq")),
            P(("dp", "seq")),
            P(("dp", "seq")),
            P(("dp", "seq")),
        ),
        check_vma=False,
    )
```

profile of v0, /device:TPU:0, one launch (start us, length us, event | category | flops | bytes accessed | tf_op | source)
XLA Modules:
  0.0 2451.1 jit_solution(14941699949892705448)
XLA Ops:
  18.9 3.9 copy.70
  30.5 10.9 all-gather
  41.4 8.3 all-gather.1
  52.0 4.0 copy.61
  56.0 17.9 all-gather.7.cloned.1.call-done
  73.9 28.1 %while.10 = (s32[]{:T(128)}, bf16[4,1,2,256,128]{3,4,2,0,1:T(8,128)(2,1)}, f32[4,1,2,256]{3,2,1,0:T(2,128)S(1)}, s32[2048]{0:T(1024)S(1)}, s32[1,256]{1,0:T(1,12...) while((s32[]{:T(128)}, ...), condition=%wide.region_6.7_spmd, body=%wide.region_3.6_spmd.sunk | while | flops 551026176 | bytes 16158833 | solution.py:146
  102.0 3.5 fusion.100
  105.8 48.4 %all-reduce.11.cloned.1.call-done = f32[256,1024]{1,0:T(8,128)} async-done(((f32[256,1024]{1,0:T(8,128)}), f32[256,1024]{1,0:T(8,128)}) %all-reduce.11.cloned.1.call-update) | async-done | bytes 1048592 | tf_op jit(solution)/shard_map/psum | solution.py:152
  165.2 36.0 %all-reduce.13.cloned.1.call-done = bf16[256,1024]{1,0:T(8,128)(2,1)} async-done(((bf16[256,1024]{1,0:T(8,128)(2,1)}), bf16[256,1024]{1,0:T(8,128)(2,1)}) %all-reduce.13.cloned.1.call-update) | async-done | bytes 524304 | tf_op jit(solution)/shard_map/psum | solution.py:173
  211.3 82.1 %while.27 = (s32[]{:T(128)}, f32[4,1,2,256,128]{4,3,2,1,0:T(8,128)}, bf16[4,2048,128]{1,2,0:T(8,128)(2,1)}, bf16[4,2048,128]{1,2,0:T(8,128)(2,1)}, s32[2048]{0:T...) while((s32[]{:T(128)}, ...), condition=%wide.region_14.15_spmd, body=%wide.region_12.14_spmd.sunk | while | flops 1353776640 | bytes 65831648 | solution.py:226
  228.3 3.5 fusion.174
  248.8 3.5 fusion.174
  269.3 3.5 fusion.174
  289.8 3.5 fusion.174
  304.7 21.6 reduce-scatter.10.cloned.1.call-done
  329.6 31.5 %reduce-scatter.12.cloned.1.call-done = bf16[4,256,128]{1,2,0:T(8,128)(2,1)} async-done(((bf16[4,2048,128]{1,2,0:T(8,128)(2,1)}), bf16[4,256,128]{1,2,0:T(8,128)(2,1)}) %reduce-scatter.12.cloned.1.call-update) | async-done | bytes 262160 | tf_op jit(solution)/shard_map/reduce_scatter | solution.py:233
  364.0 4.2 fusion.91
  371.9 4.1 fusion.83
  380.0 5.0 fusion.105
  385.0 4.9 fusion.106
  390.0 4.9 fusion.75
  397.5 6.5 all-reduce.5
  404.0 7.5 all-reduce.15.cloned.1.call-done
  413.0 279.3 %all-reduce.4 = (f32[1024]{0:T(1024)S(1)}, f32[1024]{0:T(1024)S(1)}, f32[128]{0:T(128)S(1)}, f32[128]{0:T(128)S(1)}) all-reduce(f32[1024]{0:T(1024)S(1)} %get-tuple-element.284, f32[1024]{0:T(1024)S(1)} %get-tuple-element.280, ...), channel_id=13, replica_groups=mesh['dp'=8,'seq'=8,'tensor'=2] {'dp','seq'}, use_global_device_ids=true, to_apply=%region_29.30.clone | all-reduce | flops 2304 | bytes 17920
  694.6 3.4 fusion.72
  698.0 6.3 reduce-scatter.20.cloned.1.call-done
  704.4 285.6 %reduce-scatter.16.cloned.1.call-done = f32[16,512]{1,0:T(8,128)} async-done(((f32[1024,512]{1,0:T(8,128)}), f32[16,512]{1,0:T(8,128)}) %reduce-scatter.16.cloned.1.call-update) | async-done | bytes 32784 | tf_op jit(solution)/shard_map/reduce_scatter | solution.py:281
  990.0 289.5 %reduce-scatter.14.cloned.1.call-done = f32[16,1024]{1,0:T(8,128)} async-done(((f32[1024,1024]{1,0:T(8,128)}), f32[16,1024]{1,0:T(8,128)}) %reduce-scatter.14.cloned.1.call-update) | async-done | bytes 65552 | tf_op jit(solution)/shard_map/reduce_scatter | solution.py:280
  1279.6 285.7 %reduce-scatter.18.cloned.1.call-done = f32[16,512]{1,0:T(8,128)} async-done(((f32[1024,512]{1,0:T(8,128)}), f32[16,512]{1,0:T(8,128)}) %reduce-scatter.18.cloned.1.call-update) | async-done | bytes 32784 | tf_op jit(solution)/shard_map/reduce_scatter | solution.py:282
  1565.3 293.4 %reduce-scatter.22.cloned.1.call-done = f32[16,1536]{1,0:T(8,128)} async-done(((f32[1024,1536]{1,0:T(8,128)}), f32[16,1536]{1,0:T(8,128)}) %reduce-scatter.22.cloned.1.call-update) | async-done | bytes 98320 | tf_op jit(solution)/shard_map/reduce_scatter | solution.py:284
  1858.7 293.4 %reduce-scatter.24.cloned.1.call-done = f32[16,1536]{1,0:T(8,128)} async-done(((f32[1024,1536]{1,0:T(8,128)}), f32[16,1536]{1,0:T(8,128)}) %reduce-scatter.24.cloned.1.call-update) | async-done | bytes 98320 | tf_op jit(solution)/shard_map/reduce_scatter | solution.py:285
  2152.0 292.5 %reduce-scatter.26.cloned.1.call-done = f32[1536,16]{0,1:T(8,128)} async-done(((f32[1536,1024]{0,1:T(8,128)}), f32[1536,16]{0,1:T(8,128)}) %reduce-scatter.26.cloned.1.call-update) | async-done | bytes 98320 | tf_op jit(solution)/shard_map/reduce_scatter | solution.py:286
  (251 shorter events, 169.0 us)
Async XLA Ops:
  7.2 152.4 %copy-start = (bf16[1536,1024]{1,0:T(8,128)(2,1)S(1)}, bf16[1536,1024]{1,0:T(8,128)(2,1)}, u32[]{:S(2)}) copy-start(bf16[1536,1024]{1,0:T(8,128)(2,1)} %param.33) | copy-start | bytes 9437188
  7.2 44.9 %all-gather.5.cloned.1.call-start = ((), (), s32[]{:S(2)}) async-start(), calls=%async_computation.9 | async-start | bytes 2359296 | tf_op jit(solution)/shard_map/all_gather | solution.py:108
  9.2 13.7 copy-start.27
  9.9 4.9 copy-start.38
  9.9 4.9 copy-start.23
  14.8 3.2 copy-start.25
  14.9 3.2 copy-start.32
  16.1 57.8 %all-gather.7.cloned.1.call-start = ((), (), s32[]{:S(2)}) async-start(), calls=%async_computation.10 | async-start | bytes 2359296 | tf_op jit(solution)/shard_map/all_gather | solution.py:109
  18.9 135.3 %all-reduce.11.cloned.1.call-start = ((), (), s32[]{:S(2)}) async-start(), calls=%async_computation.11 | async-start | bytes 2097152 | tf_op jit(solution)/shard_map/psum | solution.py:152
  18.9 4.0 copy-start.39
  22.9 3.3 copy-start.34
  52.0 21.9 copy-start.24
  52.0 21.9 copy-start.31
  102.0 3.7 copy-start.37
  105.5 95.7 %all-reduce.13.cloned.1.call-start = ((), (), s32[]{:S(2)}) async-start(), calls=%async_computation.12 | async-start | bytes 1048576 | tf_op jit(solution)/shard_map/psum | solution.py:173
  165.1 161.2 %reduce-scatter.10.cloned.1.call-start = ((), (), s32[]{:S(2)}) async-start(), calls=%async_computation.13 | async-start | bytes 2359296 | tf_op jit(solution)/shard_map/reduce_scatter | solution.py:230
  201.2 4.4 copy-start.9
  211.3 2.4 copy-start.11
  293.4 67.7 %reduce-scatter.12.cloned.1.call-start = ((), (), s32[]{:S(2)}) async-start(), calls=%async_computation.14 | async-start | bytes 2359296 | tf_op jit(solution)/shard_map/reduce_scatter | solution.py:233
  294.0 117.5 %all-reduce.15.cloned.1.call-start = ((), (), s32[]{:S(2)}) async-start(), calls=%async_computation.22 | async-start | bytes 2097152 | tf_op jit(solution)/shard_map/psum | solution.py:159
  297.1 4.0 copy-start.35
  303.0 24.6 %copy-start.26 = (f32[256,4]{0,1:T(4,128)S(1)}, f32[256,4]{0,1:T(4,128)}, u32[]{:S(2)}) copy-start(f32[256,4]{0,1:T(4,128)} %copy-done.25) | copy-start | bytes 12292
  303.0 24.6 %copy-start.33 = (f32[128]{0:T(128)S(1)}, f32[128]{0:T(128)}, u32[]{:S(2)}) copy-start(f32[128]{0:T(128)} %copy-done.32) | copy-start | bytes 1540
  304.7 23.0 copy-start.30
  364.0 340.4 %reduce-scatter.20.cloned.1.call-start = ((), (), s32[]{:S(2)}) async-start(), calls=%async_computation.18 | async-start | bytes 4259840 | tf_op jit(solution)/shard_map/reduce_scatter | solution.py:283
  368.2 621.8 %reduce-scatter.16.cloned.1.call-start = ((), (), s32[]{:S(2)}) async-start(), calls=%async_computation.16 | async-start | bytes 2129920 | tf_op jit(solution)/shard_map/reduce_scatter | solution.py:281
  371.9 907.7 %reduce-scatter.14.cloned.1.call-start = ((), (), s32[]{:S(2)}) async-start(), calls=%async_computation.15 | async-start | bytes 4259840 | tf_op jit(solution)/shard_map/reduce_scatter | solution.py:280
  376.0 1189.3 %reduce-scatter.18.cloned.1.call-start = ((), (), s32[]{:S(2)}) async-start(), calls=%async_computation.17 | async-start | bytes 2129920 | tf_op jit(solution)/shard_map/reduce_scatter | solution.py:282
  379.9 1478.7 %reduce-scatter.22.cloned.1.call-start = ((), (), s32[]{:S(2)}) async-start(), calls=%async_computation.19 | async-start | bytes 6389760 | tf_op jit(solution)/shard_map/reduce_scatter | solution.py:284
  385.0 1767.1 %reduce-scatter.24.cloned.1.call-start = ((), (), s32[]{:S(2)}) async-start(), calls=%async_computation.20 | async-start | bytes 6389760 | tf_op jit(solution)/shard_map/reduce_scatter | solution.py:285
  390.0 2054.6 %reduce-scatter.26.cloned.1.call-start = ((), (), s32[]{:S(2)}) async-start(), calls=%async_computation.21 | async-start | bytes 6389760 | tf_op jit(solution)/shard_map/reduce_scatter | solution.py:286
  394.9 299.7 %copy-start.36 = (f32[256]{0:T(256)S(1)}, f32[256]{0:T(256)}, u32[]{:S(2)}) copy-start(f32[256]{0:T(256)} %get-tuple-element.363) | copy-start | bytes 3076
  (32 other events, 48.2 us)
Sparse Core Ops, SparseCore 0:
  16.3 29.7 all-gather.4
  47.7 26.1 all-gather.6
  105.6 48.4 all-reduce.10
  165.2 35.9 all-reduce.12
  293.5 32.7 reduce-scatter.9
  328.6 32.4 reduce-scatter.11
  364.1 47.3 all-reduce.14
  414.5 289.8 reduce-scatter.19
  707.3 282.6 reduce-scatter.15
  992.9 286.5 reduce-scatter.13
  1282.5 282.7 reduce-scatter.17
  1568.2 290.3 reduce-scatter.21
  1861.6 290.3 reduce-scatter.23
  2155.0 289.5 reduce-scatter.25
where the time goes:
time: 2450 us
  waiting for transfers between devices  1910 us (78%)
  blocking collectives  305 us (12%)
  matrix products  129 us (5%)
  local copies, waits for them, and re-layouts  57.4 us (2%)
  other arithmetic  33 us (1%)
    reduce_scatter x1, waiting for transfers between devices, shards(): lax.psum_scatter(gradients[4], ('dp', 'seq'), scatter_dimension=0, tiled=...  293 us
    reduce_scatter x1, waiting for transfers between devices, shards(): lax.psum_scatter(gradients[5], ('dp', 'seq'), scatter_dimension=0, tiled=...  293 us
    reduce_scatter x1, waiting for transfers between devices, shards(): lax.psum_scatter(gradients[6], ('dp', 'seq'), scatter_dimension=1, tiled=...  293 us
    reduce_scatter x1, waiting for transfers between devices, shards(): lax.psum_scatter(gradients[0], ('dp', 'seq'), scatter_dimension=0, tiled=...  290 us
    reduce_scatter x1, waiting for transfers between devices, shards(): lax.psum_scatter(gradients[2], ('dp', 'seq'), scatter_dimension=0, tiled=...  286 us
    reduce_scatter x1, waiting for transfers between devices, shards(): lax.psum_scatter(gradients[1], ('dp', 'seq'), scatter_dimension=0, tiled=...  286 us
    unnamed x1, blocking collectives  279 us
    dot_general x21, matrix products, dense(): return jnp.dot(left, right, preferred_element_type=jnp.float32)  56.7 us
  transfers between devices with their start and end apart: 14, of which 13 were waited for; matrix products, arithmetic and copies ran while one was open for 3% of the time, Pallas kernels for 0%

commit v1 on v0

--- a/solution.py
+++ b/solution.py
@@ -1,13 +1,267 @@
+import functools
 import math
 
 import jax
 import jax.numpy as jnp
 from jax import lax
+from jax.experimental import pallas as pl
+from jax.experimental.pallas import tpu as pltpu
 from jax.sharding import PartitionSpec as P
 
 EPS = 1e-06
 ROPE_BASE = 1000000.0
 NEGATIVE = -1e30
+
+
+MESH = pl.DeviceIdType.MESH
+CHUNK = 16
+DIMS = ("x3", "x1", "y3", "y1", "z")
+LOW = jnp.bfloat16
+
+
+def place():
+    dp = lax.axis_index("dp")
+    seq = lax.axis_index("seq")
+    tensor = lax.axis_index("tensor")
+    x, z = dp // 2, dp % 2
+    y, core = seq // 2, seq % 2
+    x_near = x + 1 - 2 * (x % 2)
+    y_near = y + 1 - 2 * (y % 2)
+    bits = {
+        "core": core,
+        "x3": x // 2,
+        "x1": (x // 2 + x % 2) % 2,
+        "y3": y // 2,
+        "y1": (y // 2 + y % 2) % 2,
+        "z": z,
+    }
+    partners = {
+        "core": (dp, seq + 1 - 2 * core, tensor),
+        "x3": ((3 - x) * 2 + z, seq, tensor),
+        "x1": (x_near * 2 + z, seq, tensor),
+        "y3": (dp, (3 - y) * 2 + core, tensor),
+        "y1": (dp, y_near * 2 + core, tensor),
+        "z": (dp + 1 - 2 * z, seq, tensor),
+        "tensor": (dp, seq, 1 - tensor),
+    }
+    return bits, partners
+
+
+def greet(partners):
+    barrier = pltpu.get_barrier_semaphore()
+    for partner in partners:
+        pl.semaphore_signal(barrier, inc=1, device_id=partner, device_id_type=MESH)
+    pl.semaphore_wait(barrier, len(partners))
+
+
+def stream_order(stream):
+    return ("core",) + tuple(DIMS[(stream + i) % len(DIMS)] for i in range(len(DIMS)))
+
+
+def slot_chunks(order):
+    chunks = []
+    for slot in range(2 ** len(order)):
+        bit = {d: (slot >> (len(order) - 1 - i)) & 1 for i, d in enumerate(order)}
+        x = 2 * bit["x3"] + (bit["x3"] ^ bit["x1"])
+        y = 2 * bit["y3"] + (bit["y3"] ^ bit["y1"])
+        chunks.append(((x * 2 + bit["z"]) * 4 + y) * 2 + bit["core"])
+    return chunks
+
+
+def scatter_kernel(pieces, n_lhs, n_rhs, *refs):
+    streams = len(pieces)
+    lhs = refs[:n_lhs]
+    rhs = refs[n_lhs : n_lhs + n_rhs]
+    gains_in, partial_in = refs[n_lhs + n_rhs : n_lhs + n_rhs + 2]
+    refs = refs[n_lhs + n_rhs + 2 :]
+    outs = refs[:streams]
+    gains_out, partial_out = refs[streams : streams + 2]
+    refs = refs[streams + 2 :]
+    turned, sent, held = refs[:3]
+    landed = refs[3:9]
+    gains_held = refs[9]
+    gains_landed = refs[10:16]
+    gains_last, gains_sum, send_sem, recv_sem, gains_send, gains_recv, pair_send, pair_recv = refs[16:]
+    bits, partners = place()
+    greet(list(partners.values()))
+
+    def exchange(source, target, out_sem, in_sem, partner):
+        return pltpu.make_async_remote_copy(
+            src_ref=source,
+            dst_ref=target,
+            send_sem=out_sem,
+            recv_sem=in_sem,
+            device_id=partner,
+            device_id_type=MESH,
+        )
+
+    partial_copy = exchange(
+        partial_in, partial_out, pair_send.at[0], pair_recv.at[0], partners["tensor"]
+    )
+    partial_copy.start()
+    orders = [stream_order(s) for s in range(streams)]
+    features = lhs[0].shape[1]
+    half = features // 2
+    core = bits["core"]
+    block = 128
+    copies = {}
+    used = []
+    for s in range(streams):
+        for left, right, first, columns in pieces[s]:
+            flipped = lhs[left][...].T
+            index = len(used)
+            used.append((s, left, right, first, columns))
+            for slot, chunk in enumerate(slot_chunks(orders[s])):
+                turned[index, slot * CHUNK : (slot + 1) * CHUNK, :] = flipped[
+                    chunk * CHUNK : (chunk + 1) * CHUNK, :
+                ]
+
+    def product(s, target, offset):
+        for index, (stream, _, right, first, columns) in enumerate(used):
+            if stream != s:
+                continue
+
+            def rows(i, _, index=index, right=right, first=first, columns=columns):
+                start = pl.multiple_of(i * block, block)
+                from_row = pl.multiple_of(offset + start, block)
+                target[s, pl.ds(start, block), first : first + columns] = jnp.dot(
+                    turned[index, pl.ds(from_row, block), :],
+                    rhs[right][...],
+                    preferred_element_type=jnp.float32,
+                ).astype(LOW)
+                return 0
+
+            lax.fori_loop(0, half // block, rows, 0)
+
+    for s in range(streams):
+        product(s, sent, (1 - core) * half)
+        copies[s, 0] = exchange(
+            sent.at[s], landed[0].at[s], send_sem.at[s, 0], recv_sem.at[s, 0], partners["core"]
+        )
+        copies[s, 0].start()
+    gain_chunks = gains_in.shape[0]
+    gains_copy = [None] * 6
+    gains_copy[0] = exchange(
+        gains_in.at[pl.ds((1 - core) * (gain_chunks // 2), gain_chunks // 2)],
+        gains_landed[0],
+        gains_send.at[0],
+        gains_recv.at[0],
+        partners["core"],
+    )
+    gains_copy[0].start()
+    for s in range(streams):
+        product(s, held, core * half)
+    gains_held[...] = gains_in[pl.ds(core * (gain_chunks // 2), gain_chunks // 2)]
+
+    base = [0] * streams
+    gains_base = 0
+    for step in range(6):
+        rows = half >> step
+        for s in range(streams):
+            copies[s, step].wait()
+            if step == 5:
+                mine = pl.multiple_of(base[s], CHUNK)
+                outs[s][...] = held[s, pl.ds(mine, CHUNK), :].astype(jnp.float32) + landed[5][
+                    s
+                ].astype(jnp.float32)
+                continue
+            tile = min(rows, 64)
+
+            def add(i, _, s=s, step=step, tile=tile):
+                start = pl.multiple_of(i * tile, tile)
+                here = pl.multiple_of(base[s] + start, tile)
+                held[s, pl.ds(here, tile), :] = (
+                    held[s, pl.ds(here, tile), :] + landed[step][s, pl.ds(start, tile), :]
+                )
+                return 0
+
+            lax.fori_loop(0, rows // tile, add, 0)
+            dim = orders[s][step + 1]
+            bit = bits[dim]
+            away = pl.multiple_of(base[s] + (1 - bit) * (rows // 2), CHUNK)
+            copies[s, step + 1] = exchange(
+                held.at[s, pl.ds(away, rows // 2), :],
+                landed[step + 1].at[s],
+                send_sem.at[s, step + 1],
+                recv_sem.at[s, step + 1],
+                partners[dim],
+            )
+            copies[s, step + 1].start()
+            base[s] = base[s] + bit * (rows // 2)
+        chunks = gain_chunks >> (step + 1)
+        gains_copy[step].wait()
+        gains_held[pl.ds(gains_base, chunks)] = (
+            gains_held[pl.ds(gains_base, chunks)] + gains_landed[step][...]
+        )
+        if step < 5:
+            dim = orders[0][step + 1]
+            bit = bits[dim]
+            gains_copy[step + 1] = exchange(
+                gains_held.at[pl.ds(gains_base + (1 - bit) * (chunks // 2), chunks // 2)],
+                gains_landed[step + 1],
+                gains_send.at[step + 1],
+                gains_recv.at[step + 1],
+                partners[dim],
+            )
+            gains_copy[step + 1].start()
+            gains_base = gains_base + bit * (chunks // 2)
+    gains_last[...] = gains_held[pl.ds(gains_base, 1)]
+    last = exchange(gains_last, gains_sum, pair_send.at[1], pair_recv.at[1], partners["tensor"])
+    last.start()
+    last.wait()
+    gains_out[...] = gains_last[0] + gains_sum[0]
+    partial_copy.wait()
+
+
+def scatter_gradients(pieces, lhs, rhs, gains, partial):
+    streams = len(pieces)
+    width = sum(columns for _, _, _, columns in pieces[0])
+    tokens, features = lhs[0].shape
+    half = features // 2
+    parts = sum(len(p) for p in pieces)
+    chunks = features // CHUNK
+    vmem = pl.BlockSpec(memory_space=pltpu.VMEM)
+    landed = [pltpu.VMEM((streams, half >> step, width), LOW) for step in range(6)]
+    gains_landed = [pltpu.VMEM((chunks >> (step + 1), 8, 128), jnp.float32) for step in range(6)]
+    result = pl.pallas_call(
+        functools.partial(scatter_kernel, pieces, len(lhs), len(rhs)),
+        out_shape=[jax.ShapeDtypeStruct((CHUNK, width), jnp.float32)] * streams
+        + [
+            jax.ShapeDtypeStruct((8, 128), jnp.float32),
+            jax.ShapeDtypeStruct(partial.shape, partial.dtype),
+        ],
+        in_specs=[vmem] * (len(lhs) + len(rhs) + 2),
+        out_specs=[vmem] * (streams + 2),
+        scratch_shapes=[
+            pltpu.VMEM((parts, features, tokens), LOW),
+            pltpu.VMEM((streams, half, width), LOW),
+            pltpu.VMEM((streams, half, width), LOW),
+            *landed,
+            pltpu.VMEM((chunks // 2, 8, 128), jnp.float32),
+            *gains_landed,
+            pltpu.VMEM((1, 8, 128), jnp.float32),
+            pltpu.VMEM((1, 8, 128), jnp.float32),
+            pltpu.SemaphoreType.DMA((streams, 6)),
+            pltpu.SemaphoreType.DMA((streams, 6)),
+            pltpu.SemaphoreType.DMA((6,)),
+            pltpu.SemaphoreType.DMA((6,)),
+            pltpu.SemaphoreType.DMA((2,)),
+            pltpu.SemaphoreType.DMA((2,)),
+        ],
+        compiler_params=pltpu.CompilerParams(
+            collective_id=0, has_side_effects=True, vmem_limit_bytes=60 * 1024 * 1024
+        ),
+    )(*lhs, *rhs, gains, partial)
+    return result[:streams], result[streams], result[streams + 1]
+
+
+def pack_gains(attention, mlp, query, key):
+    chunks = attention.shape[0] // CHUNK
+    packed = jnp.concatenate(
+        [entry.reshape(chunks, -1) for entry in (attention, mlp, query, key)], axis=1
+    )
+    ordered = packed[jnp.array(slot_chunks(stream_order(0)))]
+    return jnp.pad(ordered[:, None, :], ((0, 0), (0, 7), (0, 128 - ordered.shape[1])))
 
 
 def mean_rms(entries):
@@ -161,20 +415,16 @@
     )
     output = (middle + mlp_out).astype(jnp.bfloat16)[None]
     upstream = cotangent[0]
-    grad_down = dense(activated.T, upstream)
     grad_act = dense(upstream, down_weight.T)
     gate_grad_low = (
         grad_act * up_value * sigmoid_gate * (1.0 + gate_value * (1.0 - sigmoid_gate))
     ).astype(jnp.bfloat16)
     up_grad_low = (grad_act * gate_value * sigmoid_gate).astype(jnp.bfloat16)
-    grad_gate = dense(normed_mlp.T, gate_grad_low)
-    grad_up = dense(normed_mlp.T, up_grad_low)
     mlp_partial = dense(gate_grad_low, gate_weight.T) + dense(up_grad_low, up_weight.T)
     mlp_normed_grad = lax.psum(mlp_partial.astype(jnp.bfloat16), "tensor").astype(jnp.float32)
     middle_part, mlp_gain_grad = norm_back(middle, mlp_gain, mlp_normed_grad)
     grad_middle = upstream.astype(jnp.float32) + middle_part
     middle_low = grad_middle.astype(jnp.bfloat16)
-    grad_out = dense(attended_low.T, middle_low)
     attended_grad_low = dense(middle_low, out_weight.T).astype(jnp.bfloat16)
     grad_blocks = attended_grad_low.reshape(
         block_count, block_rows, key_heads, groups, head_dim
@@ -248,61 +498,53 @@
     value_grad_low = (
         value_grad.transpose(1, 0, 2).reshape(local_rows, key_heads * head_dim).astype(jnp.bfloat16)
     )
-    grad_query = dense(normed.T, query_grad_low)
-    grad_key = dense(normed.T, key_grad_low)
-    grad_value = dense(normed.T, value_grad_low)
     attention_partial = (
         dense(query_grad_low, query_weight.T)
         + dense(key_grad_low, key_weight.T)
         + dense(value_grad_low, value_weight.T)
     )
-    normed_grad, query_gain_grad, key_gain_grad = (
-        lax.psum(attention_partial.astype(jnp.bfloat16), "tensor").astype(jnp.float32),
-        lax.psum(query_gain_part.astype(jnp.bfloat16), "tensor").astype(jnp.float32),
-        lax.psum(key_gain_part.astype(jnp.bfloat16), "tensor").astype(jnp.float32),
-    )
-    input_part, attention_gain_grad = norm_back(inputs, attention_gain, normed_grad)
+    attention_gain_part = jnp.sum(attention_partial * inputs * mean_rms(inputs), axis=0)
+    width = gate_weight.shape[1]
+    q_width, k_width = query_weight.shape[1], key_weight.shape[1]
+    pieces = (
+        ((0, 0, 0, width),),
+        ((0, 1, 0, width),),
+        ((1, 2, 0, width),),
+        ((2, 3, 0, q_width), (2, 4, q_width, k_width)),
+        ((2, 5, 0, k_width), (3, 6, k_width, q_width)),
+    )
+    shares, gains, partial_other = scatter_gradients(
+        pieces,
+        (normed_mlp, upstream, normed, middle_low),
+        (
+            gate_grad_low,
+            up_grad_low,
+            activated,
+            query_grad_low,
+            key_grad_low,
+            value_grad_low,
+            attended_low,
+        ),
+        pack_gains(attention_gain_part, 0.5 * mlp_gain_grad, query_gain_part, key_gain_part),
+        attention_partial.astype(jnp.bfloat16),
+    )
+    normed_grad = attention_partial + partial_other.astype(jnp.float32)
+    input_part, _ = norm_back(inputs, attention_gain, normed_grad)
     input_grad = (grad_middle + input_part).astype(jnp.bfloat16)[None]
-    gradients = (
-        grad_query,
-        grad_key,
-        grad_value,
-        grad_out,
-        grad_gate,
-        grad_up,
-        grad_down,
-        attention_gain_grad,
-        mlp_gain_grad,
-        query_gain_grad,
-        key_gain_grad,
-    )
-    shares = (
-        lax.psum_scatter(gradients[0], ("dp", "seq"), scatter_dimension=0, tiled=True),
-        lax.psum_scatter(gradients[1], ("dp", "seq"), scatter_dimension=0, tiled=True),
-        lax.psum_scatter(gradients[2], ("dp", "seq"), scatter_dimension=0, tiled=True),
-        lax.psum_scatter(gradients[3], ("dp", "seq"), scatter_dimension=1, tiled=True),
-        lax.psum_scatter(gradients[4], ("dp", "seq"), scatter_dimension=0, tiled=True),
-        lax.psum_scatter(gradients[5], ("dp", "seq"), scatter_dimension=0, tiled=True),
-        lax.psum_scatter(gradients[6], ("dp", "seq"), scatter_dimension=1, tiled=True),
-        lax.psum_scatter(gradients[7], ("dp", "seq"), scatter_dimension=0, tiled=True),
-        lax.psum_scatter(gradients[8], ("dp", "seq"), scatter_dimension=0, tiled=True),
-        lax.psum_scatter(gradients[9], ("dp", "seq"), scatter_dimension=0, tiled=True),
-        lax.psum_scatter(gradients[10], ("dp", "seq"), scatter_dimension=0, tiled=True),
-    )
     return (
         output,
         input_grad,
+        shares[3][:, :q_width],
+        shares[3][:, q_width:],
+        shares[4][:, :k_width],
+        shares[4][:, k_width:].T,
         shares[0],
         shares[1],
-        shares[2],
-        shares[3],
-        shares[4],
-        shares[5],
-        shares[6],
-        shares[7],
-        shares[8],
-        shares[9],
-        shares[10],
+        shares[2].T,
+        gains[0, 0:16],
+        gains[0, 16:32],
+        gains[0, 32:34],
+        gains[0, 34:36],
     )
 
 

time: 2450 us -> 456 us (0.19)
  waiting for transfers between devices: 1910 us -> 165 us
  blocking collectives: 305 us -> 19 us
  Pallas kernels: 0 us -> 70 us
  matrix products: 129 us -> 97.7 us
    reduce_scatter x7 -> x0, waiting for transfers between devices: 1750 us -> none  [the longest x1 293 us: shards(): lax.psum_scatter(gradients[4], ('dp', 'seq'), scatter_dimension=0, tiled=...]
    unnamed x1 -> x0, blocking collectives: 279 us -> none
    pallas_call x0 -> x1, Pallas kernels: none -> 70 us  [scatter_gradients(): pl.pallas_call(functools.partial(scatter_kernel, pieces, len(lhs), len(rh...]
    psum x1, waiting for transfers between devices: 7.5 us -> 47.7 us  [shards(): lax.psum(dense(activated, down_weight).astype(jnp.bfloat16), 'tensor')]
    psum x1 -> x0, waiting for transfers between devices: 36 us -> none  [shards(): lax.psum(mlp_partial.astype(jnp.bfloat16), 'tensor').astype(jnp.float32)]
    dot_general x21 -> x14, matrix products: 56.7 us -> 26 us  [dense(): return jnp.dot(left, right, preferred_element_type=jnp.float32)]
  transfers between devices with their start and end apart: 14 -> 6, of which waited for: 13 -> 5; matrix products, arithmetic and copies ran while one was open for 3% -> 7% of each run, Pallas kernels for 0% -> 0%
where the time goes in v1:
time: 456 us; the launch traced here: 454 us
  waiting for transfers between devices  165 us (36%)
  matrix products  97.7 us (21%)
  Pallas kernels  70 us (15%)
  local copies, waits for them, and re-layouts  50.5 us (11%)
  other arithmetic  35.6 us (8%)
  blocking collectives  19 us (4%)
  between operations  14.8 us (3%)
    pallas_call x1, Pallas kernels, scatter_gradients(): pl.pallas_call(functools.partial(scatter_kernel, pieces, len(lhs), len(rh...  70 us
    psum x1, waiting for transfers between devices, shards(): attention_out = lax.psum(dense(attended_low, out_weight), 'tensor')  48.4 us
    psum x1, waiting for transfers between devices, shards(): lax.psum(dense(activated, down_weight).astype(jnp.bfloat16), 'tensor')  47.7 us
    reduce_scatter x1, waiting for transfers between devices, shards(): lax.psum_scatter(value_grad_all.astype(jnp.bfloat16), 'seq', scatter_dime...  30.6 us
    dot_general x14, matrix products, dense(): return jnp.dot(left, right, preferred_element_type=jnp.float32)  26 us
    reduce_scatter x1, waiting for transfers between devices, shards(): lax.psum_scatter(key_grad_all.astype(jnp.bfloat16), 'seq', scatter_dimens...  22.5 us
    all_gather x1, waiting for transfers between devices, shards(): lax.all_gather(value_local, 'seq', axis=1, tiled=True)  15.4 us
    dot_general x4, matrix products, backward_block(): jnp.einsum('gbt,gbd->td', attend_low, grad_block, preferred_element_type=...  15.2 us
  transfers between devices with their start and end apart: 6, of which 5 were waited for; matrix products, arithmetic and copies ran while one was open for 7% of the time, Pallas kernels for 0%

profile of v1, /device:TPU:0, one launch (start us, length us, event | category | flops | bytes accessed | tf_op | source)
XLA Modules:
  0.0 453.7 jit_solution(9026708337115688303)
XLA Ops:
  21.5 4.0 copy.63
  25.5 2.6 multiply_reduce_fusion.4
  33.2 10.9 %all-gather = s32[1,2048]{1,0:T(1,128)S(1)} all-gather(s32[1,256]{1,0:T(1,128)S(1)} %copy-done.35), channel_id=2, replica_groups=mesh['dp'=8,'seq'=8,'tensor'=2] {'seq'}, dimensions={1}, use_global_device_ids=true | all-gather | bytes 9216 | tf_op jit(solution)/shard_map/all_gather | solution.py:364
  44.0 8.1 %all-gather.1 = s32[1,2048]{1,0:T(1,128)S(1)} all-gather(s32[1,256]{1,0:T(1,128)S(1)} %copy-done.36), channel_id=3, replica_groups=mesh['dp'=8,'seq'=8,'tensor'=2] {'seq'}, dimensions={1}, use_global_device_ids=true | all-gather | bytes 9216 | tf_op jit(solution)/shard_map/all_gather | solution.py:365
  55.3 4.0 copy.52
  59.3 15.4 %all-gather.7.cloned.1.call-done = bf16[4,2048,128]{2,1,0:T(8,128)(2,1)} async-done(((bf16[4,256,128]{2,1,0:T(8,128)(2,1)}), bf16[4,2048,128]{2,1,0:T(8,128)(2,1)}) %all-gather.7.cloned.1.call-update) | async-done | bytes 2097168 | tf_op jit(solution)/shard_map/all_gather | solution.py:363
  74.7 28.1 %while.28 = (s32[]{:T(128)}, bf16[4,1,2,256,128]{4,3,2,1,0:T(8,128)(2,1)}, f32[4,1,2,256]{3,2,1,0:T(2,128)S(1)}, s32[2048]{0:T(1024)S(1)}, s32[1,256]{1,0:T(1,12...) while((s32[]{:T(128)}, ...), condition=%wide.region_6.7_spmd.clone, body=%wide.region_3.6_spmd.sunk.clone | while | flops 551026176 | bytes 16158825 | solution.py:400
  78.7 3.1 fusion.152
  85.7 3.1 fusion.152
  92.8 3.1 fusion.152
  99.8 3.1 fusion.152
  107.4 3.5 fusion.82
  111.2 48.4 %all-reduce.5.cloned.1.call-done = f32[256,1024]{1,0:T(8,128)} async-done(((f32[256,1024]{1,0:T(8,128)}), f32[256,1024]{1,0:T(8,128)}) %all-reduce.5.cloned.1.call-update) | async-done | bytes 1048592 | tf_op jit(solution)/shard_map/psum | solution.py:406
  171.5 47.7 %all-reduce.7.cloned.1.call-done = (bf16[256,1024]{1,0:T(8,128)(2,1)}, bf16[256,1024]{1,0:T(8,128)(2,1)}) async-done(((bf16[256,1024]{1,0:T(8,128)(2,1)}, bf16[256,1024]{1,0:T(8,128)(2,1)}), (bf16[256,1024]{1,0:T(8,128)(2,1)}, bf16[256,1024]{1,0:T(8,128)(2,1)})) %all-reduce.7.cloned.1.call-update) | async-done | bytes 1048592 | tf_op jit(solution)/shard_map/psum | solution.py:413
  223.4 65.1 %while.29 = (s32[]{:T(128)}, f32[4,1,2,256,128]{4,3,2,1,0:T(8,128)}, bf16[4,2048,128]{1,2,0:T(8,128)(2,1)}, bf16[4,2048,128]{2,1,0:T(8,128)(2,1)}, s32[2048]{0:T...) while((s32[]{:T(128)}, ...), condition=%wide.region_14.15_spmd.clone, body=%wide.region_12.14_spmd.sunk.clone | while | flops 1353776640 | bytes 59540692 | solution.py:476
  225.9 2.8 multiply_reduce_fusion.10
  235.9 3.8 fusion.165
  242.2 2.8 multiply_reduce_fusion.10
  249.7 2.5 fusion.163
  252.2 3.8 fusion.165
  258.5 2.8 multiply_reduce_fusion.10
  266.0 2.5 fusion.163
  268.4 3.8 fusion.165
  274.7 2.8 multiply_reduce_fusion.10
  282.2 2.5 fusion.163
  284.7 3.8 fusion.165
  296.2 2.9 fusion.86
  299.1 22.5 %reduce-scatter.3.cloned.1.call-done = bf16[4,256,128]{1,2,0:T(8,128)(2,1)} async-done(((bf16[4,2048,128]{1,2,0:T(8,128)(2,1)}), bf16[4,256,128]{1,2,0:T(8,128)(2,1)}) %reduce-scatter.3.cloned.1.call-update) | async-done | bytes 262160 | tf_op jit(solution)/shard_map/reduce_scatter | solution.py:480
  325.6 30.6 %reduce-scatter.5.cloned.1.call-done = bf16[4,256,128]{2,1,0:T(8,128)(2,1)} async-done(((bf16[4,2048,128]{2,1,0:T(8,128)(2,1)}), bf16[4,256,128]{2,1,0:T(8,128)(2,1)}) %reduce-scatter.5.cloned.1.call-update) | async-done | bytes 262160 | tf_op jit(solution)/shard_map/reduce_scatter | solution.py:483
  356.3 3.0 fusion.81
  361.7 70.0 %shard_map.255 = (f32[16,1536]{1,0:T(8,128)}, f32[16,1536]{1,0:T(8,128)}, f32[16,1536]{1,0:T(8,128)}, f32[16,1536]{1,0:T(8,128)}, f32[16,1536]{1,0:T(8,128)}, /*...) custom-call(bf16[256,1024]{1,0:T(8,128)(2,1)} %copy-done.12, bf16[256,1024]{1,0:T(8,128)(2,1)} %bitcast.284, ...), custom_call_target="tpu_custom_call" | custom-call | tf_op jit(solution)/shard_map/pallas_call | solution.py:226
  441.7 3.3 fusion.72
  (272 shorter events, 115.7 us)
Async XLA Ops:
  7.2 157.8 %copy-start = (bf16[1536,1024]{1,0:T(8,128)(2,1)S(1)}, bf16[1536,1024]{1,0:T(8,128)(2,1)}, u32[]{:S(2)}) copy-start(bf16[1536,1024]{1,0:T(8,128)(2,1)} %param.34) | copy-start | bytes 9437188
  7.2 48.1 %all-gather.5.cloned.1.call-start = ((), (), s32[]{:S(2)}) async-start(), calls=%async_computation.2 | async-start | bytes 2359296 | tf_op jit(solution)/shard_map/all_gather | solution.py:362
  9.2 16.3 %copy-start.46 = (f32[256]{0:T(256)}, f32[256]{0:T(256)S(1)}, u32[]{:S(2)}) copy-start(f32[256]{0:T(256)S(1)} %get-tuple-element.355) | copy-start | bytes 3076
  9.9 15.6 %copy-start.42 = (f32[1024]{0:T(1024)}, f32[1024]{0:T(1024)S(1)}, u32[]{:S(2)}) copy-start(f32[1024]{0:T(1024)S(1)} %convert_element_type.140) | copy-start | bytes 12292
  10.6 4.9 %copy-start.56 = (bf16[128]{0:T(256)(128)(2,1)S(1)}, bf16[128]{0:T(256)(128)(2,1)}, u32[]{:S(2)}) copy-start(bf16[128]{0:T(256)(128)(2,1)} %param.29) | copy-start | bytes 772
  17.0 57.8 %all-gather.7.cloned.1.call-start = ((), (), s32[]{:S(2)}) async-start(), calls=%async_computation.3 | async-start | bytes 2359296 | tf_op jit(solution)/shard_map/all_gather | solution.py:363
  21.5 138.1 %all-reduce.5.cloned.1.call-start = ((), (), s32[]{:S(2)}) async-start(), calls=%async_computation.4 | async-start | bytes 2097152 | tf_op jit(solution)/shard_map/psum | solution.py:406
  21.5 4.0 copy-start.57
  29.3 14.7 %copy-start.36 = (s32[1,256]{1,0:T(1,128)S(1)}, s32[1,256]{1,0:T(1,128)}, u32[]{:S(2)}) copy-start(s32[1,256]{1,0:T(1,128)} %param.23) | copy-start | bytes 3076
  55.3 19.4 %copy-start.48 = (f32[4,1,2,256]{3,2,1,0:T(2,128)S(1)}, f32[4,1,2,256]{3,2,1,0:T(2,128)}, u32[]{:S(2)}) copy-start(f32[4,1,2,256]{3,2,1,0:T(2,128)} %custom-call.2) | copy-start | bytes 24580
  110.9 108.3 %all-reduce.7.cloned.1.call-start = ((), (), s32[]{:S(2)}) async-start(), calls=%async_computation.7 | async-start | bytes 2097152 | tf_op jit(solution)/shard_map/psum | solution.py:413
  169.6 49.6 %copy-start.4 = (f32[256,1024]{1,0:T(8,128)S(1)}, f32[256,1024]{1,0:T(8,128)}, u32[]{:S(2)}) copy-start(f32[256,1024]{1,0:T(8,128)} %copy-done.3) | copy-start | bytes 3145732
  171.4 49.3 %copy-start.22 = (bf16[1,256,1024]{2,1,0:T(8,128)(2,1)S(1)}, bf16[1,256,1024]{2,1,0:T(8,128)(2,1)}, u32[]{:S(2)}) copy-start(bf16[1,256,1024]{2,1,0:T(8,128)(2,1)} %param.21) | copy-start | bytes 1572868
  171.5 150.1 %reduce-scatter.3.cloned.1.call-start = ((), (), s32[]{:S(2)}) async-start(), calls=%async_computation.5 | async-start | bytes 2359296 | tf_op jit(solution)/shard_map/reduce_scatter | solution.py:480
  288.5 67.8 %reduce-scatter.5.cloned.1.call-start = ((), (), s32[]{:S(2)}) async-start(), calls=%async_computation.6 | async-start | bytes 2359296 | tf_op jit(solution)/shard_map/reduce_scatter | solution.py:483
  291.5 4.7 %copy-start.11 = (bf16[1024,1024]{1,0:T(8,128)(2,1)S(1)}, bf16[1024,1024]{1,0:T(8,128)(2,1)}, u32[]{:S(2)}) copy-start(bf16[1024,1024]{1,0:T(8,128)(2,1)} %param.25) | copy-start | bytes 6291460
  296.2 26.5 %copy-start.16 = (f32[256,4,128]{0,2,1:T(8,128)S(1)}, f32[256,4,128]{0,2,1:T(8,128)}, u32[]{:S(2)}) copy-start(f32[256,4,128]{0,2,1:T(8,128)} %copy-done.15) | copy-start | bytes 1572868
  296.2 26.5 %copy-start.41 = (f32[256,4]{0,1:T(4,128)S(1)}, f32[256,4]{0,1:T(4,128)}, u32[]{:S(2)}) copy-start(f32[256,4]{0,1:T(4,128)} %copy-done.40) | copy-start | bytes 12292
  296.2 26.5 %copy-start.50 = (f32[128]{0:T(128)S(1)}, f32[128]{0:T(128)}, u32[]{:S(2)}) copy-start(f32[128]{0:T(128)} %copy-done.49) | copy-start | bytes 1540
  299.1 23.8 %copy-start.45 = (f32[256,4]{0,1:T(4,128)S(1)}, f32[256,4]{0,1:T(4,128)}, u32[]{:S(2)}) copy-start(f32[256,4]{0,1:T(4,128)} %get-tuple-element.350) | copy-start | bytes 12292
  323.0 33.3 %copy-start.6 = (bf16[1,256,1024]{2,1,0:T(8,128)(2,1)S(1)}, bf16[1,256,1024]{2,1,0:T(8,128)(2,1)}, u32[]{:S(2)}) copy-start(bf16[1,256,1024]{2,1,0:T(8,128)(2,1)} %param.20) | copy-start | bytes 1572868
  323.0 33.3 %copy-start.47 = (f32[256]{0:T(256)S(1)}, f32[256]{0:T(256)}, u32[]{:S(2)}) copy-start(f32[256]{0:T(256)} %copy-done.46) | copy-start | bytes 3076
  356.3 4.6 %copy-start.30 = (bf16[4,256,128]{2,1,0:T(8,128)(2,1)S(1)}, bf16[4,256,128]{2,1,0:T(8,128)(2,1)}, u32[]{:S(2)}) copy-start(bf16[4,256,128]{2,1,0:T(8,128)(2,1)} %reduce-scatter.5.cloned.1.call-done) | copy-start | bytes 786436
  359.3 81.0 %copy-start.10 = (f32[256,1024]{1,0:T(8,128)}, f32[256,1024]{1,0:T(8,128)S(1)}, u32[]{:S(2)}) copy-start(f32[256,1024]{1,0:T(8,128)S(1)} %get-tuple-element.362) | copy-start | bytes 3145732
  361.6 78.6 %copy-start.43 = (f32[1024]{0:T(1024)S(1)}, f32[1024]{0:T(1024)}, u32[]{:S(2)}) copy-start(f32[1024]{0:T(1024)} %copy-done.42) | copy-start | bytes 12292
  361.7 79.9 %copy-start.23 = (bf16[1,256,1024]{2,1,0:T(8,128)(2,1)S(1)}, bf16[1,256,1024]{2,1,0:T(8,128)(2,1)}, u32[]{:S(2)}) copy-start(bf16[1,256,1024]{2,1,0:T(8,128)(2,1)} %param.21) | copy-start | bytes 1572868
  431.7 9.9 %copy-start.5 = (f32[256,1024]{1,0:T(8,128)S(1)}, f32[256,1024]{1,0:T(8,128)}, u32[]{:S(2)}) copy-start(f32[256,1024]{1,0:T(8,128)} %copy-done.3) | copy-start | bytes 3145732
  431.7 9.9 %copy-start.7 = (bf16[1,256,1024]{2,1,0:T(8,128)(2,1)S(1)}, bf16[1,256,1024]{2,1,0:T(8,128)(2,1)}, u32[]{:S(2)}) copy-start(bf16[1,256,1024]{2,1,0:T(8,128)(2,1)} %param.20) | copy-start | bytes 1572868
  431.7 9.9 %copy-start.17 = (bf16[256,1024]{1,0:T(8,128)(2,1)S(1)}, bf16[256,1024]{1,0:T(8,128)(2,1)}, u32[]{:S(2)}) copy-start(bf16[256,1024]{1,0:T(8,128)(2,1)} %get-tuple-element.322) | copy-start | bytes 1572868
  431.7 9.9 %copy-start.53 = (f32[256]{0:T(256)S(1)}, f32[256]{0:T(256)}, u32[]{:S(2)}) copy-start(f32[256]{0:T(256)} %get-tuple-element.354) | copy-start | bytes 3076
  441.6 5.3 %copy-start.1 = (bf16[1536,1024]{1,0:T(8,128)(2,1)S(1)}, bf16[1536,1024]{1,0:T(8,128)(2,1)}, u32[]{:S(2)}) copy-start(bf16[1536,1024]{1,0:T(8,128)(2,1)} %param.34) | copy-start | bytes 9437188
  441.7 4.6 %copy-start.37 = (f32[16,1536]{1,0:T(8,128)S(1)}, f32[16,1536]{1,0:T(8,128)}, u32[]{:S(2)}) copy-start(f32[16,1536]{1,0:T(8,128)} %get-tuple-element.221) | copy-start | bytes 294916
  (41 other events, 81.4 us)
Sparse Core Ops, SparseCore 0:
  17.1 29.7 all-gather.4
  48.6 26.1 all-gather.6
  111.0 48.4 all-reduce.4
  171.6 47.5 all-reduce.6
  288.7 32.8 reduce-scatter.2
  323.8 32.4 reduce-scatter.4

commit v2 on v1

--- a/solution.py
+++ b/solution.py
@@ -264,6 +264,489 @@
     return jnp.pad(ordered[:, None, :], ((0, 0), (0, 7), (0, 128 - ordered.shape[1])))
 
 
+def remote(source, target, out_sem, in_sem, partner):
+    return pltpu.make_async_remote_copy(
+        src_ref=source,
+        dst_ref=target,
+        send_sem=out_sem,
+        recv_sem=in_sem,
+        device_id=partner,
+        device_id_type=MESH,
+    )
+
+
+def over_tiles(count, body):
+    def step(i, _):
+        body(i)
+        return 0
+
+    lax.fori_loop(0, count, step, 0)
+
+
+def at_tile(i, size):
+    return pl.ds(pl.multiple_of(i * size, size), size)
+
+
+def times(left, right):
+    return jnp.dot(left, right, preferred_element_type=jnp.float32)
+
+
+def times_turned(left, right):
+    return lax.dot_general(
+        left, right, (((1,), (1,)), ((), ())), preferred_element_type=jnp.float32
+    )
+
+
+def inverse_rms(entries):
+    return lax.rsqrt(jnp.mean(entries * entries, axis=-1, keepdims=True) + EPS)
+
+
+def forward_kernel(
+    tokens,
+    cotangent,
+    positions,
+    segments,
+    frequencies,
+    attention_gain,
+    query_gain,
+    key_gain,
+    mlp_gain,
+    wq_far,
+    wk_far,
+    wv_far,
+    wo_far,
+    wg_far,
+    wu_far,
+    wd_far,
+    normed,
+    query_raw,
+    key_raw,
+    query,
+    kv,
+    meta,
+    cosine,
+    sine,
+    attended,
+    middle,
+    normed_mlp,
+    activated,
+    gate_grad,
+    up_grad,
+    mlp_out,
+    grad_middle,
+    middle_low,
+    attended_grad,
+    inner,
+    mlp_gain_grad,
+    wq,
+    wk,
+    wv,
+    wo,
+    wg,
+    wu,
+    wd,
+    bias,
+    total,
+    weight_sum,
+    act_grad,
+    part_out,
+    part_in,
+    weight_sem,
+    kv_send,
+    kv_recv,
+    meta_send,
+    meta_recv,
+    pair_send,
+    pair_recv,
+):
+    dp, seq, tensor = lax.axis_index("dp"), lax.axis_index("seq"), lax.axis_index("tensor")
+    core, y = seq % 2, seq // 2
+    after, before, across = (y + 1) % 4, (y + 3) % 4, (y + 2) % 4
+    near = (dp, y * 2 + 1 - core, tensor)
+    ahead = (dp, after * 2 + core, tensor)
+    behind = (dp, before * 2 + core, tensor)
+    pair = (dp, seq, 1 - tensor)
+    others = [(dp, (seq + step) % 8, tensor) for step in range(1, 8)]
+    rows = tokens.shape[0]
+    heads = kv.shape[2]
+    hd = kv.shape[4]
+    greet(others + [pair])
+    fetches = [
+        pltpu.make_async_copy(far, held, weight_sem.at[i])
+        for i, (far, held) in enumerate(
+            zip(
+                (wk_far, wv_far, wq_far, wo_far, wd_far, wg_far, wu_far),
+                (wk, wv, wq, wo, wd, wg, wu),
+            )
+        )
+    ]
+    for fetch in fetches:
+        fetch.start()
+    got_wk, got_wv, got_wq, got_wo, got_wd, got_wg, got_wu = fetches
+
+    meta[seq] = jnp.zeros_like(meta[seq])
+    meta[seq, 0:1, :] = positions[...]
+    meta[seq, 1:2, :] = segments[...]
+    metas = [
+        remote(meta.at[seq], meta.at[seq], meta_send.at[i], meta_recv.at[i], other)
+        for i, other in enumerate(others)
+    ]
+    for copy in metas:
+        copy.start()
+
+    place_rows = jnp.broadcast_to(positions[...].astype(jnp.float32), (rows, rows)).T
+    segment_rows = jnp.broadcast_to(segments[...].astype(jnp.float32), (rows, rows)).T
+    angle = place_rows[:, :hd] * frequencies[...]
+    cosine[...] = jnp.cos(angle)
+    lane = lax.broadcasted_iota(jnp.int32, (rows, hd), 1)
+    sine[...] = jnp.where(lane < hd // 2, -1.0, 1.0) * jnp.sin(angle)
+
+    def turn(entries):
+        return entries * cosine[...] + pltpu.roll(entries, hd // 2, 1) * sine[...]
+
+    x = tokens[...].astype(jnp.float32)
+    normed[...] = (x * inverse_rms(x) * attention_gain[...].astype(jnp.float32)).astype(LOW)
+
+    tile = 2 * hd
+    got_wk.wait()
+
+    def key_tile(i):
+        raw = times(normed[...], wk[:, at_tile(i, tile)])
+        key_raw[:, at_tile(i, tile)] = raw
+        for g in range(2):
+            head = raw[:, g * hd : (g + 1) * hd]
+            scaled = head * inverse_rms(head) * key_gain[...].astype(jnp.float32)
+            kv[seq, 0, 2 * i + g] = turn(scaled).astype(LOW)
+
+    over_tiles(heads // 2, key_tile)
+
+    def own(half, kind, target, index):
+        copy = remote(
+            kv.at[seq, half], kv.at[seq, half], kv_send.at[index], kv_recv.at[kind, half], target
+        )
+        copy.start()
+        return copy
+
+    sends = [own(0, 1, ahead, 0), own(0, 2, behind, 1), own(0, 0, near, 2)]
+    got_wv.wait()
+
+    def value_tile(i):
+        raw = times(normed[...], wv[:, at_tile(i, tile)]).astype(LOW)
+        for g in range(2):
+            kv[seq, 1, 2 * i + g] = raw[:, g * hd : (g + 1) * hd]
+
+    over_tiles(heads // 2, value_tile)
+    sends += [own(1, 1, ahead, 3), own(1, 2, behind, 4), own(1, 0, near, 5)]
+    got_wq.wait()
+    scale = math.log2(math.e) / math.sqrt(hd)
+
+    def query_tile(i):
+        raw = times(normed[...], wq[:, at_tile(i, tile)])
+        query_raw[:, at_tile(i, tile)] = raw
+        for g in range(2):
+            head = raw[:, g * hd : (g + 1) * hd]
+            scaled = head * inverse_rms(head) * (query_gain[...].astype(jnp.float32) * scale)
+            query[i, g * rows : (g + 1) * rows, :] = turn(scaled).astype(LOW)
+
+    over_tiles(heads, query_tile)
+    total[...] = jnp.zeros_like(total)
+    weight_sum[...] = jnp.zeros_like(weight_sum)
+    for copy in metas:
+        copy.wait()
+
+    def attend(slot):
+        key_place = meta[slot, 0:1, :].astype(jnp.float32)
+        key_segment = meta[slot, 1:2, :].astype(jnp.float32)
+        allowed = (key_place <= place_rows) & (key_segment == segment_rows)
+        bias[...] = jnp.where(allowed, 0.0, NEGATIVE)
+
+        def head(j):
+            scores = times_turned(query[j], kv[slot, 0, j])
+            weights = jnp.concatenate(
+                [jnp.exp2(scores[g * rows : (g + 1) * rows] + bias[...]) for g in range(2)], axis=0
+            )
+            weight_sum[j] += weights[:, :hd] + weights[:, hd:]
+            total[j] += times(weights.astype(LOW), kv[slot, 1, j])
+
+        over_tiles(heads, head)
+
+    def arrived(slot, kind, half):
+        remote(
+            kv.at[slot, half], kv.at[slot, half], kv_send.at[0], kv_recv.at[kind, half], near
+        ).wait_recv()
+
+    def pass_on(slot, half, kind, target, index):
+        copy = remote(
+            kv.at[slot, half], kv.at[slot, half], kv_send.at[index], kv_recv.at[kind, half], target
+        )
+        copy.start()
+        sends.append(copy)
+
+    attend(seq)
+    near_slot = y * 2 + 1 - core
+    arrived(near_slot, 0, 0)
+    arrived(near_slot, 0, 1)
+    attend(near_slot)
+    before_slot, after_slot, across_slot = before * 2 + core, after * 2 + core, across * 2 + core
+    arrived(before_slot, 1, 0)
+    pass_on(before_slot, 0, 3, ahead, 6)
+    pass_on(before_slot, 0, 4, near, 7)
+    arrived(after_slot, 2, 0)
+    pass_on(after_slot, 0, 5, near, 8)
+    arrived(after_slot, 2, 1)
+    pass_on(after_slot, 1, 3, behind, 9)
+    pass_on(after_slot, 1, 5, near, 10)
+    arrived(before_slot, 1, 1)
+    pass_on(before_slot, 1, 4, near, 11)
+    attend(before_slot)
+    attend(after_slot)
+    for far_y, kind in ((before, 4), (after, 5)):
+        slot = far_y * 2 + 1 - core
+        arrived(slot, kind, 0)
+        arrived(slot, kind, 1)
+        attend(slot)
+    arrived(across_slot, 3, 0)
+    pass_on(across_slot, 0, 6, near, 12)
+    arrived(across_slot, 3, 1)
+    pass_on(across_slot, 1, 6, near, 13)
+    attend(across_slot)
+    far_slot = across * 2 + 1 - core
+    arrived(far_slot, 6, 0)
+    arrived(far_slot, 6, 1)
+    attend(far_slot)
+
+    def finish(j):
+        inverse = 1.0 / jnp.sum(weight_sum[j], axis=-1, keepdims=True)
+        result = total[j] * inverse
+        total[j] = result
+        weight_sum[j] = jnp.broadcast_to(inverse, result.shape)
+        for g in range(2):
+            attended[:, at_tile(2 * j + g, hd)] = result[g * rows : (g + 1) * rows].astype(LOW)
+
+    over_tiles(heads, finish)
+    got_wo.wait()
+    wide = 256
+    features = tokens.shape[1]
+    hidden = wg.shape[1]
+
+    def out_tile(i):
+        part_out[0, :, at_tile(i, wide)] = times(attended[...], wo[:, at_tile(i, wide)]).astype(LOW)
+
+    over_tiles(features // wide, out_tile)
+    first = remote(part_out.at[0], part_in.at[0], pair_send.at[0], pair_recv.at[0], pair)
+    first.start()
+    got_wd.wait()
+
+    def act_grad_tile(i):
+        act_grad[:, at_tile(i, wide)] = times_turned(cotangent[...], wd[at_tile(i, wide), :])
+
+    over_tiles(hidden // wide, act_grad_tile)
+    got_wg.wait()
+    got_wu.wait()
+    first.wait()
+    mid = (
+        tokens[...].astype(jnp.float32)
+        + (part_out[0].astype(jnp.float32) + part_in[0].astype(jnp.float32))
+    )
+    middle[...] = mid
+    normed_mlp[...] = (mid * inverse_rms(mid) * mlp_gain[...].astype(jnp.float32)).astype(LOW)
+
+    def hidden_tile(i):
+        here = at_tile(i, wide)
+        gate_here = times(normed_mlp[...], wg[:, here])
+        up_here = times(normed_mlp[...], wu[:, here])
+        sigmoid = 1.0 / (1.0 + jnp.exp(-gate_here))
+        silu = gate_here * sigmoid
+        grad = act_grad[:, here]
+        activated[:, here] = (silu * up_here).astype(LOW)
+        gate_grad[:, here] = (
+            grad * up_here * sigmoid * (1.0 + gate_here * (1.0 - sigmoid))
+        ).astype(LOW)
+        up_grad[:, here] = (grad * silu).astype(LOW)
+
+    over_tiles(hidden // wide, hidden_tile)
+
+    def back_tile(i):
+        here = at_tile(i, wide)
+        part_out[1, :, here] = (
+            times_turned(gate_grad[...], wg[here, :]) + times_turned(up_grad[...], wu[here, :])
+        ).astype(LOW)
+
+    over_tiles(features // wide, back_tile)
+    second = remote(part_out.at[1], part_in.at[1], pair_send.at[1], pair_recv.at[1], pair)
+    second.start()
+
+    def down_tile(i):
+        mlp_out[:, at_tile(i, wide)] = times(activated[...], wd[:, at_tile(i, wide)]).astype(LOW)
+
+    over_tiles(features // wide, down_tile)
+    for copy in sends:
+        copy.wait_send()
+    second.wait()
+    mid = middle[...]
+    inverse = inverse_rms(mid)
+    dy = part_out[1].astype(jnp.float32) + part_in[1].astype(jnp.float32)
+    mlp_gain_grad[...] = jnp.sum(dy * mid * inverse, axis=0, keepdims=True)
+    scaled = dy * mlp_gain[...].astype(jnp.float32)
+    grad = (
+        cotangent[...].astype(jnp.float32)
+        + inverse * scaled
+        - mid * (inverse * inverse * inverse) * jnp.mean(scaled * mid, axis=-1, keepdims=True)
+    )
+    grad_middle[...] = grad
+    middle_low[...] = grad.astype(LOW)
+
+    def attended_grad_tile(j):
+        both = times_turned(middle_low[...], wo[at_tile(j, 2 * hd), :]).astype(LOW)
+        both = both.astype(jnp.float32)
+        for g in range(2):
+            here = slice(g * rows, (g + 1) * rows)
+            normal = both[:, g * hd : (g + 1) * hd] * weight_sum[j, here, :]
+            attended_grad[j, here, :] = normal.astype(LOW)
+            inner[j, here, :] = jnp.broadcast_to(
+                jnp.sum(normal * total[j, here, :], axis=-1, keepdims=True), (rows, hd)
+            )
+
+    over_tiles(heads, attended_grad_tile)
+
+
+def forward(
+    tokens, cotangent, positions, segments, attention_gain, query_weight, key_weight, value_weight,
+    query_gain, key_gain, out_weight, mlp_gain, gate_weight, up_weight, down_weight,
+):
+    rows, features = tokens.shape
+    hd = query_gain.shape[1]
+    heads = key_weight.shape[1] // hd
+    q_width, k_width, hidden = query_weight.shape[1], key_weight.shape[1], gate_weight.shape[1]
+    half = jnp.arange(hd // 2, dtype=jnp.float32)
+    inverse = 1.0 / ROPE_BASE ** (half * 2.0 / hd)
+    frequencies = jnp.concatenate([inverse, inverse])[None]
+    vmem = pl.BlockSpec(memory_space=pltpu.VMEM)
+    far = pl.BlockSpec(memory_space=pl.ANY)
+    f32 = jnp.float32
+    outs = dict(
+        normed=((rows, features), LOW),
+        query_raw=((rows, q_width), f32),
+        key_raw=((rows, k_width), f32),
+        query=((heads, 2 * rows, hd), LOW),
+        kv=((8, 2, heads, rows, hd), LOW),
+        meta=((8, 8, rows), jnp.int32),
+        cosine=((rows, hd), f32),
+        sine=((rows, hd), f32),
+        attended=((rows, q_width), LOW),
+        middle=((rows, features), f32),
+        normed_mlp=((rows, features), LOW),
+        activated=((rows, hidden), LOW),
+        gate_grad=((rows, hidden), LOW),
+        up_grad=((rows, hidden), LOW),
+        mlp_out=((rows, features), LOW),
+        grad_middle=((rows, features), f32),
+        middle_low=((rows, features), LOW),
+        attended_grad=((heads, 2 * rows, hd), LOW),
+        inner=((heads, 2 * rows, hd), f32),
+        mlp_gain_grad=((1, features), f32),
+    )
+    weights = (
+        query_weight, key_weight, value_weight, out_weight, gate_weight, up_weight, down_weight,
+    )
+    results = pl.pallas_call(
+        forward_kernel,
+        out_shape=[jax.ShapeDtypeStruct(shape, kind) for shape, kind in outs.values()],
+        in_specs=[vmem] * 9 + [far] * 7,
+        out_specs=[vmem] * len(outs),
+        scratch_shapes=[pltpu.VMEM(w.shape, LOW) for w in weights]
+        + [
+            pltpu.VMEM((rows, rows), f32),
+            pltpu.VMEM((heads, 2 * rows, hd), f32),
+            pltpu.VMEM((heads, 2 * rows, hd), f32),
+            pltpu.VMEM((rows, hidden), f32),
+            pltpu.VMEM((2, rows, features), LOW),
+            pltpu.VMEM((2, rows, features), LOW),
+            pltpu.SemaphoreType.DMA((7,)),
+            pltpu.SemaphoreType.DMA((14,)),
+            pltpu.SemaphoreType.DMA((7, 2)),
+            pltpu.SemaphoreType.DMA((7,)),
+            pltpu.SemaphoreType.DMA((7,)),
+            pltpu.SemaphoreType.DMA((2,)),
+            pltpu.SemaphoreType.DMA((2,)),
+        ],
+        compiler_params=pltpu.CompilerParams(
+            collective_id=1, has_side_effects=True, vmem_limit_bytes=60 * 1024 * 1024
+        ),
+    )(
+        tokens,
+        cotangent,
+        positions,
+        segments,
+        frequencies,
+        attention_gain,
+        query_gain,
+        key_gain,
+        mlp_gain,
+        *weights,
+    )
+    return dict(zip(outs, results))
+
+
+def backward_kernel(query, kv, meta, positions, segments, attended_grad, inner, query_grad, kv_grad, bias):
+    rows = positions.shape[1]
+    heads, hd = kv.shape[2], kv.shape[4]
+    place_rows = jnp.broadcast_to(positions[...].astype(jnp.float32), (rows, rows)).T
+    segment_rows = jnp.broadcast_to(segments[...].astype(jnp.float32), (rows, rows)).T
+    query_grad[...] = jnp.zeros_like(query_grad)
+
+    def block(slot):
+        key_place = meta[slot, 0:1, :].astype(jnp.float32)
+        key_segment = meta[slot, 1:2, :].astype(jnp.float32)
+        allowed = (key_place <= place_rows) & (key_segment == segment_rows)
+        bias[...] = jnp.where(allowed, 0.0, NEGATIVE)
+
+        def head(j):
+            key, value = kv[slot, 0, j], kv[slot, 1, j]
+            scores = times_turned(query[j], key)
+            grad = times_turned(attended_grad[j], value)
+            weights, scores_grad = [], []
+            for g in range(2):
+                here = slice(g * rows, (g + 1) * rows)
+                weight = jnp.exp2(scores[here] + bias[...])
+                inside = jnp.concatenate([inner[j, here, :]] * 2, axis=1)
+                weights.append(weight.astype(LOW))
+                scores_grad.append((weight * (grad[here] - inside)).astype(LOW))
+            weights = jnp.concatenate(weights, axis=0)
+            scores_grad = jnp.concatenate(scores_grad, axis=0)
+            query_grad[j] += times(scores_grad, key)
+            kv_grad[slot, 0, j] = (
+                lax.dot_general(
+                    scores_grad, query[j], (((0,), (0,)), ((), ())),
+                    preferred_element_type=jnp.float32,
+                )
+                * math.log(2)
+            ).astype(LOW)
+            kv_grad[slot, 1, j] = lax.dot_general(
+                weights, attended_grad[j], (((0,), (0,)), ((), ())),
+                preferred_element_type=jnp.float32,
+            ).astype(LOW)
+
+        over_tiles(heads, head)
+
+    over_tiles(8, block)
+
+
+def attention_backward(f, positions, segments):
+    vmem = pl.BlockSpec(memory_space=pltpu.VMEM)
+    return pl.pallas_call(
+        backward_kernel,
+        out_shape=[
+            jax.ShapeDtypeStruct(f["query"].shape, jnp.float32),
+            jax.ShapeDtypeStruct(f["kv"].shape, LOW),
+        ],
+        in_specs=[vmem] * 7,
+        out_specs=[vmem] * 2,
+        scratch_shapes=[pltpu.VMEM((positions.shape[1], positions.shape[1]), jnp.float32)],
+        compiler_params=pltpu.CompilerParams(vmem_limit_bytes=60 * 1024 * 1024),
+    )(f["query"], f["kv"], f["meta"], positions, segments, f["attended_grad"], f["inner"])
+
+
 def mean_rms(entries):
     return lax.rsqrt(jnp.mean(entries * entries, axis=-1, keepdims=True) + EPS)
 
@@ -276,35 +759,6 @@
         scaled * entries, axis=-1, keepdims=True
     )
     return (entries_grad, gain_grad)
-
-
-def rope_tables(token_place, head_dim):
-    half_dim = head_dim // 2
-    inverse = 1.0 / ROPE_BASE ** (jnp.arange(half_dim, dtype=jnp.float32) * 2.0 / head_dim)
-    angles = token_place.astype(jnp.float32)[:, None] * inverse[None, :]
-    return (jnp.cos(angles), jnp.sin(angles))
-
-
-def rotate(entries, cosine_table, sine_table):
-    half_dim = entries.shape[-1] // 2
-    front_half = entries[..., :half_dim]
-    back_half = entries[..., half_dim:]
-    cosine = cosine_table[:, None, :]
-    sine = sine_table[:, None, :]
-    return jnp.concatenate(
-        [front_half * cosine - back_half * sine, back_half * cosine + front_half * sine], axis=-1
-    )
-
-
-def unrotate(gradient, cosine_table, sine_table):
-    half_dim = gradient.shape[-1] // 2
-    front_half = gradient[..., :half_dim]
-    back_half = gradient[..., half_dim:]
-    cosine = cosine_table[:, None, :]
-    sine = sine_table[:, None, :]
-    return jnp.concatenate(
-        [front_half * cosine + back_half * sine, back_half * cosine - front_half * sine], axis=-1
-    )
 
 
 def dense(left, right):
@@ -332,177 +786,59 @@
     local_rows = tokens.shape[1]
     key_heads = key_weight.shape[1] // head_dim
     query_heads = query_weight.shape[1] // head_dim
-    groups = query_heads // key_heads
-    block_rows = min(512, local_rows)
-    block_count = local_rows // block_rows
+    f = forward(
+        tokens[0], cotangent[0], positions, segments, attention_gain[None], query_weight,
+        key_weight, value_weight, query_gain[None], key_gain[None], out_weight, mlp_gain[None],
+        gate_weight, up_weight, down_weight,
+    )
     score_scale = 1.0 / math.sqrt(head_dim)
     attention_gain = attention_gain.astype(jnp.float32)
-    mlp_gain = mlp_gain.astype(jnp.float32)
     query_gain = query_gain.astype(jnp.float32)
     key_gain = key_gain.astype(jnp.float32)
     inputs = tokens[0].astype(jnp.float32)
-    token_place = positions[0]
-    segment = segments[0]
-    cosine_table, sine_table = rope_tables(token_place, head_dim)
-    normed = (inputs * mean_rms(inputs) * attention_gain).astype(jnp.bfloat16)
-    query_raw = dense(normed, query_weight).reshape(local_rows, query_heads, head_dim)
-    key_raw = dense(normed, key_weight).reshape(local_rows, key_heads, head_dim)
-    value_low = (
-        dense(normed, value_weight).astype(jnp.bfloat16).reshape(local_rows, key_heads, head_dim)
-    )
-    query_low = rotate(
-        query_raw * mean_rms(query_raw) * query_gain, cosine_table, sine_table
-    ).astype(jnp.bfloat16)
-    key_low = rotate(key_raw * mean_rms(key_raw) * key_gain, cosine_table, sine_table).astype(
-        jnp.bfloat16
-    )
-    key_local = key_low.transpose(1, 0, 2)
-    value_local = value_low.transpose(1, 0, 2)
-    key_all, value_all, place_all, segment_all = (
-        lax.all_gather(key_local, "seq", axis=1, tiled=True),
-        lax.all_gather(value_local, "seq", axis=1, tiled=True),
-        lax.all_gather(token_place, "seq", axis=0, tiled=True),
-        lax.all_gather(segment, "seq", axis=0, tiled=True),
-    )
-    query_blocks = query_low.reshape(
-        block_count, block_rows, key_heads, groups, head_dim
-    ).transpose(2, 0, 3, 1, 4)
-    place_blocks = token_place.reshape(block_count, block_rows)
-    segment_blocks = segment.reshape(block_count, block_rows)
-
-    def block_mask(query_place, query_segment, key_place, key_segment):
-        return (key_place[None, :] <= query_place[:, None]) & (
-            key_segment[None, :] == query_segment[:, None]
-        )
-
-    def forward_head(element):
-        query_head, key_head, value_head = element
-
-        def forward_block(pieces):
-            query_block, query_place, query_segment = pieces
-            scores = (
-                jnp.einsum("gbd,td->gbt", query_block, key_head, preferred_element_type=jnp.float32)
-                * score_scale
-            )
-            allowed = block_mask(query_place, query_segment, place_all, segment_all)[None]
-            scores = jnp.where(allowed, scores, NEGATIVE)
-            largest = jnp.max(scores, axis=-1, keepdims=True)
-            exponent = jnp.exp(scores - largest)
-            row_total = jnp.sum(exponent, axis=-1, keepdims=True)
-            attend = (exponent / row_total).astype(jnp.bfloat16)
-            attended = jnp.einsum(
-                "gbt,td->gbd", attend, value_head, preferred_element_type=jnp.float32
-            )
-            return (attended, largest[..., 0] + jnp.log(row_total[..., 0]))
-
-        return lax.map(forward_block, (query_head, place_blocks, segment_blocks))
-
-    attended, log_total = lax.map(forward_head, (query_blocks, key_all, value_all))
-    attended_low = (
-        attended.transpose(1, 3, 0, 2, 4)
-        .reshape(local_rows, query_heads * head_dim)
-        .astype(jnp.bfloat16)
-    )
-    attention_out = lax.psum(dense(attended_low, out_weight), "tensor")
-    middle = inputs + attention_out
-    normed_mlp = (middle * mean_rms(middle) * mlp_gain).astype(jnp.bfloat16)
-    gate_value = dense(normed_mlp, gate_weight)
-    up_value = dense(normed_mlp, up_weight)
-    sigmoid_gate = jax.nn.sigmoid(gate_value)
-    activated = (gate_value * sigmoid_gate * up_value).astype(jnp.bfloat16)
-    mlp_out = lax.psum(dense(activated, down_weight).astype(jnp.bfloat16), "tensor").astype(
-        jnp.float32
-    )
-    output = (middle + mlp_out).astype(jnp.bfloat16)[None]
+    query_grad_blocks, kv_grad_all = attention_backward(f, positions, segments)
+    mlp_other = lax.ppermute(f["mlp_out"], "tensor", ((0, 1), (1, 0)))
+    output = (
+        f["middle"] + (f["mlp_out"].astype(jnp.float32) + mlp_other.astype(jnp.float32))
+    ).astype(jnp.bfloat16)[None]
+    kv_grad = lax.psum_scatter(kv_grad_all, "seq", scatter_dimension=0, tiled=True)[0]
+    cosine_table, sine_table = f["cosine"][:, None, :], f["sine"][:, None, :]
+
+    def unrotate(gradient):
+        half_dim = head_dim // 2
+        turned = jnp.concatenate([gradient[..., half_dim:], gradient[..., :half_dim]], axis=-1)
+        return gradient * cosine_table - turned * sine_table
+
+    query_rot_grad = (
+        query_grad_blocks.reshape(key_heads, 2, local_rows, head_dim)
+        .transpose(2, 0, 1, 3)
+        .reshape(local_rows, query_heads, head_dim)
+        * score_scale
+    )
+    query_raw_grad, query_gain_part = norm_back(
+        f["query_raw"].reshape(local_rows, query_heads, head_dim),
+        query_gain,
+        unrotate(query_rot_grad),
+    )
+    key_raw_grad, key_gain_part = norm_back(
+        f["key_raw"].reshape(local_rows, key_heads, head_dim),
+        key_gain,
+        unrotate(kv_grad[0].astype(jnp.float32).transpose(1, 0, 2)),
+    )
+    query_grad_low = query_raw_grad.reshape(local_rows, -1).astype(jnp.bfloat16)
+    key_grad_low = key_raw_grad.reshape(local_rows, -1).astype(jnp.bfloat16)
+    value_grad_low = kv_grad[1].transpose(1, 0, 2).reshape(local_rows, -1)
+    normed, normed_mlp, middle_low = f["normed"], f["normed_mlp"], f["middle_low"]
+    attended_low, grad_middle = f["attended"], f["grad_middle"]
+    gate_grad_low, up_grad_low, activated = f["gate_grad"], f["up_grad"], f["activated"]
     upstream = cotangent[0]
-    grad_act = dense(upstream, down_weight.T)
-    gate_grad_low = (
-        grad_act * up_value * sigmoid_gate * (1.0 + gate_value * (1.0 - sigmoid_gate))
-    ).astype(jnp.bfloat16)
-    up_grad_low = (grad_act * gate_value * sigmoid_gate).astype(jnp.bfloat16)
-    mlp_partial = dense(gate_grad_low, gate_weight.T) + dense(up_grad_low, up_weight.T)
-    mlp_normed_grad = lax.psum(mlp_partial.astype(jnp.bfloat16), "tensor").astype(jnp.float32)
-    middle_part, mlp_gain_grad = norm_back(middle, mlp_gain, mlp_normed_grad)
-    grad_middle = upstream.astype(jnp.float32) + middle_part
-    middle_low = grad_middle.astype(jnp.bfloat16)
-    attended_grad_low = dense(middle_low, out_weight.T).astype(jnp.bfloat16)
-    grad_blocks = attended_grad_low.reshape(
-        block_count, block_rows, key_heads, groups, head_dim
-    ).transpose(2, 0, 3, 1, 4)
-    key_use, value_use, place_use, segment_use = (key_all, value_all, place_all, segment_all)
-
-    def backward_head(element):
-        query_head, grad_head, total_head, key_head, value_head = element
-
-        def backward_block(carried, pieces):
-            key_sum, value_sum = carried
-            query_block, grad_block, total_block, query_place, query_segment = pieces
-            scores = (
-                jnp.einsum("gbd,td->gbt", query_block, key_head, preferred_element_type=jnp.float32)
-                * score_scale
-            )
-            allowed = block_mask(query_place, query_segment, place_use, segment_use)[None]
-            attend = jnp.where(allowed, jnp.exp(scores - total_block[..., None]), 0.0)
-            attend_low = attend.astype(jnp.bfloat16)
-            grad_attend = jnp.einsum(
-                "gbd,td->gbt", grad_block, value_head, preferred_element_type=jnp.float32
-            )
-            inner_sum = jnp.sum(attend * grad_attend, axis=-1, keepdims=True)
-            scores_grad = (attend * (grad_attend - inner_sum)).astype(jnp.bfloat16)
-            query_grad = (
-                jnp.einsum("gbt,td->gbd", scores_grad, key_head, preferred_element_type=jnp.float32)
-                * score_scale
-            )
-            key_sum = (
-                key_sum
-                + jnp.einsum(
-                    "gbt,gbd->td", scores_grad, query_block, preferred_element_type=jnp.float32
-                )
-                * score_scale
-            )
-            value_sum = value_sum + jnp.einsum(
-                "gbt,gbd->td", attend_low, grad_block, preferred_element_type=jnp.float32
-            )
-            return ((key_sum, value_sum), query_grad)
-
-        initial = jnp.zeros(key_head.shape, jnp.float32)
-        sums, query_grad = lax.scan(
-            backward_block,
-            (initial, initial),
-            (query_head, grad_head, total_head, place_blocks, segment_blocks),
-        )
-        return (query_grad, sums[0], sums[1])
-
-    query_grad_blocks, key_grad_all, value_grad_all = lax.map(
-        backward_head, (query_blocks, grad_blocks, log_total, key_use, value_use)
-    )
-    key_grad, value_grad = (
-        lax.psum_scatter(
-            key_grad_all.astype(jnp.bfloat16), "seq", scatter_dimension=1, tiled=True
-        ).astype(jnp.float32),
-        lax.psum_scatter(
-            value_grad_all.astype(jnp.bfloat16), "seq", scatter_dimension=1, tiled=True
-        ).astype(jnp.float32),
-    )
-    query_rot_grad = query_grad_blocks.transpose(1, 3, 0, 2, 4).reshape(
-        local_rows, query_heads, head_dim
-    )
-    query_raw_grad, query_gain_part = norm_back(
-        query_raw, query_gain, unrotate(query_rot_grad, cosine_table, sine_table)
-    )
-    key_raw_grad, key_gain_part = norm_back(
-        key_raw, key_gain, unrotate(key_grad.transpose(1, 0, 2), cosine_table, sine_table)
-    )
-    query_grad_low = query_raw_grad.reshape(local_rows, query_heads * head_dim).astype(jnp.bfloat16)
-    key_grad_low = key_raw_grad.reshape(local_rows, key_heads * head_dim).astype(jnp.bfloat16)
-    value_grad_low = (
-        value_grad.transpose(1, 0, 2).reshape(local_rows, key_heads * head_dim).astype(jnp.bfloat16)
-    )
+    mlp_gain_grad = f["mlp_gain_grad"][0]
     attention_partial = (
         dense(query_grad_low, query_weight.T)
         + dense(key_grad_low, key_weight.T)
         + dense(value_grad_low, value_weight.T)
     )
+    partial_low = attention_partial.astype(jnp.bfloat16)
     attention_gain_part = jnp.sum(attention_partial * inputs * mean_rms(inputs), axis=0)
     width = gate_weight.shape[1]
     q_width, k_width = query_weight.shape[1], key_weight.shape[1]
@@ -526,9 +862,9 @@
             attended_low,
         ),
         pack_gains(attention_gain_part, 0.5 * mlp_gain_grad, query_gain_part, key_gain_part),
-        attention_partial.astype(jnp.bfloat16),
-    )
-    normed_grad = attention_partial + partial_other.astype(jnp.float32)
+        partial_low,
+    )
+    normed_grad = partial_low.astype(jnp.float32) + partial_other.astype(jnp.float32)
     input_part, _ = norm_back(inputs, attention_gain, normed_grad)
     input_grad = (grad_middle + input_part).astype(jnp.bfloat16)[None]
     return (

time: 456 us -> 247 us (0.54)
  waiting for transfers between devices: 165 us -> 7.6 us
  Pallas kernels: 70 us -> 172 us
  matrix products: 97.7 us -> 3.8 us
  local copies, waits for them, and re-layouts: 50.5 us -> 26.7 us
  blocking collectives: 19 us -> 0 us
  other arithmetic: 35.6 us -> 20.6 us
    pallas_call x0 -> x2, Pallas kernels: none -> 102 us  [the longest x1 76.6 us: forward(): pl.pallas_call(forward_kernel, out_shape=[jax.ShapeDtypeStruct(shape, kin...]
    psum x2 -> x0, waiting for transfers between devices: 96.1 us -> none  [the longest x1 48.4 us: shards(): attention_out = lax.psum(dense(attended_low, out_weight), 'tensor')]
    dot_general x28 -> x0, matrix products: 71.8 us -> none  [the longest x4 15.2 us: backward_block(): jnp.einsum('gbt,gbd->td', attend_low, grad_block, preferred_element_type=...]
    reduce_scatter x2 -> x1, waiting for transfers between devices: 53.2 us -> 7.58 us  [shards(): lax.psum_scatter(kv_grad_all, 'seq', scatter_dimension=0, tiled=True)[0]]
    dot_general x14 -> x3, matrix products: 26 us -> 3.8 us  [dense(): return jnp.dot(left, right, preferred_element_type=jnp.float32)]
    all_gather x2 -> x0, blocking collectives: 19 us -> none  [the longest x1 10.9 us: shards(): lax.all_gather(token_place, 'seq', axis=0, tiled=True)]
    all_gather x2 -> x0, waiting for transfers between devices: 15.4 us -> none  [the longest x1 15.4 us: shards(): lax.all_gather(value_local, 'seq', axis=1, tiled=True)]
    while x25 -> x0, local copies, waits for them, and re-layouts: 10.1 us -> none
  transfers between devices with their start and end apart: 6 -> 2, of which waited for: 5 -> 1; matrix products, arithmetic and copies ran while one was open for 7% -> 11% of each run, Pallas kernels for 0% -> 0%
where the time goes in v2:
time: 247 us; the launch traced here: 246 us
  Pallas kernels  172 us (70%)
  local copies, waits for them, and re-layouts  26.7 us (11%)
  other arithmetic  20.6 us (8%)
  between operations  14.4 us (6%)
  waiting for transfers between devices  7.6 us (3%)
  matrix products  3.8 us (2%)
    pallas_call x1, Pallas kernels, forward(): pl.pallas_call(forward_kernel, out_shape=[jax.ShapeDtypeStruct(shape, kin...  76.6 us
    pallas_call x1, Pallas kernels, scatter_gradients(): pl.pallas_call(functools.partial(scatter_kernel, pieces, len(lhs), len(rh...  70.2 us
    pallas_call x1, Pallas kernels, attention_backward(): pl.pallas_call(backward_kernel, out_shape=[jax.ShapeDtypeStruct(f['query'...  25 us
    reduce_scatter x1, waiting for transfers between devices, shards(): lax.psum_scatter(kv_grad_all, 'seq', scatter_dimension=0, tiled=True)[0]  7.58 us
  transfers between devices with their start and end apart: 2, of which 1 were waited for; matrix products, arithmetic and copies ran while one was open for 11% of the time, Pallas kernels for 0%

profile of v2, /device:TPU:0, one launch (start us, length us, event | category | flops | bytes accessed | tf_op | source)
XLA Modules:
  0.0 246.4 jit_solution(3900139915243339392)
XLA Ops:
  7.2 1.3 broadcast_in_dim.19.attention_gain
  8.5 1.3 broadcast_in_dim.43.mlp_gain
  10.4 76.6 %shard_map.255 = (bf16[256,1024]{1,0:T(8,128)(2,1)}, f32[256,1024]{1,0:T(8,128)}, f32[256,512]{1,0:T(8,128)}, bf16[4,512,128]{2,1,0:T(8,128)(2,1)}, bf16[8,2,4,2...) custom-call(bf16[256,1024]{1,0:T(8,128)(2,1)} %bitcast.118, ...), custom_call_target="tpu_custom_call" | custom-call | tf_op jit(solution)/shard_map/pallas_call | solution.py:652
  87.0 25.0 %shard_map.256 = (f32[4,512,128]{2,1,0:T(8,128)}, bf16[8,2,4,256,128]{4,3,2,1,0:T(8,128)(2,1)}) custom-call(bf16[4,512,128]{2,1,0:T(8,128)(2,1)} %get-tuple-element.46.query, bf16[8,2,4,256,128]{4,3,2,1,0:T(8,128)(2,1)} %get-tuple-element.47.kv, s32[8,8,256]{2,1,0:T(8,128)} %get-tuple-element.48.meta, s32[1,256]{1,0:T(1,128)} %positions.3, ...), custom_call_target="tpu_custom_call" | custom-call | tf_op jit(solution)/shard_map/pallas_call | solution.py:737
  112.1 1.4 collective-permute-start
  113.9 2.0 copy.60
  116.0 1.2 reshape.161
  117.2 1.2 copy.41
  118.4 1.8 reshape.155
  120.3 1.7 slice_bitcast_fusion.8
  122.0 1.8 multiply_reduce_fusion.1
  124.7 3.1 %fusion.15 = f32[128]{0:T(128)} fusion(f32[2048,128]{1,0:T(8,128)} %reshape.161, f32[2048,64]{1,0:T(8,128)} %get-tuple-element.80, f32[2048,64]{1,0:T(8,128)} %get-tuple-element.79, f32[2048,128]{1,0:T(8,128)S(1)} %bitcast.117, f32[2048]{0:T(1024)S(1)} %rsqrt.41, f32[256,128]{1,0:T(8,128)S(1)} %copy-done.10, f32[256,128]{1,0:T(8,128)S(1)} %broadcast_multiply_fusion.1), kind=kLoop, calls=%fused_computation.28 | loop fusion | flops 1834880 | bytes 3416576 | tf_op jit(solution)/shard_map/reduce_sum | solution.py:757
  127.7 0.8 reshape.162
  130.0 1.1 multiply_reduce_fusion.4
  132.3 1.2 mul.257
  134.0 2.7 %fusion.9.refs_7_ = bf16[256,1024]{1,0:T(8,128)(2,1)S(1)} fusion(f32[32,8,8,128]{3,2,1,0:T(8,128)S(1)} %bitcast.123, f32[256,1024]{1,0:T(8,128)S(1)} %copy-done.1, f32[32,8,8,128]{3,2,1,0:T(8,128)S(1)} %bitcast.122, f32[32,8,8,128]{3,2,1,0:T(8,128)} %bitcast.125, f32[256,1024]{1,0:T(8,128)} %reshape.155, f32[32,8,8,128]{3,2,1,0:T(8,128)S(1)} %bitcast.124, ...), kind=kLoop, calls=%fused_computation.17 | loop fusion | flops 2097152 | bytes 7868416 | tf_op jit(solution)/shard_map/convert_element_type | solution.py:828
  136.7 1.7 fusion.23
  138.5 2.3 fusion.16
  140.7 7.6 %reduce-scatter.2.cloned.1.call-done = bf16[1,2,4,256,128]{4,3,2,1,0:T(8,128)(2,1)} async-done(((bf16[8,2,4,256,128]{4,3,2,1,0:T(8,128)(2,1)}), bf16[1,2,4,256,128]{4,3,2,1,0:T(8,128)(2,1)}) %reduce-scatter.2.cloned.1.call-update) | async-done | bytes 524304 | tf_op jit(solution)/shard_map/reduce_scatter | solution.py:804
  148.3 1.2 slice_bitcast_fusion
  150.3 0.8 convolution_add_fusion.1
  151.1 1.3 copy_bitcast_fusion
  152.4 1.3 fusion.21
  155.3 70.2 %shard_map.257 = (f32[16,1536]{1,0:T(8,128)}, f32[16,1536]{1,0:T(8,128)}, f32[16,1536]{1,0:T(8,128)}, f32[16,1536]{1,0:T(8,128)}, f32[16,1536]{1,0:T(8,128)}, /*...) custom-call(bf16[256,1024]{1,0:T(8,128)(2,1)} %get-tuple-element.56.refs_0_, bf16[256,1024]{1,0:T(8,128)(2,1)} %bitcast.128, ...), custom_call_target="tpu_custom_call" | custom-call | tf_op jit(solution)/shard_map/pallas_call | solution.py:226
  225.6 1.5 slice.50
  227.1 1.4 slice.51
  228.5 1.5 slice_bitcast_fusion.2
  230.0 1.4 slice.52
  231.3 1.3 slice_bitcast_fusion.5
  232.7 1.3 slice_bitcast_fusion.3
  234.0 1.4 fusion.7
  235.4 2.2 fusion.17
  (86 shorter events, 9.4 us)
Async XLA Ops:
  7.2 141.2 %reduce-scatter.2.cloned.1.call-start = ((), (), s32[]{:S(2)}) async-start(), calls=%async_computation.1 | async-start | bytes 4718592 | tf_op jit(solution)/shard_map/reduce_scatter | solution.py:804
  112.0 1.5 copy-start.23
  112.0 1.5 copy-start.24
  112.0 1.5 copy-start.21
  112.0 1.5 copy-start.17
  112.0 3.9 %copy-start.1 = (f32[256,1024]{1,0:T(8,128)S(1)}, f32[256,1024]{1,0:T(8,128)}, u32[]{:S(2)}) copy-start(f32[256,1024]{1,0:T(8,128)} %get-tuple-element.45) | copy-start | bytes 3145732
  112.1 26.4 %collective-permute-start = (bf16[256,1024]{1,0:T(8,128)(2,1)}, bf16[256,1024]{1,0:T(8,128)(2,1)}, u32[]{:S(2)}, u32[]{:S(2)}) collective-permute-start(bf16[256,1024]{1,0:T(8,128)(2,1)} %get-tuple-element.43), channel_id=1, source_target_pairs={{0,1},{1,0},{2,3},{3,2},{4,5},{5,4},{6,7},{7,6},{8,9},{9,8},{10,11... | collective-permute-start | bytes 1572872 | tf_op jit(solution)/shard_map/ppermute | solution.py:800
  113.5 8.5 %copy-start.22 = (f32[128]{0:T(128)}, f32[128]{0:T(128)S(1)}, u32[]{:S(2)}) copy-start(f32[128]{0:T(128)S(1)} %convert_element_type.51) | copy-start | bytes 1540
  113.7 4.6 %copy-start.4 = (f32[256,512]{0,1:T(8,128)}, f32[256,512]{0,1:T(8,128)S(1)}, u32[]{:S(2)}) copy-start(f32[256,512]{0,1:T(8,128)S(1)} %copy.33) | copy-start | bytes 1572868
  116.0 4.2 %copy-start.15 = (f32[256,128]{1,0:T(8,128)S(1)}, f32[256,128]{1,0:T(8,128)}, u32[]{:S(2)}) copy-start(f32[256,128]{1,0:T(8,128)} %get-tuple-element.52) | copy-start | bytes 393220
  120.3 1.8 copy-start.9
  120.3 1.8 copy-start.10
  123.8 7.3 %copy-start = (bf16[1,256,1024]{2,1,0:T(8,128)(2,1)S(1)}, bf16[1,256,1024]{2,1,0:T(8,128)(2,1)}, u32[]{:S(2)}) copy-start(bf16[1,256,1024]{2,1,0:T(8,128)(2,1)} %param.16) | copy-start | bytes 1572868
  127.7 5.8 %copy-start.14 = (f32[256,8]{1,0:T(8,128)S(1)}, f32[256,8]{1,0:T(8,128)}, u32[]{:S(2)}) copy-start(f32[256,8]{1,0:T(8,128)} %get-tuple-element.99) | copy-start | bytes 24580
  133.9 2.8 %copy-start.2 = (bf16[1024,1024]{1,0:T(8,128)(2,1)S(1)}, bf16[1024,1024]{1,0:T(8,128)(2,1)}, u32[]{:S(2)}) copy-start(bf16[1024,1024]{1,0:T(8,128)(2,1)} %wq_far.1) | copy-start | bytes 6291460
  136.7 4.1 %copy-start.5 = (bf16[256,1024]{1,0:T(8,128)(2,1)}, bf16[256,1024]{1,0:T(8,128)(2,1)S(1)}, u32[]{:S(2)}) copy-start(bf16[256,1024]{1,0:T(8,128)(2,1)S(1)} %fusion.9.refs_7_) | copy-start | bytes 1572868
  136.7 1.8 copy-start.13
  138.5 11.3 %copy-start.16 = (f32[256,128]{1,0:T(8,128)S(1)}, f32[256,128]{1,0:T(8,128)}, u32[]{:S(2)}) copy-start(f32[256,128]{1,0:T(8,128)} %get-tuple-element.52) | copy-start | bytes 393220
  140.7 9.6 %copy-start.6 = (bf16[1024,512]{1,0:T(8,128)(2,1)S(1)}, bf16[1024,512]{1,0:T(8,128)(2,1)}, u32[]{:S(2)}) copy-start(bf16[1024,512]{1,0:T(8,128)(2,1)} %wk_far.1) | copy-start | bytes 3145732
  148.3 1.4 copy-start.11
  148.3 2.0 copy-start.8
  150.3 2.1 copy-start.7
  155.3 78.7 %copy-start.3 = (bf16[256,1024]{1,0:T(8,128)(2,1)S(1)}, bf16[256,1024]{1,0:T(8,128)(2,1)}, u32[]{:S(2)}) copy-start(bf16[256,1024]{1,0:T(8,128)(2,1)} %get-tuple-element.77.refs_12_) | copy-start | bytes 1572868
  155.3 80.1 %copy-start.12 = (f32[256,1024]{1,0:T(8,128)S(1)}, f32[256,1024]{1,0:T(8,128)}, u32[]{:S(2)}) copy-start(f32[256,1024]{1,0:T(8,128)} %get-tuple-element.44) | copy-start | bytes 3145732
  225.6 12.0 %copy-start.20 = (f32[16,1536]{1,0:T(8,128)S(1)}, f32[16,1536]{1,0:T(8,128)}, u32[]{:S(2)}) copy-start(f32[16,1536]{1,0:T(8,128)} %get-tuple-element.121) | copy-start | bytes 294916
  225.6 12.7 %copy-start.19 = (f32[16,1536]{1,0:T(8,128)S(1)}, f32[16,1536]{1,0:T(8,128)}, u32[]{:S(2)}) copy-start(f32[16,1536]{1,0:T(8,128)} %get-tuple-element.122) | copy-start | bytes 294916
  225.6 13.3 %copy-start.18 = (f32[16,1536]{1,0:T(8,128)S(1)}, f32[16,1536]{1,0:T(8,128)}, u32[]{:S(2)}) copy-start(f32[16,1536]{1,0:T(8,128)} %get-tuple-element.69) | copy-start | bytes 294916
Sparse Core Ops, SparseCore 0:
  112.2 36.1 reduce-scatter.1

commit v3 on v2

--- a/solution.py
+++ b/solution.py
@@ -66,202 +66,6 @@
         y = 2 * bit["y3"] + (bit["y3"] ^ bit["y1"])
         chunks.append(((x * 2 + bit["z"]) * 4 + y) * 2 + bit["core"])
     return chunks
-
-
-def scatter_kernel(pieces, n_lhs, n_rhs, *refs):
-    streams = len(pieces)
-    lhs = refs[:n_lhs]
-    rhs = refs[n_lhs : n_lhs + n_rhs]
-    gains_in, partial_in = refs[n_lhs + n_rhs : n_lhs + n_rhs + 2]
-    refs = refs[n_lhs + n_rhs + 2 :]
-    outs = refs[:streams]
-    gains_out, partial_out = refs[streams : streams + 2]
-    refs = refs[streams + 2 :]
-    turned, sent, held = refs[:3]
-    landed = refs[3:9]
-    gains_held = refs[9]
-    gains_landed = refs[10:16]
-    gains_last, gains_sum, send_sem, recv_sem, gains_send, gains_recv, pair_send, pair_recv = refs[16:]
-    bits, partners = place()
-    greet(list(partners.values()))
-
-    def exchange(source, target, out_sem, in_sem, partner):
-        return pltpu.make_async_remote_copy(
-            src_ref=source,
-            dst_ref=target,
-            send_sem=out_sem,
-            recv_sem=in_sem,
-            device_id=partner,
-            device_id_type=MESH,
-        )
-
-    partial_copy = exchange(
-        partial_in, partial_out, pair_send.at[0], pair_recv.at[0], partners["tensor"]
-    )
-    partial_copy.start()
-    orders = [stream_order(s) for s in range(streams)]
-    features = lhs[0].shape[1]
-    half = features // 2
-    core = bits["core"]
-    block = 128
-    copies = {}
-    used = []
-    for s in range(streams):
-        for left, right, first, columns in pieces[s]:
-            flipped = lhs[left][...].T
-            index = len(used)
-            used.append((s, left, right, first, columns))
-            for slot, chunk in enumerate(slot_chunks(orders[s])):
-                turned[index, slot * CHUNK : (slot + 1) * CHUNK, :] = flipped[
-                    chunk * CHUNK : (chunk + 1) * CHUNK, :
-                ]
-
-    def product(s, target, offset):
-        for index, (stream, _, right, first, columns) in enumerate(used):
-            if stream != s:
-                continue
-
-            def rows(i, _, index=index, right=right, first=first, columns=columns):
-                start = pl.multiple_of(i * block, block)
-                from_row = pl.multiple_of(offset + start, block)
-                target[s, pl.ds(start, block), first : first + columns] = jnp.dot(
-                    turned[index, pl.ds(from_row, block), :],
-                    rhs[right][...],
-                    preferred_element_type=jnp.float32,
-                ).astype(LOW)
-                return 0
-
-            lax.fori_loop(0, half // block, rows, 0)
-
-    for s in range(streams):
-        product(s, sent, (1 - core) * half)
-        copies[s, 0] = exchange(
-            sent.at[s], landed[0].at[s], send_sem.at[s, 0], recv_sem.at[s, 0], partners["core"]
-        )
-        copies[s, 0].start()
-    gain_chunks = gains_in.shape[0]
-    gains_copy = [None] * 6
-    gains_copy[0] = exchange(
-        gains_in.at[pl.ds((1 - core) * (gain_chunks // 2), gain_chunks // 2)],
-        gains_landed[0],
-        gains_send.at[0],
-        gains_recv.at[0],
-        partners["core"],
-    )
-    gains_copy[0].start()
-    for s in range(streams):
-        product(s, held, core * half)
-    gains_held[...] = gains_in[pl.ds(core * (gain_chunks // 2), gain_chunks // 2)]
-
-    base = [0] * streams
-    gains_base = 0
-    for step in range(6):
-        rows = half >> step
-        for s in range(streams):
-            copies[s, step].wait()
-            if step == 5:
-                mine = pl.multiple_of(base[s], CHUNK)
-                outs[s][...] = held[s, pl.ds(mine, CHUNK), :].astype(jnp.float32) + landed[5][
-                    s
-                ].astype(jnp.float32)
-                continue
-            tile = min(rows, 64)
-
-            def add(i, _, s=s, step=step, tile=tile):
-                start = pl.multiple_of(i * tile, tile)
-                here = pl.multiple_of(base[s] + start, tile)
-                held[s, pl.ds(here, tile), :] = (
-                    held[s, pl.ds(here, tile), :] + landed[step][s, pl.ds(start, tile), :]
-                )
-                return 0
-
-            lax.fori_loop(0, rows // tile, add, 0)
-            dim = orders[s][step + 1]
-            bit = bits[dim]
-            away = pl.multiple_of(base[s] + (1 - bit) * (rows // 2), CHUNK)
-            copies[s, step + 1] = exchange(
-                held.at[s, pl.ds(away, rows // 2), :],
-                landed[step + 1].at[s],
-                send_sem.at[s, step + 1],
-                recv_sem.at[s, step + 1],
-                partners[dim],
-            )
-            copies[s, step + 1].start()
-            base[s] = base[s] + bit * (rows // 2)
-        chunks = gain_chunks >> (step + 1)
-        gains_copy[step].wait()
-        gains_held[pl.ds(gains_base, chunks)] = (
-            gains_held[pl.ds(gains_base, chunks)] + gains_landed[step][...]
-        )
-        if step < 5:
-            dim = orders[0][step + 1]
-            bit = bits[dim]
-            gains_copy[step + 1] = exchange(
-                gains_held.at[pl.ds(gains_base + (1 - bit) * (chunks // 2), chunks // 2)],
-                gains_landed[step + 1],
-                gains_send.at[step + 1],
-                gains_recv.at[step + 1],
-                partners[dim],
-            )
-            gains_copy[step + 1].start()
-            gains_base = gains_base + bit * (chunks // 2)
-    gains_last[...] = gains_held[pl.ds(gains_base, 1)]
-    last = exchange(gains_last, gains_sum, pair_send.at[1], pair_recv.at[1], partners["tensor"])
-    last.start()
-    last.wait()
-    gains_out[...] = gains_last[0] + gains_sum[0]
-    partial_copy.wait()
-
-
-def scatter_gradients(pieces, lhs, rhs, gains, partial):
-    streams = len(pieces)
-    width = sum(columns for _, _, _, columns in pieces[0])
-    tokens, features = lhs[0].shape
-    half = features // 2
-    parts = sum(len(p) for p in pieces)
-    chunks = features // CHUNK
-    vmem = pl.BlockSpec(memory_space=pltpu.VMEM)
-    landed = [pltpu.VMEM((streams, half >> step, width), LOW) for step in range(6)]
-    gains_landed = [pltpu.VMEM((chunks >> (step + 1), 8, 128), jnp.float32) for step in range(6)]
-    result = pl.pallas_call(
-        functools.partial(scatter_kernel, pieces, len(lhs), len(rhs)),
-        out_shape=[jax.ShapeDtypeStruct((CHUNK, width), jnp.float32)] * streams
-        + [
-            jax.ShapeDtypeStruct((8, 128), jnp.float32),
-            jax.ShapeDtypeStruct(partial.shape, partial.dtype),
-        ],
-        in_specs=[vmem] * (len(lhs) + len(rhs) + 2),
-        out_specs=[vmem] * (streams + 2),
-        scratch_shapes=[
-            pltpu.VMEM((parts, features, tokens), LOW),
-            pltpu.VMEM((streams, half, width), LOW),
-            pltpu.VMEM((streams, half, width), LOW),
-            *landed,
-            pltpu.VMEM((chunks // 2, 8, 128), jnp.float32),
-            *gains_landed,
-            pltpu.VMEM((1, 8, 128), jnp.float32),
-            pltpu.VMEM((1, 8, 128), jnp.float32),
-            pltpu.SemaphoreType.DMA((streams, 6)),
-            pltpu.SemaphoreType.DMA((streams, 6)),
-            pltpu.SemaphoreType.DMA((6,)),
-            pltpu.SemaphoreType.DMA((6,)),
-            pltpu.SemaphoreType.DMA((2,)),
-            pltpu.SemaphoreType.DMA((2,)),
-        ],
-        compiler_params=pltpu.CompilerParams(
-            collective_id=0, has_side_effects=True, vmem_limit_bytes=60 * 1024 * 1024
-        ),
-    )(*lhs, *rhs, gains, partial)
-    return result[:streams], result[streams], result[streams + 1]
-
-
-def pack_gains(attention, mlp, query, key):
-    chunks = attention.shape[0] // CHUNK
-    packed = jnp.concatenate(
-        [entry.reshape(chunks, -1) for entry in (attention, mlp, query, key)], axis=1
-    )
-    ordered = packed[jnp.array(slot_chunks(stream_order(0)))]
-    return jnp.pad(ordered[:, None, :], ((0, 0), (0, 7), (0, 128 - ordered.shape[1])))
 
 
 def remote(source, target, out_sem, in_sem, partner):
@@ -603,9 +407,8 @@
             here = slice(g * rows, (g + 1) * rows)
             normal = both[:, g * hd : (g + 1) * hd] * weight_sum[j, here, :]
             attended_grad[j, here, :] = normal.astype(LOW)
-            inner[j, here, :] = jnp.broadcast_to(
-                jnp.sum(normal * total[j, here, :], axis=-1, keepdims=True), (rows, hd)
-            )
+            summed = jnp.sum((normal * total[j, here, :]).T, axis=0, keepdims=True)
+            inner[j, :, here] = jnp.broadcast_to(summed, (8, rows))
 
     over_tiles(heads, attended_grad_tile)
 
@@ -643,7 +446,7 @@
         grad_middle=((rows, features), f32),
         middle_low=((rows, features), LOW),
         attended_grad=((heads, 2 * rows, hd), LOW),
-        inner=((heads, 2 * rows, hd), f32),
+        inner=((heads, 8, 2 * rows), f32),
         mlp_gain_grad=((1, features), f32),
     )
     weights = (
@@ -688,81 +491,447 @@
     return dict(zip(outs, results))
 
 
-def backward_kernel(query, kv, meta, positions, segments, attended_grad, inner, query_grad, kv_grad, bias):
-    rows = positions.shape[1]
+EARLY = (("normed_mlp", "gate_grad"), ("normed_mlp", "up_grad"), ("cotangent", "activated"), ("middle_low", "attended"))
+EARLY_TILES = (6, 5, 4, 4, 3)
+LATE_TILES = (2, 2, 2, 1, 1)
+WIDE = 256
+
+
+def split_streams(sizes, tiles):
+    bounds, start = [], 0
+    for size in sizes:
+        bounds.append((start, start + size))
+        start += size
+    streams, first = [], 0
+    for count in tiles:
+        last = first + count * WIDE
+        pieces = []
+        for matrix, (low, high) in enumerate(bounds):
+            begin, end = max(first, low), min(last, high)
+            if begin < end:
+                pieces.append((matrix, begin - low, begin, end - begin))
+        streams.append((first, last - first, pieces))
+        first = last
+    assert first == start
+    return streams
+
+
+class Scatter:
+    def __init__(self, streams, lhs, rhs, turned, sent, held, held_first, landed, send_sem, recv_sem, bits, partners):
+        self.streams, self.lhs, self.rhs = streams, lhs, rhs
+        self.turned, self.sent, self.held, self.held_first = turned, sent, held, held_first
+        self.landed, self.send_sem, self.recv_sem = landed, send_sem, recv_sem
+        self.bits, self.partners = bits, partners
+        self.orders = [stream_order(s) for s in range(len(streams))]
+        self.half = landed[0].shape[0]
+        self.copies = {}
+        self.base = [0] * len(streams)
+
+    def turn(self):
+        self.pairs = []
+        flipped = {}
+        for s, (_, _, pieces) in enumerate(self.streams):
+            for matrix, _, _, _ in pieces:
+                ref = self.lhs[matrix]
+                if (s, id(ref)) in self.pairs:
+                    continue
+                if id(ref) not in flipped:
+                    flipped[id(ref)] = ref[...].T
+                index = len(self.pairs)
+                self.pairs.append((s, id(ref)))
+                for slot, chunk in enumerate(slot_chunks(self.orders[s])):
+                    self.turned[index, slot * CHUNK : (slot + 1) * CHUNK, :] = flipped[id(ref)][
+                        chunk * CHUNK : (chunk + 1) * CHUNK, :
+                    ]
+
+    def product(self, s, target, target_first, offset):
+        for matrix, column, first, columns in self.streams[s][2]:
+            index = self.pairs.index((s, id(self.lhs[matrix])))
+            right = self.rhs[matrix]
+
+            def tile(i, index=index, right=right, column=column, first=first):
+                here = pl.multiple_of(i * WIDE, WIDE)
+                target[:, pl.ds(target_first + first + here, WIDE)] = times(
+                    self.turned[index, pl.ds(pl.multiple_of(offset, CHUNK), self.half), :],
+                    right[:, pl.ds(column + here, WIDE)],
+                ).astype(LOW)
+
+            over_tiles(columns // WIDE, tile)
+
+    def send(self, step, s, source):
+        first, columns, _ = self.streams[s]
+        copy = remote(
+            source,
+            self.landed[step].at[:, pl.ds(first, columns)],
+            self.send_sem.at[s, step],
+            self.recv_sem.at[s, step],
+            self.partners[self.orders[s][step]],
+        )
+        copy.start()
+        self.copies[s, step] = copy
+
+    def open(self):
+        core = self.bits["core"]
+        for s, (first, columns, _) in enumerate(self.streams):
+            self.product(s, self.sent, 0, (1 - core) * self.half)
+            self.send(0, s, self.sent.at[:, pl.ds(first, columns)])
+        for s in range(len(self.streams)):
+            self.product(s, self.held, self.held_first, core * self.half)
+
+    def step(self, step, out=None):
+        rows = self.half >> step
+        for s, (first, columns, _) in enumerate(self.streams):
+            self.copies[s, step].wait()
+            mine = pl.ds(self.held_first + first, columns)
+            if step == 5:
+                out[:, pl.ds(first, columns)] = self.held[
+                    pl.ds(pl.multiple_of(self.base[s], CHUNK), CHUNK), mine
+                ].astype(jnp.float32) + self.landed[5][:, pl.ds(first, columns)].astype(jnp.float32)
+                continue
+            tile = min(rows, 64)
+
+            def add(i, s=s, tile=tile, first=first, columns=columns, mine=mine):
+                start = pl.multiple_of(i * tile, tile)
+                here = pl.ds(pl.multiple_of(self.base[s] + start, tile), tile)
+                self.held[here, mine] = (
+                    self.held[here, mine]
+                    + self.landed[step][pl.ds(start, tile), pl.ds(first, columns)]
+                )
+
+            over_tiles(rows // tile, add)
+            bit = self.bits[self.orders[s][step + 1]]
+            away = pl.multiple_of(self.base[s] + (1 - bit) * (rows // 2), CHUNK)
+            self.send(step + 1, s, self.held.at[pl.ds(away, rows // 2), mine])
+            self.base[s] = self.base[s] + bit * (rows // 2)
+
+
+def backward_kernel(early_streams, late_streams, *refs):
+    (
+        tokens, cotangent, positions, segments, query_gain, key_gain, wq_far, wk_far, wv_far,
+        normed, normed_mlp, middle_low, gate_grad, up_grad, activated, attended, query, kv, meta,
+        attended_grad, inner, query_raw, key_raw, cosine, sine, mlp_out, mlp_gain_grad,
+        early_out, late_out, mlp_other, partial, partial_other, gains,
+        turned, sent, held, bias, query_turned, away_grad, near_grad, core_grad, far_grad,
+        query_low, key_low, value_low, gains_sent, gains_landed,
+    ) = refs[:47]
+    early_landed, late_landed = refs[47:53], refs[53:59]
+    (
+        early_send, early_recv, late_send, late_recv, pair_send, pair_recv, core_send, core_recv,
+        far_send, far_recv, gains_send, gains_recv, weight_sem,
+    ) = refs[59:]
+    bits, partners = place()
+    dp, seq, tensor = lax.axis_index("dp"), lax.axis_index("seq"), lax.axis_index("tensor")
+    core, y = seq % 2, seq // 2
+    rows = tokens.shape[0]
     heads, hd = kv.shape[2], kv.shape[4]
-    place_rows = jnp.broadcast_to(positions[...].astype(jnp.float32), (rows, rows)).T
-    segment_rows = jnp.broadcast_to(segments[...].astype(jnp.float32), (rows, rows)).T
-    query_grad[...] = jnp.zeros_like(query_grad)
-
-    def block(slot):
-        key_place = meta[slot, 0:1, :].astype(jnp.float32)
-        key_segment = meta[slot, 1:2, :].astype(jnp.float32)
-        allowed = (key_place <= place_rows) & (key_segment == segment_rows)
-        bias[...] = jnp.where(allowed, 0.0, NEGATIVE)
+    features = tokens.shape[1]
+    half = features // 2
+    across = (dp, (y + 2) % 4 * 2 + core, tensor)
+    greet(list(partners.values()) + [across])
+    pair = partners["tensor"]
+    outward = remote(mlp_out, mlp_other, pair_send.at[0], pair_recv.at[0], pair)
+    outward.start()
+    by_name = dict(
+        normed_mlp=normed_mlp, cotangent=cotangent, middle_low=middle_low, gate_grad=gate_grad,
+        up_grad=up_grad, activated=activated, attended=attended,
+    )
+    early = Scatter(
+        early_streams, [by_name[l] for l, _ in EARLY], [by_name[r] for _, r in EARLY],
+        turned, sent, held, 0, early_landed, early_send, early_recv, bits, partners,
+    )
+    early.turn()
+    early.open()
+
+    place_rows = positions[...].astype(jnp.float32)
+    segment_rows = segments[...].astype(jnp.float32)
+    query_turned[...] = jnp.zeros_like(query_turned)
+
+    def block(slot, target):
+        def column(row):
+            return jnp.broadcast_to(row.astype(jnp.float32), (rows, rows)).T
+
+        allowed = (column(meta[slot, 0:1, :]) <= place_rows) & (
+            column(meta[slot, 1:2, :]) == segment_rows
+        )
+        one = jnp.where(allowed, 0.0, NEGATIVE)
+        bias[:, :rows] = one
+        bias[:, rows:] = one
 
         def head(j):
             key, value = kv[slot, 0, j], kv[slot, 1, j]
-            scores = times_turned(query[j], key)
-            grad = times_turned(attended_grad[j], value)
-            weights, scores_grad = [], []
-            for g in range(2):
-                here = slice(g * rows, (g + 1) * rows)
-                weight = jnp.exp2(scores[here] + bias[...])
-                inside = jnp.concatenate([inner[j, here, :]] * 2, axis=1)
-                weights.append(weight.astype(LOW))
-                scores_grad.append((weight * (grad[here] - inside)).astype(LOW))
-            weights = jnp.concatenate(weights, axis=0)
-            scores_grad = jnp.concatenate(scores_grad, axis=0)
-            query_grad[j] += times(scores_grad, key)
-            kv_grad[slot, 0, j] = (
-                lax.dot_general(
-                    scores_grad, query[j], (((0,), (0,)), ((), ())),
-                    preferred_element_type=jnp.float32,
+            weight = jnp.exp2(times_turned(key, query[j]) + bias[...])
+            grad = times_turned(value, attended_grad[j])
+            scores_grad = (weight * (grad - inner[j, 0:1, :])).astype(LOW)
+            target[1, j] = times(weight.astype(LOW), attended_grad[j]).astype(LOW)
+            target[0, j] = (times(scores_grad, query[j]) * math.log(2)).astype(LOW)
+            query_turned[j] += lax.dot_general(
+                key, scores_grad, (((0,), (0,)), ((), ())), preferred_element_type=jnp.float32
+            )
+
+        over_tiles(heads, head)
+
+    sends = []
+    for i, shift in enumerate((2, 1, 3, 0)):
+        chip = (y + shift) % 4
+        block(chip * 2 + 1 - core, away_grad.at[i])
+        copy = remote(
+            away_grad.at[i], core_grad.at[i], core_send.at[i], core_recv.at[i], partners["core"]
+        )
+        copy.start()
+        block(chip * 2 + core, near_grad.at[i])
+        if i < 4:
+            early.step(i)
+        copy.wait()
+        near_grad[i] = near_grad[i] + core_grad[i]
+        if shift:
+            copy = remote(
+                near_grad.at[i],
+                far_grad.at[i],
+                far_send.at[i],
+                far_recv.at[i],
+                (dp, chip * 2 + core, tensor),
+            )
+            copy.start()
+            sends.append(copy)
+
+    q_width, k_width = wq_far.shape[1], wk_far.shape[1]
+    key_first, value_first = 2 * q_width, 2 * q_width + 2 * k_width
+    fetches = []
+    for i, (far, first) in enumerate(((wq_far, 0), (wk_far, key_first), (wv_far, value_first))):
+        width = far.shape[1]
+        for part in range(2):
+            fetches.append(
+                pltpu.make_async_copy(
+                    far.at[pl.ds(part * half, half), :],
+                    sent.at[:, pl.ds(first + part * width, width)],
+                    weight_sem.at[i, part],
                 )
-                * math.log(2)
-            ).astype(LOW)
-            kv_grad[slot, 1, j] = lax.dot_general(
-                weights, attended_grad[j], (((0,), (0,)), ((), ())),
-                preferred_element_type=jnp.float32,
-            ).astype(LOW)
-
-        over_tiles(heads, head)
-
-    over_tiles(8, block)
-
-
-def attention_backward(f, positions, segments):
+            )
+            fetches[-1].start()
+    early.step(4)
+
+    def back(raw, gain, gradient):
+        turned_back = gradient * cosine[...] - pltpu.roll(gradient, hd // 2, 1) * sine[...]
+        inverse = inverse_rms(raw)
+        scaled = turned_back * gain
+        raw_grad = inverse * scaled - raw * (inverse * inverse * inverse) * jnp.mean(
+            scaled * raw, axis=-1, keepdims=True
+        )
+        return raw_grad, jnp.sum(turned_back * raw * inverse, axis=0, keepdims=True)
+
+    gains_sent[0] = jnp.zeros_like(gains_sent[0])
+    query_gain_row = query_gain[...].astype(jnp.float32)
+    key_gain_row = key_gain[...].astype(jnp.float32)
+
+    def query_head(j):
+        gradient = query_turned[j].T * (1.0 / math.sqrt(hd))
+        for g in range(2):
+            here = at_tile(2 * j + g, hd)
+            raw_grad, part = back(
+                query_raw[:, here], query_gain_row, gradient[g * rows : (g + 1) * rows]
+            )
+            query_low[:, here] = raw_grad.astype(LOW)
+            gains_sent[0, 2:3, :hd] += part
+
+    over_tiles(heads, query_head)
+    for copy in sends:
+        copy.wait()
+
+    def key_head(j):
+        key_sum = near_grad[3, 0, j].astype(jnp.float32)
+        value_sum = near_grad[3, 1, j].astype(jnp.float32)
+        for i in range(3):
+            key_sum = key_sum + far_grad[i, 0, j].astype(jnp.float32)
+            value_sum = value_sum + far_grad[i, 1, j].astype(jnp.float32)
+        here = at_tile(j, hd)
+        raw_grad, part = back(key_raw[:, here], key_gain_row, key_sum)
+        key_low[:, here] = raw_grad.astype(LOW)
+        value_low[:, here] = value_sum.astype(LOW)
+        gains_sent[0, 3:4, :hd] += part
+
+    over_tiles(heads, key_head)
+    for fetch in fetches:
+        fetch.wait()
+    x = tokens[...].astype(jnp.float32)
+    inverse = inverse_rms(x)
+
+    def partial_tile(part):
+        def tile(i):
+            here = at_tile(i, WIDE)
+
+            def weight(first, width):
+                return sent[here, pl.ds(first + part * width, width)]
+
+            result = (
+                times_turned(query_low[...], weight(0, q_width))
+                + times_turned(key_low[...], weight(key_first, k_width))
+                + times_turned(value_low[...], weight(value_first, k_width))
+            )
+            there = pl.ds(pl.multiple_of(part * half + i * WIDE, WIDE), WIDE)
+            partial[:, there] = result.astype(LOW)
+            across_x = tokens[:, there].astype(jnp.float32) * inverse
+            gains_sent[0, 0:1, there] = jnp.sum(result * across_x, axis=0, keepdims=True)
+
+        return tile
+
+    for part in range(2):
+        over_tiles(half // WIDE, partial_tile(part))
+    outward_partial = remote(partial, partial_other, pair_send.at[1], pair_recv.at[1], pair)
+    outward_partial.start()
+    gains_sent[0, 1:2, :] = 0.5 * mlp_gain_grad[...]
+    gain_dims = ("core",) + DIMS + ("tensor",)
+
+    def send_gains(step):
+        copy = remote(
+            gains_sent.at[step], gains_landed.at[step], gains_send.at[step], gains_recv.at[step],
+            partners[gain_dims[step]],
+        )
+        copy.start()
+        return copy
+
+    def next_gains(step, copy):
+        copy.wait()
+        total = gains_sent[step] + gains_landed[step]
+        if step == len(gain_dims) - 1:
+            gains[...] = total
+            return None
+        gains_sent[step + 1] = total
+        return send_gains(step + 1)
+
+    gains_copy = send_gains(0)
+    early.step(5, early_out)
+    late = Scatter(
+        late_streams, [normed] * 3, [query_low, key_low, value_low],
+        turned, early_landed[0], early_landed[0], 2 * features, late_landed, late_send, late_recv,
+        bits, partners,
+    )
+    late.turn()
+    late.open()
+    for step in range(6):
+        late.step(step, late_out)
+        gains_copy = next_gains(step, gains_copy)
+    next_gains(6, gains_copy)
+    outward.wait()
+    outward_partial.wait()
+
+
+def backward(f, tokens, cotangent, positions, segments, query_gain, key_gain, weights):
+    rows, features = tokens.shape
+    heads, hd = f["kv"].shape[2], f["kv"].shape[4]
+    q_width, k_width = weights[0].shape[1], weights[1].shape[1]
+    hidden = f["gate_grad"].shape[1]
+    early_streams = split_streams((hidden, hidden, hidden, q_width), EARLY_TILES)
+    late_streams = split_streams((q_width, k_width, k_width), LATE_TILES)
+    early_width = 3 * hidden + q_width
+    late_width = q_width + 2 * k_width
+    half = features // 2
     vmem = pl.BlockSpec(memory_space=pltpu.VMEM)
+    far = pl.BlockSpec(memory_space=pl.ANY)
+    f32 = jnp.float32
+    outs = [
+        jax.ShapeDtypeStruct((CHUNK, early_width), f32),
+        jax.ShapeDtypeStruct((CHUNK, late_width), f32),
+        jax.ShapeDtypeStruct((rows, features), LOW),
+        jax.ShapeDtypeStruct((rows, features), LOW),
+        jax.ShapeDtypeStruct((rows, features), LOW),
+        jax.ShapeDtypeStruct((8, features), f32),
+    ]
+    kept = [
+        f[name]
+        for name in (
+            "normed", "normed_mlp", "middle_low", "gate_grad", "up_grad", "activated", "attended",
+            "query", "kv", "meta", "attended_grad", "inner", "query_raw", "key_raw", "cosine",
+            "sine", "mlp_out", "mlp_gain_grad",
+        )
+    ]
+    dma = pltpu.SemaphoreType.DMA
     return pl.pallas_call(
-        backward_kernel,
-        out_shape=[
-            jax.ShapeDtypeStruct(f["query"].shape, jnp.float32),
-            jax.ShapeDtypeStruct(f["kv"].shape, LOW),
+        functools.partial(backward_kernel, early_streams, late_streams),
+        out_shape=outs,
+        in_specs=[vmem] * 6 + [far] * 3 + [vmem] * len(kept),
+        out_specs=[vmem] * len(outs),
+        scratch_shapes=[
+            pltpu.VMEM((7, features, rows), LOW),
+            pltpu.VMEM((half, early_width), LOW),
+            pltpu.VMEM((half, early_width), LOW),
+            pltpu.VMEM((rows, 2 * rows), f32),
+            pltpu.VMEM((heads, hd, 2 * rows), f32),
+            pltpu.VMEM((4, 2, heads, rows, hd), LOW),
+            pltpu.VMEM((4, 2, heads, rows, hd), LOW),
+            pltpu.VMEM((4, 2, heads, rows, hd), LOW),
+            pltpu.VMEM((3, 2, heads, rows, hd), LOW),
+            pltpu.VMEM((rows, q_width), LOW),
+            pltpu.VMEM((rows, k_width), LOW),
+            pltpu.VMEM((rows, k_width), LOW),
+            pltpu.VMEM((7, 8, features), f32),
+            pltpu.VMEM((7, 8, features), f32),
+        ]
+        + [pltpu.VMEM((half >> step, early_width), LOW) for step in range(6)]
+        + [pltpu.VMEM((half >> step, late_width), LOW) for step in range(6)]
+        + [
+            dma((5, 6)), dma((5, 6)), dma((5, 6)), dma((5, 6)), dma((2,)), dma((2,)), dma((4,)),
+            dma((4,)), dma((3,)), dma((3,)), dma((7,)), dma((7,)), dma((3, 2)),
         ],
-        in_specs=[vmem] * 7,
-        out_specs=[vmem] * 2,
-        scratch_shapes=[pltpu.VMEM((positions.shape[1], positions.shape[1]), jnp.float32)],
-        compiler_params=pltpu.CompilerParams(vmem_limit_bytes=60 * 1024 * 1024),
-    )(f["query"], f["kv"], f["meta"], positions, segments, f["attended_grad"], f["inner"])
-
-
-def mean_rms(entries):
-    return lax.rsqrt(jnp.mean(entries * entries, axis=-1, keepdims=True) + EPS)
-
-
-def norm_back(entries, gain_vec, gradient):
-    inverse = mean_rms(entries)
-    scaled = gradient * gain_vec
-    gain_grad = jnp.sum((gradient * entries * inverse).reshape(-1, entries.shape[-1]), axis=0)
-    entries_grad = inverse * scaled - entries * inverse**3 * jnp.mean(
-        scaled * entries, axis=-1, keepdims=True
-    )
-    return (entries_grad, gain_grad)
-
-
-def dense(left, right):
-    return jnp.dot(left, right, preferred_element_type=jnp.float32)
+        compiler_params=pltpu.CompilerParams(
+            collective_id=0, has_side_effects=True, vmem_limit_bytes=62 * 1024 * 1024
+        ),
+    )(tokens, cotangent, positions, segments, query_gain, key_gain, *weights, *kept)
+
+
+def finish_kernel(
+    tokens, attention_gain, middle, mlp_out, mlp_other, grad_middle, partial, partial_other, early,
+    late, gains, output, input_grad, grad_query, grad_key, grad_value, grad_out, grad_gate,
+    grad_up, grad_down, gains_out,
+):
+    hidden, q_width, k_width = grad_gate.shape[1], grad_query.shape[1], grad_key.shape[1]
+    output[...] = (
+        middle[...] + (mlp_out[...].astype(jnp.float32) + mlp_other[...].astype(jnp.float32))
+    ).astype(LOW)
+    x = tokens[...].astype(jnp.float32)
+    inverse = inverse_rms(x)
+    scaled = (
+        partial[...].astype(jnp.float32) + partial_other[...].astype(jnp.float32)
+    ) * attention_gain[...].astype(jnp.float32)
+    input_grad[...] = (
+        grad_middle[...]
+        + inverse * scaled
+        - x * (inverse * inverse * inverse) * jnp.mean(scaled * x, axis=-1, keepdims=True)
+    ).astype(LOW)
+    grad_gate[...] = early[:, :hidden]
+    grad_up[...] = early[:, hidden : 2 * hidden]
+    grad_down[...] = early[:, 2 * hidden : 3 * hidden].T
+    grad_out[...] = early[:, 3 * hidden :].T
+    grad_query[...] = late[:, :q_width]
+    grad_key[...] = late[:, q_width : q_width + k_width]
+    grad_value[...] = late[:, q_width + k_width :]
+    chunk = lax.axis_index("dp") * 8 + lax.axis_index("seq")
+    features = gains.shape[1]
+    wide = pltpu.roll(gains[0:8, :], lax.rem(features - chunk * CHUNK, features), 1)
+    thin = pltpu.roll(gains[0:8, :128], lax.rem(128 - chunk * 2, 128), 1)
+    gains_out[0:2, :] = wide[0:2, :128]
+    gains_out[2:4, :] = thin[2:4, :]
+
+
+def finish(tokens, attention_gain, f, mlp_other, partial, partial_other, early, late, gains, widths):
+    q_width, k_width, hidden = widths
+    rows, features = tokens.shape
+    f32 = jnp.float32
+    vmem = pl.BlockSpec(memory_space=pltpu.VMEM)
+    shapes = (
+        ((rows, features), LOW), ((rows, features), LOW), ((CHUNK, q_width), f32),
+        ((CHUNK, k_width), f32), ((CHUNK, k_width), f32), ((q_width, CHUNK), f32),
+        ((CHUNK, hidden), f32), ((CHUNK, hidden), f32), ((hidden, CHUNK), f32), ((8, 128), f32),
+    )
+    return pl.pallas_call(
+        finish_kernel,
+        out_shape=[jax.ShapeDtypeStruct(shape, kind) for shape, kind in shapes],
+        in_specs=[vmem] * 11,
+        out_specs=[vmem] * len(shapes),
+        compiler_params=pltpu.CompilerParams(vmem_limit_bytes=40 * 1024 * 1024),
+    )(
+        tokens, attention_gain, f["middle"], f["mlp_out"], mlp_other, f["grad_middle"], partial,
+        partial_other, early, late, gains,
+    )
 
 
 def shards(
@@ -782,105 +951,28 @@
     up_weight,
     down_weight,
 ):
-    head_dim = query_gain.shape[0]
-    local_rows = tokens.shape[1]
-    key_heads = key_weight.shape[1] // head_dim
-    query_heads = query_weight.shape[1] // head_dim
     f = forward(
         tokens[0], cotangent[0], positions, segments, attention_gain[None], query_weight,
         key_weight, value_weight, query_gain[None], key_gain[None], out_weight, mlp_gain[None],
         gate_weight, up_weight, down_weight,
     )
-    score_scale = 1.0 / math.sqrt(head_dim)
-    attention_gain = attention_gain.astype(jnp.float32)
-    query_gain = query_gain.astype(jnp.float32)
-    key_gain = key_gain.astype(jnp.float32)
-    inputs = tokens[0].astype(jnp.float32)
-    query_grad_blocks, kv_grad_all = attention_backward(f, positions, segments)
-    mlp_other = lax.ppermute(f["mlp_out"], "tensor", ((0, 1), (1, 0)))
-    output = (
-        f["middle"] + (f["mlp_out"].astype(jnp.float32) + mlp_other.astype(jnp.float32))
-    ).astype(jnp.bfloat16)[None]
-    kv_grad = lax.psum_scatter(kv_grad_all, "seq", scatter_dimension=0, tiled=True)[0]
-    cosine_table, sine_table = f["cosine"][:, None, :], f["sine"][:, None, :]
-
-    def unrotate(gradient):
-        half_dim = head_dim // 2
-        turned = jnp.concatenate([gradient[..., half_dim:], gradient[..., :half_dim]], axis=-1)
-        return gradient * cosine_table - turned * sine_table
-
-    query_rot_grad = (
-        query_grad_blocks.reshape(key_heads, 2, local_rows, head_dim)
-        .transpose(2, 0, 1, 3)
-        .reshape(local_rows, query_heads, head_dim)
-        * score_scale
-    )
-    query_raw_grad, query_gain_part = norm_back(
-        f["query_raw"].reshape(local_rows, query_heads, head_dim),
-        query_gain,
-        unrotate(query_rot_grad),
-    )
-    key_raw_grad, key_gain_part = norm_back(
-        f["key_raw"].reshape(local_rows, key_heads, head_dim),
-        key_gain,
-        unrotate(kv_grad[0].astype(jnp.float32).transpose(1, 0, 2)),
-    )
-    query_grad_low = query_raw_grad.reshape(local_rows, -1).astype(jnp.bfloat16)
-    key_grad_low = key_raw_grad.reshape(local_rows, -1).astype(jnp.bfloat16)
-    value_grad_low = kv_grad[1].transpose(1, 0, 2).reshape(local_rows, -1)
-    normed, normed_mlp, middle_low = f["normed"], f["normed_mlp"], f["middle_low"]
-    attended_low, grad_middle = f["attended"], f["grad_middle"]
-    gate_grad_low, up_grad_low, activated = f["gate_grad"], f["up_grad"], f["activated"]
-    upstream = cotangent[0]
-    mlp_gain_grad = f["mlp_gain_grad"][0]
-    attention_partial = (
-        dense(query_grad_low, query_weight.T)
-        + dense(key_grad_low, key_weight.T)
-        + dense(value_grad_low, value_weight.T)
-    )
-    partial_low = attention_partial.astype(jnp.bfloat16)
-    attention_gain_part = jnp.sum(attention_partial * inputs * mean_rms(inputs), axis=0)
-    width = gate_weight.shape[1]
-    q_width, k_width = query_weight.shape[1], key_weight.shape[1]
-    pieces = (
-        ((0, 0, 0, width),),
-        ((0, 1, 0, width),),
-        ((1, 2, 0, width),),
-        ((2, 3, 0, q_width), (2, 4, q_width, k_width)),
-        ((2, 5, 0, k_width), (3, 6, k_width, q_width)),
-    )
-    shares, gains, partial_other = scatter_gradients(
-        pieces,
-        (normed_mlp, upstream, normed, middle_low),
-        (
-            gate_grad_low,
-            up_grad_low,
-            activated,
-            query_grad_low,
-            key_grad_low,
-            value_grad_low,
-            attended_low,
-        ),
-        pack_gains(attention_gain_part, 0.5 * mlp_gain_grad, query_gain_part, key_gain_part),
-        partial_low,
-    )
-    normed_grad = partial_low.astype(jnp.float32) + partial_other.astype(jnp.float32)
-    input_part, _ = norm_back(inputs, attention_gain, normed_grad)
-    input_grad = (grad_middle + input_part).astype(jnp.bfloat16)[None]
+    early, late, mlp_other, partial, partial_other, gains = backward(
+        f, tokens[0], cotangent[0], positions, segments, query_gain[None], key_gain[None],
+        (query_weight, key_weight, value_weight),
+    )
+    results = finish(
+        tokens[0], attention_gain[None], f, mlp_other, partial, partial_other, early, late, gains,
+        (query_weight.shape[1], key_weight.shape[1], gate_weight.shape[1]),
+    )
+    gains = results[-1]
     return (
-        output,
-        input_grad,
-        shares[3][:, :q_width],
-        shares[3][:, q_width:],
-        shares[4][:, :k_width],
-        shares[4][:, k_width:].T,
-        shares[0],
-        shares[1],
-        shares[2].T,
-        gains[0, 0:16],
-        gains[0, 16:32],
-        gains[0, 32:34],
-        gains[0, 34:36],
+        results[0][None],
+        results[1][None],
+        *results[2:-1],
+        gains[0, :CHUNK],
+        gains[1, :CHUNK],
+        gains[2, :2],
+        gains[3, :2],
     )
 
 

time: 247 us -> 208 us (0.84)
  Pallas kernels: 172 us -> 192 us
  other arithmetic: 20.6 us -> 0.6 us
  between operations: 14.4 us -> 0.73 us
  local copies, waits for them, and re-layouts: 26.7 us -> 13.5 us
  waiting for transfers between devices: 7.6 us -> 0 us
  matrix products: 3.8 us -> 0 us
    pallas_call x2, Pallas kernels: 95.3 us -> 116 us  [the longest x1 114 us: backward(): pl.pallas_call(functools.partial(backward_kernel, early_streams, late_str...]
    reduce_sum x6 -> x0, other arithmetic: 8.02 us -> none  [the longest x2 3.61 us: norm_back(): jnp.sum((gradient * entries * inverse).reshape(-1, entries.shape[-1]), ax...]
    reduce_scatter x1 -> x0, waiting for transfers between devices: 7.58 us -> none  [shards(): lax.psum_scatter(kv_grad_all, 'seq', scatter_dimension=0, tiled=True)[0]]
    unnamed x54 -> x24, local copies, waits for them, and re-layouts: 3.22 us -> 9.91 us
    reshape x7 -> x0, local copies, waits for them, and re-layouts: 6.21 us -> none  [the longest x1 2.04 us: shards(): query_grad_blocks.reshape(key_heads, 2, local_rows, head_dim)]
    broadcast_in_dim x2 -> x0, other arithmetic: 4.5 us -> none  [the longest x1 2.28 us: shards(): (f['middle'] + (f['mlp_out'].astype(jnp.float32) + mlp_other.astype(jnp.f...]
    slice x4 -> x0, local copies, waits for them, and re-layouts: 4.47 us -> none  [the longest x1 1.52 us: shards(): shares[3][:, :q_width]]
    dot_general x3 -> x0, matrix products: 3.8 us -> none  [dense(): return jnp.dot(left, right, preferred_element_type=jnp.float32)]
  transfers between devices with their start and end apart: 2 -> 0, of which waited for: 1 -> 0; matrix products, arithmetic and copies ran while one was open for 11% -> 0% of each run, Pallas kernels for 0% -> 0%
where the time goes in v3:
time: 208 us; the launch traced here: 207 us
  Pallas kernels  192 us (92%)
  local copies, waits for them, and re-layouts  13.5 us (6%)
    pallas_call x1, Pallas kernels, backward(): pl.pallas_call(functools.partial(backward_kernel, early_streams, late_str...  114 us
    pallas_call x1, Pallas kernels, forward(): pl.pallas_call(forward_kernel, out_shape=[jax.ShapeDtypeStruct(shape, kin...  76.4 us
    unnamed x24, local copies, waits for them, and re-layouts  9.91 us

profile of v3, /device:TPU:0, one launch (start us, length us, event | category | flops | bytes accessed | tf_op | source)
XLA Modules:
  0.0 207.0 jit_solution(3989348968195322649)
XLA Ops:
  0.7 0.6 maximum_bitcast_fusion.frequencies
  1.2 1.3 broadcast_in_dim.24.attention_gain
  2.5 1.3 broadcast_in_dim.28.mlp_gain
  3.8 76.4 %shard_map.246 = (bf16[256,1024]{1,0:T(8,128)(2,1)}, f32[256,1024]{1,0:T(8,128)}, f32[256,512]{1,0:T(8,128)}, bf16[4,512,128]{2,1,0:T(8,128)(2,1)}, bf16[8,2,4,2...) custom-call(bf16[256,1024]{1,0:T(8,128)(2,1)} %bitcast.16, ...), custom_call_target="tpu_custom_call" | custom-call | tf_op jit(solution)/shard_map/pallas_call | solution.py:455
  80.2 0.0 copy-start
  80.2 0.0 copy-start.1
  80.2 0.0 copy-start.9
  80.2 113.7 %shard_map.247 = (f32[16,5632]{1,0:T(8,128)}, f32[16,2048]{1,0:T(8,128)}, bf16[256,1024]{1,0:T(8,128)(2,1)}, bf16[256,1024]{1,0:T(8,128)(2,1)}, bf16[256,1024]{1,0:T(8,128)(2,1)}, /*index=5*/f32[8,1024]{1,0:T(8,128)}) custom-call(bf16[256,1024]{1,0:T(8,128)(2,1)} %bitcast.17, bf16[256,1024]{1,0:T(8,128)(2,1)} %bitcast.20, s32[1,256]{1,0:T(1,128)} %refs_2_.1, ...), custom_call_target="tpu_custom_call" | custom-call | tf_op jit(solution)/shard_map/pallas_call | solution.py:848
  193.9 0.0 copy-done
  194.0 0.0 copy-done.1
  194.0 0.0 copy-done.9
  194.0 0.0 copy-start.2
  194.0 1.2 copy-done.2
  195.2 0.0 copy-start.3
  195.2 1.2 copy-done.3
  196.4 0.0 copy-start.4
  196.4 1.0 copy-done.4
  197.5 0.0 copy-start.5
  197.5 1.0 copy-done.5
  198.5 0.0 copy-start.6
  198.5 1.0 copy-done.6
  199.6 0.0 copy-start.7
  199.6 1.0 copy-done.7
  200.5 0.0 copy-start.8
  200.5 0.9 copy-done.8
  201.4 0.0 copy-start.10
  201.4 0.8 copy-done.10
  202.2 2.1 shard_map.248
  204.3 0.5 slice_bitcast_fusion.2
  204.8 0.5 slice_bitcast_fusion
  205.3 0.8 copy.28
  206.1 0.9 copy.29
  (1 shorter events, 0.0 us)
Async XLA Ops:
  80.2 113.8 %copy-start = (bf16[1,256,1024]{2,1,0:T(8,128)(2,1)S(1)}, bf16[1,256,1024]{2,1,0:T(8,128)(2,1)}, u32[]{:S(2)}) copy-start(bf16[1,256,1024]{2,1,0:T(8,128)(2,1)} %param.15) | copy-start | bytes 1572868
  80.2 113.8 %copy-start.1 = (bf16[256,1024]{1,0:T(8,128)(2,1)S(1)}, bf16[256,1024]{1,0:T(8,128)(2,1)}, u32[]{:S(2)}) copy-start(bf16[256,1024]{1,0:T(8,128)(2,1)} %get-tuple-element.50.refs_25_.mlp_out) | copy-start | bytes 1572868
  80.2 113.8 %copy-start.9 = (bf16[1,1024]{1,0:T(2,128)(2,1)S(1)}, bf16[1,1024]{1,0:T(2,128)(2,1)}, u32[]{:S(2)}) copy-start(bf16[1,1024]{1,0:T(2,128)(2,1)} %broadcast_in_dim.24.attention_gain) | copy-start | bytes 6148
  194.0 1.2 copy-start.2
  195.2 1.2 copy-start.3
  196.4 1.0 copy-start.4
  197.5 1.0 copy-start.5
  198.5 1.0 copy-start.6
  199.6 1.0 copy-start.7
  200.5 0.9 copy-start.8
  201.4 0.8 copy-start.10

commit v4 on v3

v4 whole, which is shorter than its diff:
```python
import functools
import math

import jax
import jax.numpy as jnp
from jax import lax
from jax.experimental import pallas as pl
from jax.experimental.pallas import tpu as pltpu
from jax.sharding import PartitionSpec as P

EPS = 1e-06
ROPE_BASE = 1000000.0
NEGATIVE = -1e30


MESH = pl.DeviceIdType.MESH
CHUNK = 16
DIMS = ("x3", "x1", "y3", "y1", "z")
LOW = jnp.bfloat16


def place():
    dp = lax.axis_index("dp")
    seq = lax.axis_index("seq")
    tensor = lax.axis_index("tensor")
    x, z = dp // 2, dp % 2
    y, core = seq // 2, seq % 2
    x_near = x + 1 - 2 * (x % 2)
    y_near = y + 1 - 2 * (y % 2)
    bits = {
        "core": core,
        "x3": x // 2,
        "x1": (x // 2 + x % 2) % 2,
        "y3": y // 2,
        "y1": (y // 2 + y % 2) % 2,
        "z": z,
    }
    partners = {
        "core": (dp, seq + 1 - 2 * core, tensor),
        "x3": ((3 - x) * 2 + z, seq, tensor),
        "x1": (x_near * 2 + z, seq, tensor),
        "y3": (dp, (3 - y) * 2 + core, tensor),
        "y1": (dp, y_near * 2 + core, tensor),
        "z": (dp + 1 - 2 * z, seq, tensor),
        "tensor": (dp, seq, 1 - tensor),
    }
    return bits, partners


def greet(partners):
    barrier = pltpu.get_barrier_semaphore()
    for partner in partners:
        pl.semaphore_signal(barrier, inc=1, device_id=partner, device_id_type=MESH)
    pl.semaphore_wait(barrier, len(partners))


ORDERS = (
    ("core", "x3", "x1", "z", "y3", "y1"),
    ("core", "x1", "x3", "z", "y1", "y3"),
    ("core", "y3", "z", "x1", "x3", "y1"),
    ("core", "y1", "z", "x3", "x1", "y3"),
    ("core", "z", "x1", "x3", "y3", "y1"),
)


def slot_chunks(order):
    chunks = []
    for slot in range(2 ** len(order)):
        bit = {d: (slot >> (len(order) - 1 - i)) & 1 for i, d in enumerate(order)}
        x = 2 * bit["x3"] + (bit["x3"] ^ bit["x1"])
        y = 2 * bit["y3"] + (bit["y3"] ^ bit["y1"])
        chunks.append(((x * 2 + bit["z"]) * 4 + y) * 2 + bit["core"])
    return chunks


def remote(source, target, out_sem, in_sem, partner):
    return pltpu.make_async_remote_copy(
        src_ref=source,
        dst_ref=target,
        send_sem=out_sem,
        recv_sem=in_sem,
        device_id=partner,
        device_id_type=MESH,
    )


def over_tiles(count, body):
    def step(i, _):
        body(i)
        return 0

    lax.fori_loop(0, count, step, 0)


def at_tile(i, size):
    return pl.ds(pl.multiple_of(i * size, size), size)


def times(left, right):
    return jnp.dot(left, right, preferred_element_type=jnp.float32)


def times_turned(left, right):
    return lax.dot_general(
        left, right, (((1,), (1,)), ((), ())), preferred_element_type=jnp.float32
    )


def inverse_rms(entries):
    return lax.rsqrt(jnp.mean(entries * entries, axis=-1, keepdims=True) + EPS)


EARLY_TILES = (6, 6, 4, 2, 4)
LATE_TILES = (2, 2, 2, 1, 1)
SHIFTS = (2, 1, 3, 0)
WIDE = 256


def split_streams(sizes, tiles):
    bounds, start = [], 0
    for size in sizes:
        bounds.append((start, start + size))
        start += size
    streams, first = [], 0
    for count in tiles:
        last = first + count * WIDE
        pieces = []
        for matrix, (low, high) in enumerate(bounds):
            begin, end = max(first, low), min(last, high)
            if begin < end:
                pieces.append((matrix, begin - low, begin, end - begin))
        streams.append((first, last - first, pieces))
        first = last
    assert first == start
    return streams


class Panels:
    def __init__(self, rows, panels):
        self.rows = rows
        self.panels = panels

    def find(self, first):
        start = 0
        for ref, row, columns in self.panels:
            if first < start + columns:
                return ref, row, first - start
            start += columns
        raise ValueError


class Scatter:
    def __init__(self, streams, lhs, rhs, turned, sent, held, landed, send_sem, recv_sem, bits, partners):
        self.streams, self.lhs, self.rhs = streams, lhs, rhs
        self.turned, self.sent, self.held = turned, sent, held
        self.landed, self.send_sem, self.recv_sem = landed, send_sem, recv_sem
        self.bits, self.partners = bits, partners
        self.half = sent.rows
        self.copies = {}
        self.base = [0] * len(streams)

    def open(self, s):
        first, columns, pieces = self.streams[s]
        core = self.bits["core"]
        chunks = slot_chunks(ORDERS[s])
        for kept in (False, True):
            ref, row, column = (self.held if kept else self.sent).find(first)
            offset = core * self.half if kept else (1 - core) * self.half
            for index, (matrix, left_column, begin, width) in enumerate(pieces):
                if not kept:
                    flipped = self.lhs[matrix][...].T
                    for slot, chunk in enumerate(chunks):
                        self.turned[index, slot * CHUNK : (slot + 1) * CHUNK, :] = flipped[
                            chunk * CHUNK : (chunk + 1) * CHUNK, :
                        ]
                target = column + begin - first
                right = self.rhs[matrix]

                def tile(i, index=index, right=right, left_column=left_column, target=target):
                    here = pl.multiple_of(i * WIDE, WIDE)
                    ref[row : row + self.half, pl.ds(target + here, WIDE)] = times(
                        self.turned[index, pl.ds(pl.multiple_of(offset, CHUNK), self.half), :],
                        right[:, pl.ds(left_column + here, WIDE)],
                    ).astype(LOW)

                over_tiles(width // WIDE, tile)
            if not kept:
                self.send(
                    0, s, ref.at[pl.ds(row, self.half), pl.ds(column, columns)]
                )

    def send(self, step, s, source):
        first, columns, _ = self.streams[s]
        ref, column = self.landed[step]
        copy = remote(
            source,
            ref.at[:, pl.ds(column + first, columns)],
            self.send_sem.at[s, step],
            self.recv_sem.at[s, step],
            self.partners[ORDERS[s][step]],
        )
        copy.start()
        self.copies[s, step] = copy

    def step(self, step, out=None, streams=range(5)):
        rows = self.half >> step
        for s in streams:
            first, columns, _ = self.streams[s]
            self.copies[s, step].wait()
            ref, row, column = self.held.find(first)
            mine = pl.ds(column, columns)
            landed, from_column = self.landed[step]
            theirs = pl.ds(from_column + first, columns)
            if step == 5:
                out[:, pl.ds(first, columns)] = ref[
                    pl.ds(pl.multiple_of(row + self.base[s], CHUNK), CHUNK), mine
                ].astype(jnp.float32) + landed[:, theirs].astype(jnp.float32)
                continue
            tile = min(rows, 64)

            def add(i, s=s, tile=tile, ref=ref, row=row, mine=mine, landed=landed, theirs=theirs):
                start = pl.multiple_of(i * tile, tile)
                here = pl.ds(pl.multiple_of(row + self.base[s] + start, tile), tile)
                ref[here, mine] = ref[here, mine] + landed[pl.ds(start, tile), theirs]

            over_tiles(rows // tile, add)
            bit = self.bits[ORDERS[s][step + 1]]
            away = pl.multiple_of(row + self.base[s] + (1 - bit) * (rows // 2), CHUNK)
            self.send(step + 1, s, ref.at[pl.ds(away, rows // 2), mine])
            self.base[s] = self.base[s] + bit * (rows // 2)


def layer_kernel(early_streams, late_streams, *refs):
    (
        tokens, cotangent, positions, segments, frequencies, attention_gain, query_gain,
        key_gain, mlp_gain, wq_far, wk_far, wv_far, wo_far, wg_far, wu_far, wd_far, middle,
        mlp_out, mlp_other, grad_middle, partial, partial_other, early_out, late_out, gains,
        normed, query_raw, key_raw, query, kv, meta, cosine, sine, attended, normed_mlp,
        activated, gate_grad, up_grad, middle_low, attended_grad, inner, mlp_gain_grad, wq, wk,
        wv, wo, wg, wu, wd, bias, total, weight_sum, act_grad, part_out, part_in, turned, held,
        far_grad, gains_sent, gains_landed, weight_sem, kv_send, kv_recv, meta_send, meta_recv,
        pair_send, pair_recv, early_send, early_recv, late_send, late_recv, core_send,
        core_recv, far_send, far_recv, gains_send, gains_recv,
    ) = refs[: -11]
    early_landed, late_landed = refs[-11:-5], refs[-5:]
    bits, partners = place()
    dp, seq, tensor = lax.axis_index("dp"), lax.axis_index("seq"), lax.axis_index("tensor")
    core, y = seq % 2, seq // 2
    after, before, across = (y + 1) % 4, (y + 3) % 4, (y + 2) % 4
    near = (dp, y * 2 + 1 - core, tensor)
    ahead = (dp, after * 2 + core, tensor)
    behind = (dp, before * 2 + core, tensor)
    pair = (dp, seq, 1 - tensor)
    others = [(dp, (seq + step) % 8, tensor) for step in range(1, 8)]
    rows = tokens.shape[0]
    heads = kv.shape[2]
    hd = kv.shape[4]
    greet(others + [partners[name] for name in ("x3", "x1", "z", "tensor")])
    fetches = [
        pltpu.make_async_copy(far, held, weight_sem.at[i])
        for i, (far, held) in enumerate(
            zip(
                (wk_far, wv_far, wq_far, wo_far, wd_far, wg_far, wu_far),
                (wk, wv, wq, wo, wd, wg, wu),
            )
        )
    ]
    for fetch in fetches:
        fetch.start()
    got_wk, got_wv, got_wq, got_wo, got_wd, got_wg, got_wu = fetches

    meta[seq] = jnp.zeros_like(meta[seq])
    meta[seq, 0:1, :] = positions[...]
    meta[seq, 1:2, :] = segments[...]
    metas = [
        remote(meta.at[seq], meta.at[seq], meta_send.at[i], meta_recv.at[i], other)
        for i, other in enumerate(others)
    ]
    for copy in metas:
        copy.start()

    place_rows = jnp.broadcast_to(positions[...].astype(jnp.float32), (rows, rows)).T
    segment_rows = jnp.broadcast_to(segments[...].astype(jnp.float32), (rows, rows)).T
    angle = place_rows[:, :hd] * frequencies[...]
    cosine[...] = jnp.cos(angle)
    lane = lax.broadcasted_iota(jnp.int32, (rows, hd), 1)
    sine[...] = jnp.where(lane < hd // 2, -1.0, 1.0) * jnp.sin(angle)

    def turn(entries):
        return entries * cosine[...] + pltpu.roll(entries, hd // 2, 1) * sine[...]

    x = tokens[...].astype(jnp.float32)
    normed[...] = (x * inverse_rms(x) * attention_gain[...].astype(jnp.float32)).astype(LOW)

    tile = 2 * hd
    got_wk.wait()

    def key_tile(i):
        raw = times(normed[...], wk[:, at_tile(i, tile)])
        key_raw[:, at_tile(i, tile)] = raw
        for g in range(2):
            head = raw[:, g * hd : (g + 1) * hd]
            scaled = head * inverse_rms(head) * key_gain[...].astype(jnp.float32)
            kv[seq, 0, 2 * i + g] = turn(scaled).astype(LOW)

    over_tiles(heads // 2, key_tile)

    def own(half, kind, target, index):
        copy = remote(
            kv.at[seq, half], kv.at[seq, half], kv_send.at[index], kv_recv.at[kind, half], target
        )
        copy.start()
        return copy

    sends = [own(0, 1, ahead, 0), own(0, 2, behind, 1), own(0, 0, near, 2)]
    got_wv.wait()

    def value_tile(i):
        raw = times(normed[...], wv[:, at_tile(i, tile)]).astype(LOW)
        for g in range(2):
            kv[seq, 1, 2 * i + g] = raw[:, g * hd : (g + 1) * hd]

    over_tiles(heads // 2, value_tile)
    sends += [own(1, 1, ahead, 3), own(1, 2, behind, 4), own(1, 0, near, 5)]
    got_wq.wait()
    scale = math.log2(math.e) / math.sqrt(hd)

    def query_tile(i):
        raw = times(normed[...], wq[:, at_tile(i, tile)])
        query_raw[:, at_tile(i, tile)] = raw
        for g in range(2):
            head = raw[:, g * hd : (g + 1) * hd]
            scaled = head * inverse_rms(head) * (query_gain[...].astype(jnp.float32) * scale)
            query[i, g * rows : (g + 1) * rows, :] = turn(scaled).astype(LOW)

    over_tiles(heads, query_tile)
    total[...] = jnp.zeros_like(total)
    weight_sum[...] = jnp.zeros_like(weight_sum)
    for copy in metas:
        copy.wait()

    def attend(slot):
        key_place = meta[slot, 0:1, :].astype(jnp.float32)
        key_segment = meta[slot, 1:2, :].astype(jnp.float32)
        allowed = (key_place <= place_rows) & (key_segment == segment_rows)
        bias[:, :rows] = jnp.where(allowed, 0.0, NEGATIVE)

        def head(j):
            scores = times_turned(query[j], kv[slot, 0, j])
            weights = jnp.concatenate(
                [jnp.exp2(scores[g * rows : (g + 1) * rows] + bias[:, :rows]) for g in range(2)], axis=0
            )
            weight_sum[j] += weights[:, :hd] + weights[:, hd:]
            total[j] += times(weights.astype(LOW), kv[slot, 1, j])

        over_tiles(heads, head)

    def arrived(slot, kind, half):
        remote(
            kv.at[slot, half], kv.at[slot, half], kv_send.at[0], kv_recv.at[kind, half], near
        ).wait_recv()

    def pass_on(slot, half, kind, target, index):
        copy = remote(
            kv.at[slot, half], kv.at[slot, half], kv_send.at[index], kv_recv.at[kind, half], target
        )
        copy.start()
        sends.append(copy)

    attend(seq)
    near_slot = y * 2 + 1 - core
    arrived(near_slot, 0, 0)
    arrived(near_slot, 0, 1)
    attend(near_slot)
    before_slot, after_slot, across_slot = before * 2 + core, after * 2 + core, across * 2 + core
    arrived(before_slot, 1, 0)
    pass_on(before_slot, 0, 3, ahead, 6)
    pass_on(before_slot, 0, 4, near, 7)
    arrived(after_slot, 2, 0)
    pass_on(after_slot, 0, 5, near, 8)
    arrived(after_slot, 2, 1)
    pass_on(after_slot, 1, 3, behind, 9)
    pass_on(after_slot, 1, 5, near, 10)
    arrived(before_slot, 1, 1)
    pass_on(before_slot, 1, 4, near, 11)
    attend(before_slot)
    attend(after_slot)
    for far_y, kind in ((before, 4), (after, 5)):
        slot = far_y * 2 + 1 - core
        arrived(slot, kind, 0)
        arrived(slot, kind, 1)
        attend(slot)
    arrived(across_slot, 3, 0)
    pass_on(across_slot, 0, 6, near, 12)
    arrived(across_slot, 3, 1)
    pass_on(across_slot, 1, 6, near, 13)
    attend(across_slot)
    far_slot = across * 2 + 1 - core
    arrived(far_slot, 6, 0)
    arrived(far_slot, 6, 1)
    attend(far_slot)

    def finish(j):
        inverse = 1.0 / jnp.sum(weight_sum[j], axis=-1, keepdims=True)
        result = total[j] * inverse
        total[j] = result
        weight_sum[j] = jnp.broadcast_to(inverse, result.shape)
        for g in range(2):
            attended[:, at_tile(2 * j + g, hd)] = result[g * rows : (g + 1) * rows].astype(LOW)

    over_tiles(heads, finish)
    got_wo.wait()
    wide = 256
    features = tokens.shape[1]
    hidden = wg.shape[1]

    def out_tile(i):
        part_out[0, :, at_tile(i, wide)] = times(attended[...], wo[:, at_tile(i, wide)]).astype(LOW)

    over_tiles(features // wide, out_tile)
    first = remote(part_out.at[0], part_in.at[0], pair_send.at[0], pair_recv.at[0], pair)
    first.start()
    got_wd.wait()

    def act_grad_tile(i):
        act_grad[:, at_tile(i, wide)] = times_turned(cotangent[...], wd[at_tile(i, wide), :])

    over_tiles(hidden // wide, act_grad_tile)
    got_wg.wait()
    got_wu.wait()
    first.wait()
    mid = (
        tokens[...].astype(jnp.float32)
        + (part_out[0].astype(jnp.float32) + part_in[0].astype(jnp.float32))
    )
    middle[...] = mid
    normed_mlp[...] = (mid * inverse_rms(mid) * mlp_gain[...].astype(jnp.float32)).astype(LOW)

    def hidden_tile(i):
        here = at_tile(i, wide)
        gate_here = times(normed_mlp[...], wg[:, here])
        up_here = times(normed_mlp[...], wu[:, here])
        sigmoid = 1.0 / (1.0 + jnp.exp(-gate_here))
        silu = gate_here * sigmoid
        grad = act_grad[:, here]
        activated[:, here] = (silu * up_here).astype(LOW)
        gate_grad[:, here] = (
            grad * up_here * sigmoid * (1.0 + gate_here * (1.0 - sigmoid))
        ).astype(LOW)
        up_grad[:, here] = (grad * silu).astype(LOW)

    over_tiles(hidden // wide, hidden_tile)

    def back_tile(i):
        here = at_tile(i, wide)
        part_out[1, :, here] = (
            times_turned(gate_grad[...], wg[here, :]) + times_turned(up_grad[...], wu[here, :])
        ).astype(LOW)

    over_tiles(features // wide, back_tile)
    second = remote(part_out.at[1], part_in.at[1], pair_send.at[1], pair_recv.at[1], pair)
    second.start()

    def down_tile(i):
        mlp_out[:, at_tile(i, wide)] = times(activated[...], wd[:, at_tile(i, wide)]).astype(LOW)

    over_tiles(features // wide, down_tile)
    half = features // 2
    early = Scatter(
        early_streams, [normed_mlp, normed_mlp, cotangent, middle_low],
        [gate_grad, up_grad, activated, attended], turned,
        Panels(half, [(wg, 0, hidden), (wg, half, hidden), (wu, 0, hidden), (wu, half, hidden)]),
        Panels(half, [(held, 0, held.shape[1])]), [(ref, 0) for ref in early_landed],
        early_send, early_recv, bits, partners,
    )
    for s in range(4):
        early.open(s)
    early.step(0, streams=range(4))
    for copy in sends:
        copy.wait_send()
    second.wait()
    outward = remote(mlp_out, mlp_other, pair_send.at[2], pair_recv.at[2], pair)
    outward.start()
    mid = middle[...]
    inverse = inverse_rms(mid)
    dy = part_out[1].astype(jnp.float32) + part_in[1].astype(jnp.float32)
    mlp_gain_grad[...] = jnp.sum(dy * mid * inverse, axis=0, keepdims=True)
    scaled = dy * mlp_gain[...].astype(jnp.float32)
    grad = (
        cotangent[...].astype(jnp.float32)
        + inverse * scaled
        - mid * (inverse * inverse * inverse) * jnp.mean(scaled * mid, axis=-1, keepdims=True)
    )
    grad_middle[...] = grad
    middle_low[...] = grad.astype(LOW)

    def attended_grad_tile(j):
        both = times_turned(middle_low[...], wo[at_tile(j, 2 * hd), :]).astype(LOW)
        both = both.astype(jnp.float32)
        for g in range(2):
            here = slice(g * rows, (g + 1) * rows)
            normal = both[:, g * hd : (g + 1) * hd] * weight_sum[j, here, :]
            attended_grad[j, here, :] = normal.astype(LOW)
            summed = jnp.sum((normal * total[j, here, :]).T, axis=0, keepdims=True)
            inner[j, :, here] = jnp.broadcast_to(summed, (8, rows))

    over_tiles(heads, attended_grad_tile)


    early.open(4)
    place_row = positions[...].astype(jnp.float32)
    segment_row = segments[...].astype(jnp.float32)
    act_grad[...] = jnp.zeros_like(act_grad)

    def query_turned(j):
        return pl.ds(pl.multiple_of(j % 2 * hd, hd), hd), at_tile(j // 2, 2 * rows)

    def block(slot, target, first):
        def column(row):
            return jnp.broadcast_to(row.astype(jnp.float32), (rows, rows)).T

        allowed = (column(meta[slot, 0:1, :]) <= place_row) & (
            column(meta[slot, 1:2, :]) == segment_row
        )
        one = jnp.where(allowed, 0.0, NEGATIVE)
        bias[:, :rows] = one
        bias[:, rows:] = one

        def head(j):
            key, value = kv[slot, 0, j], kv[slot, 1, j]
            weight = jnp.exp2(times_turned(key, query[j]) + bias[...])
            grad = times_turned(value, attended_grad[j])
            scores_grad = (weight * (grad - inner[j, 0:1, :])).astype(LOW)
            down = pl.ds(first, rows)
            target[down, at_tile(heads + j, hd)] = times(
                weight.astype(LOW), attended_grad[j]
            ).astype(LOW)
            target[down, at_tile(j, hd)] = (times(scores_grad, query[j]) * math.log(2)).astype(LOW)
            act_grad[query_turned(j)] += lax.dot_general(
                key, scores_grad, (((0,), (0,)), ((), ())), preferred_element_type=jnp.float32
            )

        over_tiles(heads, head)

    grad_width = 2 * heads * hd
    far_sends, crossing = [], []

    def grad_rows(ref, i):
        return ref.at[pl.ds(i * rows, rows), pl.ds(0, grad_width)]

    for i, shift in enumerate(SHIFTS):
        chip = (y + shift) % 4
        block(chip * 2 + 1 - core, wg, i * rows)
        copy = remote(
            grad_rows(wg, i), grad_rows(wd, i), core_send.at[i], core_recv.at[i], partners["core"]
        )
        copy.start()
        block(chip * 2 + core, wu, i * rows)
        copy.wait()
        down, wide_grad = slice(i * rows, (i + 1) * rows), slice(0, grad_width)
        wu[down, wide_grad] = wu[down, wide_grad] + wd[down, wide_grad]
        if shift:
            copy = remote(
                grad_rows(wu, i),
                far_grad.at[i],
                far_send.at[i],
                far_recv.at[i],
                (dp, chip * 2 + core, tensor),
            )
            copy.start()
            far_sends.append(copy)
        if i == 0:
            early.step(0, streams=range(4, 5))
    early.step(1)

    def back(raw, gain, gradient):
        turned_back = gradient * cosine[...] - pltpu.roll(gradient, hd // 2, 1) * sine[...]
        inverse = inverse_rms(raw)
        scaled = turned_back * gain
        raw_grad = inverse * scaled - raw * (inverse * inverse * inverse) * jnp.mean(
            scaled * raw, axis=-1, keepdims=True
        )
        return raw_grad, jnp.sum(turned_back * raw * inverse, axis=0, keepdims=True)

    gains_sent[0] = jnp.zeros_like(gains_sent[0])
    query_gain_row = query_gain[...].astype(jnp.float32)
    key_gain_row = key_gain[...].astype(jnp.float32)

    def query_head(j):
        gradient = act_grad[query_turned(j)].T * (1.0 / math.sqrt(hd))
        for g in range(2):
            here = at_tile(2 * j + g, hd)
            raw_grad, part = back(
                query_raw[:, here], query_gain_row, gradient[g * rows : (g + 1) * rows]
            )
            attended[:, here] = raw_grad.astype(LOW)
            gains_sent[0, 2:3, :hd] += part

    over_tiles(heads, query_head)
    early.step(2)
    for copy in far_sends:
        copy.wait()

    def key_head(j):
        here, there = at_tile(j, hd), at_tile(heads + j, hd)
        key_sum = wu[3 * rows : 4 * rows, here].astype(jnp.float32)
        value_sum = wu[3 * rows : 4 * rows, there].astype(jnp.float32)
        for i in range(3):
            key_sum = key_sum + far_grad[i, :, here].astype(jnp.float32)
            value_sum = value_sum + far_grad[i, :, there].astype(jnp.float32)
        raw_grad, part = back(key_raw[:, here], key_gain_row, key_sum)
        gate_grad[:, here] = raw_grad.astype(LOW)
        up_grad[:, here] = value_sum.astype(LOW)
        gains_sent[0, 3:4, :hd] += part

    over_tiles(heads, key_head)
    x = tokens[...].astype(jnp.float32)
    inverse = inverse_rms(x)
    k_width = wk.shape[1]

    def partial_tile(i):
        here = at_tile(i, WIDE)
        result = (
            times_turned(attended[...], wq[here, :])
            + times_turned(gate_grad[:, :k_width], wk[here, :])
            + times_turned(up_grad[:, :k_width], wv[here, :])
        )
        partial[:, here] = result.astype(LOW)
        gains_sent[0, 0:1, here] = jnp.sum(
            result * (tokens[:, here].astype(jnp.float32) * inverse), axis=0, keepdims=True
        )

    over_tiles(features // WIDE, partial_tile)
    outward_partial = remote(partial, partial_other, pair_send.at[3], pair_recv.at[3], pair)
    outward_partial.start()
    gains_sent[0, 1:2, :] = 0.5 * mlp_gain_grad[...]
    gain_dims = ("tensor", "core") + DIMS

    def send_gains(step):
        copy = remote(
            gains_sent.at[step], gains_landed.at[step], gains_send.at[step], gains_recv.at[step],
            partners[gain_dims[step]],
        )
        copy.start()
        return copy

    def next_gains(step, copy):
        copy.wait()
        total = gains_sent[step] + gains_landed[step]
        if step == len(gain_dims) - 1:
            gains[...] = total
            return None
        gains_sent[step + 1] = total
        return send_gains(step + 1)

    early.step(3)
    gains_copy = send_gains(0)
    late = Scatter(
        late_streams, [normed] * 3, [attended, gate_grad, up_grad], turned,
        Panels(half, [(wg, 0, hidden), (wg, half, hidden)]),
        Panels(half, [(wu, 0, hidden), (wu, half, hidden)]),
        [(early_landed[0], 0)] + [(ref, 0) for ref in late_landed],
        late_send, late_recv, bits, partners,
    )
    for s in range(5):
        late.open(s)
    early.step(4)
    gains_copy = next_gains(0, gains_copy)
    for step in range(6):
        if step == 1:
            early.step(5, early_out)
        late.step(step, late_out)
        gains_copy = next_gains(step + 1, gains_copy)
    outward.wait()
    outward_partial.wait()


def layer(
    tokens, cotangent, positions, segments, attention_gain, query_weight, key_weight, value_weight,
    query_gain, key_gain, out_weight, mlp_gain, gate_weight, up_weight, down_weight,
):
    rows, features = tokens.shape
    hd = query_gain.shape[1]
    heads = key_weight.shape[1] // hd
    half = features // 2
    q_width, k_width, hidden = query_weight.shape[1], key_weight.shape[1], gate_weight.shape[1]
    early_streams = split_streams((hidden, hidden, hidden, q_width), EARLY_TILES)
    late_streams = split_streams((q_width, k_width, k_width), LATE_TILES)
    early_width = 3 * hidden + q_width
    late_width = q_width + 2 * k_width
    pairs = jnp.arange(hd // 2, dtype=jnp.float32)
    inverse = 1.0 / ROPE_BASE ** (pairs * 2.0 / hd)
    frequencies = jnp.concatenate([inverse, inverse])[None]
    vmem = pl.BlockSpec(memory_space=pltpu.VMEM)
    far = pl.BlockSpec(memory_space=pl.ANY)
    f32 = jnp.float32
    outs = dict(
        middle=((rows, features), f32),
        mlp_out=((rows, features), LOW),
        mlp_other=((rows, features), LOW),
        grad_middle=((rows, features), f32),
        partial=((rows, features), LOW),
        partial_other=((rows, features), LOW),
        early=((CHUNK, early_width), f32),
        late=((CHUNK, late_width), f32),
        gains=((8, features), f32),
    )
    results = pl.pallas_call(
        functools.partial(layer_kernel, early_streams, late_streams),
        out_shape=[jax.ShapeDtypeStruct(shape, kind) for shape, kind in outs.values()],
        in_specs=[vmem] * 9 + [far] * 7,
        out_specs=[vmem] * len(outs),
        scratch_shapes=[
            pltpu.VMEM((rows, features), LOW),
            pltpu.VMEM((rows, q_width), f32),
            pltpu.VMEM((rows, k_width), f32),
            pltpu.VMEM((heads, 2 * rows, hd), LOW),
            pltpu.VMEM((8, 2, heads, rows, hd), LOW),
            pltpu.VMEM((8, 8, rows), jnp.int32),
            pltpu.VMEM((rows, hd), f32),
            pltpu.VMEM((rows, hd), f32),
            pltpu.VMEM((rows, q_width), LOW),
            pltpu.VMEM((rows, features), LOW),
            pltpu.VMEM((rows, hidden), LOW),
            pltpu.VMEM((rows, hidden), LOW),
            pltpu.VMEM((rows, hidden), LOW),
            pltpu.VMEM((rows, features), LOW),
            pltpu.VMEM((heads, 2 * rows, hd), LOW),
            pltpu.VMEM((heads, 8, 2 * rows), f32),
            pltpu.VMEM((1, features), f32),
            pltpu.VMEM(query_weight.shape, LOW),
            pltpu.VMEM(key_weight.shape, LOW),
            pltpu.VMEM(value_weight.shape, LOW),
            pltpu.VMEM(out_weight.shape, LOW),
            pltpu.VMEM(gate_weight.shape, LOW),
            pltpu.VMEM(up_weight.shape, LOW),
            pltpu.VMEM(down_weight.shape, LOW),
            pltpu.VMEM((rows, 2 * rows), f32),
            pltpu.VMEM((heads, 2 * rows, hd), f32),
            pltpu.VMEM((heads, 2 * rows, hd), f32),
            pltpu.VMEM((rows, hidden), f32),
            pltpu.VMEM((2, rows, features), LOW),
            pltpu.VMEM((2, rows, features), LOW),
            pltpu.VMEM((1, features, rows), LOW),
            pltpu.VMEM((half, early_width), LOW),
            pltpu.VMEM((3, rows, 2 * k_width), LOW),
            pltpu.VMEM((7, 8, features), f32),
            pltpu.VMEM((7, 8, features), f32),
            pltpu.SemaphoreType.DMA((7,)),
            pltpu.SemaphoreType.DMA((14,)),
            pltpu.SemaphoreType.DMA((7, 2)),
            pltpu.SemaphoreType.DMA((7,)),
            pltpu.SemaphoreType.DMA((7,)),
            pltpu.SemaphoreType.DMA((4,)),
            pltpu.SemaphoreType.DMA((4,)),
            pltpu.SemaphoreType.DMA((5, 6)),
            pltpu.SemaphoreType.DMA((5, 6)),
            pltpu.SemaphoreType.DMA((5, 6)),
            pltpu.SemaphoreType.DMA((5, 6)),
            pltpu.SemaphoreType.DMA((4,)),
            pltpu.SemaphoreType.DMA((4,)),
            pltpu.SemaphoreType.DMA((3,)),
            pltpu.SemaphoreType.DMA((3,)),
            pltpu.SemaphoreType.DMA((7,)),
            pltpu.SemaphoreType.DMA((7,)),
        ]
        + [pltpu.VMEM((half >> step, early_width), LOW) for step in range(6)]
        + [pltpu.VMEM((half >> step, late_width), LOW) for step in range(1, 6)],
        compiler_params=pltpu.CompilerParams(
            collective_id=0, has_side_effects=True, vmem_limit_bytes=63 * 1024 * 1024
        ),
    )(
        tokens, cotangent, positions, segments, frequencies, attention_gain, query_gain, key_gain,
        mlp_gain, query_weight, key_weight, value_weight, out_weight, gate_weight, up_weight,
        down_weight,
    )
    return dict(zip(outs, results))


def finish_kernel(
    tokens, attention_gain, middle, mlp_out, mlp_other, grad_middle, partial, partial_other, early,
    late, gains, output, input_grad, grad_query, grad_key, grad_value, grad_out, grad_gate,
    grad_up, grad_down, gains_out,
):
    hidden, q_width, k_width = grad_gate.shape[1], grad_query.shape[1], grad_key.shape[1]
    output[...] = (
        middle[...] + (mlp_out[...].astype(jnp.float32) + mlp_other[...].astype(jnp.float32))
    ).astype(LOW)
    x = tokens[...].astype(jnp.float32)
    inverse = inverse_rms(x)
    scaled = (
        partial[...].astype(jnp.float32) + partial_other[...].astype(jnp.float32)
    ) * attention_gain[...].astype(jnp.float32)
    input_grad[...] = (
        grad_middle[...]
        + inverse * scaled
        - x * (inverse * inverse * inverse) * jnp.mean(scaled * x, axis=-1, keepdims=True)
    ).astype(LOW)
    grad_gate[...] = early[:, :hidden]
    grad_up[...] = early[:, hidden : 2 * hidden]
    grad_down[...] = early[:, 2 * hidden : 3 * hidden].T
    grad_out[...] = early[:, 3 * hidden :].T
    grad_query[...] = late[:, :q_width]
    grad_key[...] = late[:, q_width : q_width + k_width]
    grad_value[...] = late[:, q_width + k_width :]
    chunk = lax.axis_index("dp") * 8 + lax.axis_index("seq")
    features = gains.shape[1]
    wide = pltpu.roll(gains[0:8, :], lax.rem(features - chunk * CHUNK, features), 1)
    thin = pltpu.roll(gains[0:8, :128], lax.rem(128 - chunk * 2, 128), 1)
    gains_out[0:2, :] = wide[0:2, :128]
    gains_out[2:4, :] = thin[2:4, :]


def finish(tokens, attention_gain, f, widths):
    q_width, k_width, hidden = widths
    rows, features = tokens.shape
    f32 = jnp.float32
    vmem = pl.BlockSpec(memory_space=pltpu.VMEM)
    shapes = (
        ((rows, features), LOW), ((rows, features), LOW), ((CHUNK, q_width), f32),
        ((CHUNK, k_width), f32), ((CHUNK, k_width), f32), ((q_width, CHUNK), f32),
        ((CHUNK, hidden), f32), ((CHUNK, hidden), f32), ((hidden, CHUNK), f32), ((8, 128), f32),
    )
    return pl.pallas_call(
        finish_kernel,
        out_shape=[jax.ShapeDtypeStruct(shape, kind) for shape, kind in shapes],
        in_specs=[vmem] * 11,
        out_specs=[vmem] * len(shapes),
        compiler_params=pltpu.CompilerParams(vmem_limit_bytes=60 * 1024 * 1024),
    )(
        tokens, attention_gain, f["middle"], f["mlp_out"], f["mlp_other"], f["grad_middle"],
        f["partial"], f["partial_other"], f["early"], f["late"], f["gains"],
    )


def shards(
    tokens,
    cotangent,
    positions,
    segments,
    attention_gain,
    query_weight,
    key_weight,
    value_weight,
    query_gain,
    key_gain,
    out_weight,
    mlp_gain,
    gate_weight,
    up_weight,
    down_weight,
):
    f = layer(
        tokens[0], cotangent[0], positions, segments, attention_gain[None], query_weight,
        key_weight, value_weight, query_gain[None], key_gain[None], out_weight, mlp_gain[None],
        gate_weight, up_weight, down_weight,
    )
    results = finish(
        tokens[0], attention_gain[None], f,
        (query_weight.shape[1], key_weight.shape[1], gate_weight.shape[1]),
    )
    gains = results[-1]
    return (
        results[0][None],
        results[1][None],
        *results[2:-1],
        gains[0, :CHUNK],
        gains[1, :CHUNK],
        gains[2, :2],
        gains[3, :2],
    )


def solution(mesh):
    return jax.shard_map(
        shards,
        mesh=mesh,
        in_specs=(
            P("dp", "seq", None),
            P("dp", "seq", None),
            P("dp", "seq"),
            P("dp", "seq"),
            P(),
            P(None, "tensor"),
            P(None, "tensor"),
            P(None, "tensor"),
            P(),
            P(),
            P("tensor", None),
            P(),
            P(None, "tensor"),
            P(None, "tensor"),
            P("tensor", None),
        ),
        out_specs=(
            P("dp", "seq", None),
            P("dp", "seq", None),
            P(("dp", "seq"), "tensor"),
            P(("dp", "seq"), "tensor"),
            P(("dp", "seq"), "tensor"),
            P("tensor", ("dp", "seq")),
            P(("dp", "seq"), "tensor"),
            P(("dp", "seq"), "tensor"),
            P("tensor", ("dp", "seq")),
            P(("dp", "seq")),
            P(("dp", "seq")),
            P(("dp", "seq")),
            P(("dp", "seq")),
        ),
        check_vma=False,
    )
```

time: 208 us -> 166 us (0.80)
  Pallas kernels: 192 us -> 155 us
  local copies, waits for them, and re-layouts: 13.5 us -> 8.97 us
    pallas_call x2 -> x1, Pallas kernels: 190 us -> 150 us  [layer(): pl.pallas_call(functools.partial(layer_kernel, early_streams, late_stream...]
    unnamed x24 -> x2, local copies, waits for them, and re-layouts: 9.91 us -> 3.85 us
    pallas_call x1, Pallas kernels: 2.06 us -> 4.72 us  [finish(): pl.pallas_call(finish_kernel, out_shape=[jax.ShapeDtypeStruct(shape, kind...]
where the time goes in v4:
time: 166 us; the launch traced here: 165 us
  Pallas kernels  155 us (93%)
  local copies, waits for them, and re-layouts  8.97 us (5%)
    pallas_call x1, Pallas kernels, layer(): pl.pallas_call(functools.partial(layer_kernel, early_streams, late_stream...  150 us
    pallas_call x1, Pallas kernels, finish(): pl.pallas_call(finish_kernel, out_shape=[jax.ShapeDtypeStruct(shape, kind...  4.72 us
    unnamed x2, local copies, waits for them, and re-layouts  3.85 us

profile of v4, /device:TPU:0, one launch (start us, length us, event | category | flops | bytes accessed | tf_op | source)
XLA Modules:
  0.0 165.3 jit_solution(13055204616834867823)
XLA Ops:
  0.7 0.6 maximum_bitcast_fusion.refs_4_
  1.2 1.3 broadcast_in_dim.22.refs_5_.attention_gain
  2.5 1.3 broadcast_in_dim.26.refs_8_
  3.8 150.3 %shard_map.246 = (f32[256,1024]{1,0:T(8,128)}, bf16[256,1024]{1,0:T(8,128)(2,1)}, bf16[256,1024]{1,0:T(8,128)(2,1)}, f32[256,1024]{1,0:T(8,128)}, bf16[256,1024]...) custom-call(bf16[256,1024]{1,0:T(8,128)(2,1)} %bitcast.16, ...), custom_call_target="tpu_custom_call" | custom-call | tf_op jit(solution)/shard_map/pallas_call | solution.py:708
  154.1 4.7 %shard_map.247 = (bf16[256,1024]{1,0:T(8,128)(2,1)}, bf16[256,1024]{1,0:T(8,128)(2,1)}, f32[16,1024]{1,0:T(8,128)}, f32[16,512]{1,0:T(8,128)}, f32[16,512]{1,0:T...) custom-call(bf16[256,1024]{1,0:T(8,128)(2,1)} %bitcast.17, ...), custom_call_target="tpu_custom_call" | custom-call | tf_op jit(solution)/shard_map/pallas_call | solution.py:824
  158.8 1.3 slice_bitcast_fusion.2
  160.1 1.3 slice_bitcast_fusion
  161.4 1.8 %copy.28 = f32[1024,16]{0,1:T(8,128)} copy(f32[1024,16]{1,0:T(8,128)} %get-tuple-element.56) | data formatting | bytes 131072
  163.2 2.0 %copy.29 = f32[1536,16]{0,1:T(8,128)} copy(f32[1536,16]{1,0:T(8,128)} %get-tuple-element.59) | data formatting | bytes 196608
  (1 shorter events, 0.0 us)

commit v5 on v4

--- a/solution.py
+++ b/solution.py
@@ -35,6 +35,14 @@
         "y1": (y // 2 + y % 2) % 2,
         "z": z,
     }
+    def flip(dims):
+        far_x = x_near if "x1" in dims else x
+        far_x = 3 - far_x if "x3" in dims else far_x
+        far_y = y_near if "y1" in dims else y
+        far_y = 3 - far_y if "y3" in dims else far_y
+        far_z = 1 - z if "z" in dims else z
+        return (far_x * 2 + far_z, far_y * 2 + core, tensor)
+
     partners = {
         "core": (dp, seq + 1 - 2 * core, tensor),
         "x3": ((3 - x) * 2 + z, seq, tensor),
@@ -44,7 +52,7 @@
         "z": (dp + 1 - 2 * z, seq, tensor),
         "tensor": (dp, seq, 1 - tensor),
     }
-    return bits, partners
+    return bits, partners, flip
 
 
 def greet(partners):
@@ -54,13 +62,23 @@
     pl.semaphore_wait(barrier, len(partners))
 
 
-ORDERS = (
-    ("core", "x3", "x1", "z", "y3", "y1"),
-    ("core", "x1", "x3", "z", "y1", "y3"),
-    ("core", "y3", "z", "x1", "x3", "y1"),
-    ("core", "y1", "z", "x3", "x1", "y3"),
-    ("core", "z", "x1", "x3", "y3", "y1"),
+EARLY_ORDERS = (
+    ("core", "x3", "x1", "y3", "z", "y1"),
+    ("core", "x1", "x3", "y1", "z", "y3"),
+    ("core", "y3", "x3", "x1", "z", "y1"),
+    ("core", "y1", "x1", "x3", "z", "y3"),
+    ("core", "z", "y3", "x1", "x3", "y1"),
 )
+LATE_ORDERS = (
+    ("core", "x3", "x1", "y3", "y1", "z"),
+    ("core", "x1", "x3", "y1", "y3", "z"),
+    ("core", "y3", "y1", "x3", "x1", "z"),
+    ("core", "y1", "y3", "x1", "x3", "z"),
+)
+
+
+def masks(dims):
+    return [tuple(d for i, d in enumerate(dims) if m >> (len(dims) - 1 - i) & 1) for m in range(1, 8)]
 
 
 def slot_chunks(order):
@@ -111,7 +129,7 @@
 
 
 EARLY_TILES = (6, 6, 4, 2, 4)
-LATE_TILES = (2, 2, 2, 1, 1)
+LATE_TILES = (2, 2, 2, 2)
 SHIFTS = (2, 1, 3, 0)
 WIDE = 256
 
@@ -135,6 +153,23 @@
     return streams
 
 
+class Fetch:
+    def __init__(self, far, near, sem, index):
+        rows = far.shape[0] // 4
+        self.copies = [
+            pltpu.make_async_copy(
+                far.at[pl.ds(i * rows, rows), :], near.at[pl.ds(i * rows, rows), :], sem.at[index, i]
+            )
+            for i in range(4)
+        ]
+        for copy in self.copies:
+            copy.start()
+
+    def wait(self):
+        for copy in self.copies:
+            copy.wait()
+
+
 class Panels:
     def __init__(self, rows, panels):
         self.rows = rows
@@ -150,11 +185,12 @@
 
 
 class Scatter:
-    def __init__(self, streams, lhs, rhs, turned, sent, held, landed, send_sem, recv_sem, bits, partners):
+    def __init__(self, orders, streams, lhs, rhs, flipped, turned, sent, held, landed, send_sem, recv_sem, bits, partners, flip):
         self.streams, self.lhs, self.rhs = streams, lhs, rhs
+        self.orders, self.flipped, self.last = orders, flipped, None
         self.turned, self.sent, self.held = turned, sent, held
         self.landed, self.send_sem, self.recv_sem = landed, send_sem, recv_sem
-        self.bits, self.partners = bits, partners
+        self.bits, self.partners, self.flip = bits, partners, flip
         self.half = sent.rows
         self.copies = {}
         self.base = [0] * len(streams)
@@ -162,15 +198,17 @@
     def open(self, s):
         first, columns, pieces = self.streams[s]
         core = self.bits["core"]
-        chunks = slot_chunks(ORDERS[s])
+        chunks = slot_chunks(self.orders[s])
         for kept in (False, True):
             ref, row, column = (self.held if kept else self.sent).find(first)
             offset = core * self.half if kept else (1 - core) * self.half
             for index, (matrix, left_column, begin, width) in enumerate(pieces):
                 if not kept:
-                    flipped = self.lhs[matrix][...].T
+                    if self.last is not self.lhs[matrix]:
+                        self.last = self.lhs[matrix]
+                        self.flipped[...] = self.last[...].T
                     for slot, chunk in enumerate(chunks):
-                        self.turned[index, slot * CHUNK : (slot + 1) * CHUNK, :] = flipped[
+                        self.turned[index, slot * CHUNK : (slot + 1) * CHUNK, :] = self.flipped[
                             chunk * CHUNK : (chunk + 1) * CHUNK, :
                         ]
                 target = column + begin - first
@@ -197,12 +235,12 @@
             ref.at[:, pl.ds(column + first, columns)],
             self.send_sem.at[s, step],
             self.recv_sem.at[s, step],
-            self.partners[ORDERS[s][step]],
+            self.partners[self.orders[s][step]],
         )
         copy.start()
         self.copies[s, step] = copy
 
-    def step(self, step, out=None, streams=range(5)):
+    def step(self, step, streams=range(4)):
         rows = self.half >> step
         for s in streams:
             first, columns, _ = self.streams[s]
@@ -211,11 +249,6 @@
             mine = pl.ds(column, columns)
             landed, from_column = self.landed[step]
             theirs = pl.ds(from_column + first, columns)
-            if step == 5:
-                out[:, pl.ds(first, columns)] = ref[
-                    pl.ds(pl.multiple_of(row + self.base[s], CHUNK), CHUNK), mine
-                ].astype(jnp.float32) + landed[:, theirs].astype(jnp.float32)
-                continue
             tile = min(rows, 64)
 
             def add(i, s=s, tile=tile, ref=ref, row=row, mine=mine, landed=landed, theirs=theirs):
@@ -224,26 +257,68 @@
                 ref[here, mine] = ref[here, mine] + landed[pl.ds(start, tile), theirs]
 
             over_tiles(rows // tile, add)
-            bit = self.bits[ORDERS[s][step + 1]]
+            if step == 2:
+                self.spread(s)
+                continue
+            bit = self.bits[self.orders[s][step + 1]]
             away = pl.multiple_of(row + self.base[s] + (1 - bit) * (rows // 2), CHUNK)
             self.send(step + 1, s, ref.at[pl.ds(away, rows // 2), mine])
             self.base[s] = self.base[s] + bit * (rows // 2)
 
+    def landing(self, s, mask):
+        step, place_in = ((3, mask - 1), (4, mask - 5), (5, 0))[(mask > 4) + (mask > 6)]
+        ref, column = self.landed[step]
+        first, columns, _ = self.streams[s]
+        return ref.at[pl.ds(place_in * CHUNK, CHUNK), pl.ds(column + first, columns)]
+
+    def spread(self, s):
+        first, columns, _ = self.streams[s]
+        ref, row, column = self.held.find(first)
+        dims = self.orders[s][3:]
+        for mask, flipped in enumerate(masks(dims), 1):
+            slot = 0
+            for d in dims:
+                slot = slot * 2 + (1 - self.bits[d] if d in flipped else self.bits[d])
+            there = pl.multiple_of(row + self.base[s] + slot * CHUNK, CHUNK)
+            copy = remote(
+                ref.at[pl.ds(there, CHUNK), pl.ds(column, columns)],
+                self.landing(s, mask),
+                self.send_sem.at[s, 2 + mask],
+                self.recv_sem.at[s, 2 + mask],
+                self.flip(flipped),
+            )
+            copy.start()
+            self.copies[s, 2 + mask] = copy
+
+    def finish(self, out, streams=range(4)):
+        for s in streams:
+            first, columns, _ = self.streams[s]
+            ref, row, column = self.held.find(first)
+            slot = 0
+            for d in self.orders[s][3:]:
+                slot = slot * 2 + self.bits[d]
+            mine = pl.multiple_of(row + self.base[s] + slot * CHUNK, CHUNK)
+            total = ref[pl.ds(mine, CHUNK), pl.ds(column, columns)].astype(jnp.float32)
+            for mask in range(1, 8):
+                self.copies[s, 2 + mask].wait()
+                total = total + self.landing(s, mask)[...].astype(jnp.float32)
+            out[:, pl.ds(first, columns)] = total
+
 
 def layer_kernel(early_streams, late_streams, *refs):
     (
         tokens, cotangent, positions, segments, frequencies, attention_gain, query_gain,
-        key_gain, mlp_gain, wq_far, wk_far, wv_far, wo_far, wg_far, wu_far, wd_far, middle,
-        mlp_out, mlp_other, grad_middle, partial, partial_other, early_out, late_out, gains,
-        normed, query_raw, key_raw, query, kv, meta, cosine, sine, attended, normed_mlp,
+        key_gain, mlp_gain, wq_far, wk_far, wv_far, wo_far, wg_far, wu_far, wd_far, output,
+        input_grad, early_out, late_out, gains, middle, grad_middle, partial_other, normed, query_raw, key_raw, query, kv, meta, cosine, sine, attended, normed_mlp,
         activated, gate_grad, up_grad, middle_low, attended_grad, inner, mlp_gain_grad, wq, wk,
-        wv, wo, wg, wu, wd, bias, total, weight_sum, act_grad, part_out, part_in, turned, held,
+        wv, wo, wg, wu, wd, bias, total, weight_sum, act_grad, part_out, part_in, flipped, turned, held,
         far_grad, gains_sent, gains_landed, weight_sem, kv_send, kv_recv, meta_send, meta_recv,
         pair_send, pair_recv, early_send, early_recv, late_send, late_recv, core_send,
         core_recv, far_send, far_recv, gains_send, gains_recv,
     ) = refs[: -11]
     early_landed, late_landed = refs[-11:-5], refs[-5:]
-    bits, partners = place()
+    mlp_out, mlp_other, partial = part_out.at[0], part_in.at[0], part_out.at[1]
+    bits, partners, flip = place()
     dp, seq, tensor = lax.axis_index("dp"), lax.axis_index("seq"), lax.axis_index("tensor")
     core, y = seq % 2, seq // 2
     after, before, across = (y + 1) % 4, (y + 3) % 4, (y + 2) % 4
@@ -255,19 +330,13 @@
     rows = tokens.shape[0]
     heads = kv.shape[2]
     hd = kv.shape[4]
-    greet(others + [partners[name] for name in ("x3", "x1", "z", "tensor")])
-    fetches = [
-        pltpu.make_async_copy(far, held, weight_sem.at[i])
-        for i, (far, held) in enumerate(
-            zip(
-                (wk_far, wv_far, wq_far, wo_far, wd_far, wg_far, wu_far),
-                (wk, wv, wq, wo, wd, wg, wu),
-            )
-        )
-    ]
-    for fetch in fetches:
-        fetch.start()
-    got_wk, got_wv, got_wq, got_wo, got_wd, got_wg, got_wu = fetches
+    groups = {frozenset(m) for order in EARLY_ORDERS + LATE_ORDERS for m in masks(order[3:])}
+    groups |= {frozenset((name,)) for name in ("x3", "x1", "z")}
+    groups = sorted(sorted(group) for group in groups if group & {"x3", "x1", "z"})
+    greet(others + [partners["tensor"]] + [flip(group) for group in groups])
+    got_wk = Fetch(wk_far, wk, weight_sem, 0)
+    got_wv = Fetch(wv_far, wv, weight_sem, 1)
+    got_wq = Fetch(wq_far, wq, weight_sem, 2)
 
     meta[seq] = jnp.zeros_like(meta[seq])
     meta[seq, 0:1, :] = positions[...]
@@ -290,7 +359,7 @@
         return entries * cosine[...] + pltpu.roll(entries, hd // 2, 1) * sine[...]
 
     x = tokens[...].astype(jnp.float32)
-    normed[...] = (x * inverse_rms(x) * attention_gain[...].astype(jnp.float32)).astype(LOW)
+    normed[...] = (x * inverse_rms(x) * attention_gain[...].astype(jnp.float32)[None, :]).astype(LOW)
 
     tile = 2 * hd
     got_wk.wait()
@@ -300,7 +369,7 @@
         key_raw[:, at_tile(i, tile)] = raw
         for g in range(2):
             head = raw[:, g * hd : (g + 1) * hd]
-            scaled = head * inverse_rms(head) * key_gain[...].astype(jnp.float32)
+            scaled = head * inverse_rms(head) * key_gain[...].astype(jnp.float32)[None, :]
             kv[seq, 0, 2 * i + g] = turn(scaled).astype(LOW)
 
     over_tiles(heads // 2, key_tile)
@@ -323,6 +392,10 @@
     over_tiles(heads // 2, value_tile)
     sends += [own(1, 1, ahead, 3), own(1, 2, behind, 4), own(1, 0, near, 5)]
     got_wq.wait()
+    got_wo = Fetch(wo_far, wo, weight_sem, 3)
+    got_wd = Fetch(wd_far, wd, weight_sem, 4)
+    got_wg = Fetch(wg_far, wg, weight_sem, 5)
+    got_wu = Fetch(wu_far, wu, weight_sem, 6)
     scale = math.log2(math.e) / math.sqrt(hd)
 
     def query_tile(i):
@@ -330,7 +403,7 @@
         query_raw[:, at_tile(i, tile)] = raw
         for g in range(2):
             head = raw[:, g * hd : (g + 1) * hd]
-            scaled = head * inverse_rms(head) * (query_gain[...].astype(jnp.float32) * scale)
+            scaled = head * inverse_rms(head) * (query_gain[...].astype(jnp.float32)[None, :] * scale)
             query[i, g * rows : (g + 1) * rows, :] = turn(scaled).astype(LOW)
 
     over_tiles(heads, query_tile)
@@ -417,9 +490,33 @@
     def out_tile(i):
         part_out[0, :, at_tile(i, wide)] = times(attended[...], wo[:, at_tile(i, wide)]).astype(LOW)
 
-    over_tiles(features // wide, out_tile)
-    first = remote(part_out.at[0], part_in.at[0], pair_send.at[0], pair_recv.at[0], pair)
-    first.start()
+    def in_halves(body, target, source, index):
+        copies = []
+        for part in range(2):
+            count = features // wide // 2
+
+            def tile_of_part(i, part=part):
+                body(i + part * count)
+
+            over_tiles(count, tile_of_part)
+            here = pl.ds(part * features // 2, features // 2)
+            copies.append(
+                remote(
+                    source.at[:, here],
+                    target.at[:, here],
+                    pair_send.at[index, part],
+                    pair_recv.at[index, part],
+                    pair,
+                )
+            )
+            copies[-1].start()
+        return copies
+
+    def wait_all(copies):
+        for copy in copies:
+            copy.wait()
+
+    first = in_halves(out_tile, part_in.at[0], part_out.at[0], 0)
     got_wd.wait()
 
     def act_grad_tile(i):
@@ -428,13 +525,13 @@
     over_tiles(hidden // wide, act_grad_tile)
     got_wg.wait()
     got_wu.wait()
-    first.wait()
+    wait_all(first)
     mid = (
         tokens[...].astype(jnp.float32)
         + (part_out[0].astype(jnp.float32) + part_in[0].astype(jnp.float32))
     )
     middle[...] = mid
-    normed_mlp[...] = (mid * inverse_rms(mid) * mlp_gain[...].astype(jnp.float32)).astype(LOW)
+    normed_mlp[...] = (mid * inverse_rms(mid) * mlp_gain[...].astype(jnp.float32)[None, :]).astype(LOW)
 
     def hidden_tile(i):
         here = at_tile(i, wide)
@@ -457,9 +554,7 @@
             times_turned(gate_grad[...], wg[here, :]) + times_turned(up_grad[...], wu[here, :])
         ).astype(LOW)
 
-    over_tiles(features // wide, back_tile)
-    second = remote(part_out.at[1], part_in.at[1], pair_send.at[1], pair_recv.at[1], pair)
-    second.start()
+    second = in_halves(back_tile, part_in.at[1], part_out.at[1], 1)
 
     def down_tile(i):
         mlp_out[:, at_tile(i, wide)] = times(activated[...], wd[:, at_tile(i, wide)]).astype(LOW)
@@ -467,25 +562,23 @@
     over_tiles(features // wide, down_tile)
     half = features // 2
     early = Scatter(
-        early_streams, [normed_mlp, normed_mlp, cotangent, middle_low],
-        [gate_grad, up_grad, activated, attended], turned,
+        EARLY_ORDERS, early_streams, [normed_mlp, normed_mlp, cotangent, middle_low],
+        [gate_grad, up_grad, activated, attended], flipped, turned,
         Panels(half, [(wg, 0, hidden), (wg, half, hidden), (wu, 0, hidden), (wu, half, hidden)]),
         Panels(half, [(held, 0, held.shape[1])]), [(ref, 0) for ref in early_landed],
-        early_send, early_recv, bits, partners,
+        early_send, early_recv, bits, partners, flip,
     )
     for s in range(4):
         early.open(s)
     early.step(0, streams=range(4))
     for copy in sends:
         copy.wait_send()
-    second.wait()
-    outward = remote(mlp_out, mlp_other, pair_send.at[2], pair_recv.at[2], pair)
-    outward.start()
+    wait_all(second)
     mid = middle[...]
     inverse = inverse_rms(mid)
     dy = part_out[1].astype(jnp.float32) + part_in[1].astype(jnp.float32)
     mlp_gain_grad[...] = jnp.sum(dy * mid * inverse, axis=0, keepdims=True)
-    scaled = dy * mlp_gain[...].astype(jnp.float32)
+    scaled = dy * mlp_gain[...].astype(jnp.float32)[None, :]
     grad = (
         cotangent[...].astype(jnp.float32)
         + inverse * scaled
@@ -516,12 +609,8 @@
         return pl.ds(pl.multiple_of(j % 2 * hd, hd), hd), at_tile(j // 2, 2 * rows)
 
     def block(slot, target, first):
-        def column(row):
-            return jnp.broadcast_to(row.astype(jnp.float32), (rows, rows)).T
-
-        allowed = (column(meta[slot, 0:1, :]) <= place_row) & (
-            column(meta[slot, 1:2, :]) == segment_row
-        )
+        columns = meta[slot].astype(jnp.float32).T
+        allowed = (columns[:, 0:1] <= place_row) & (columns[:, 1:2] == segment_row)
         one = jnp.where(allowed, 0.0, NEGATIVE)
         bias[:, :rows] = one
         bias[:, rows:] = one
@@ -571,7 +660,11 @@
             far_sends.append(copy)
         if i == 0:
             early.step(0, streams=range(4, 5))
-    early.step(1)
+        if i == 2:
+            early.step(1)
+
+    outward = remote(mlp_out, mlp_other, pair_send.at[2, 0], pair_recv.at[2, 0], pair)
+    outward.start()
 
     def back(raw, gain, gradient):
         turned_back = gradient * cosine[...] - pltpu.roll(gradient, hd // 2, 1) * sine[...]
@@ -583,8 +676,8 @@
         return raw_grad, jnp.sum(turned_back * raw * inverse, axis=0, keepdims=True)
 
     gains_sent[0] = jnp.zeros_like(gains_sent[0])
-    query_gain_row = query_gain[...].astype(jnp.float32)
-    key_gain_row = key_gain[...].astype(jnp.float32)
+    query_gain_row = query_gain[...].astype(jnp.float32)[None, :]
+    key_gain_row = key_gain[...].astype(jnp.float32)[None, :]
 
     def query_head(j):
         gradient = act_grad[query_turned(j)].T * (1.0 / math.sqrt(hd))
@@ -597,7 +690,7 @@
             gains_sent[0, 2:3, :hd] += part
 
     over_tiles(heads, query_head)
-    early.step(2)
+    early.step(1, streams=range(4, 5))
     for copy in far_sends:
         copy.wait()
 
@@ -614,6 +707,15 @@
         gains_sent[0, 3:4, :hd] += part
 
     over_tiles(heads, key_head)
+    late = Scatter(
+        LATE_ORDERS, late_streams, [normed] * 3, [attended, gate_grad, up_grad], flipped, turned,
+        Panels(half, [(wg, 0, hidden), (wg, half, hidden)]),
+        Panels(half, [(wu, 0, hidden), (wu, half, hidden)]),
+        [(early_landed[0], 0)] + [(ref, 0) for ref in late_landed],
+        late_send, late_recv, bits, partners, flip,
+    )
+    for s in range(4):
+        late.open(s)
     x = tokens[...].astype(jnp.float32)
     inverse = inverse_rms(x)
     k_width = wk.shape[1]
@@ -630,49 +732,62 @@
             result * (tokens[:, here].astype(jnp.float32) * inverse), axis=0, keepdims=True
         )
 
-    over_tiles(features // WIDE, partial_tile)
-    outward_partial = remote(partial, partial_other, pair_send.at[3], pair_recv.at[3], pair)
-    outward_partial.start()
+    outward_partial = in_halves(partial_tile, partial_other, partial, 3)
     gains_sent[0, 1:2, :] = 0.5 * mlp_gain_grad[...]
-    gain_dims = ("tensor", "core") + DIMS
+    gain_steps = (
+        [(partners["tensor"])],
+        [(partners["core"])],
+        [flip(m) for m in (("x3",), ("x1",), ("x3", "x1"))],
+        [flip(m) for m in masks(("y3", "y1", "z"))],
+    )
 
     def send_gains(step):
-        copy = remote(
-            gains_sent.at[step], gains_landed.at[step], gains_send.at[step], gains_recv.at[step],
-            partners[gain_dims[step]],
-        )
-        copy.start()
-        return copy
-
-    def next_gains(step, copy):
-        copy.wait()
-        total = gains_sent[step] + gains_landed[step]
-        if step == len(gain_dims) - 1:
-            gains[...] = total
+        first = (0, 1, 2, 5)[step]
+        copies = [
+            remote(
+                gains_sent.at[step], gains_landed.at[first + i], gains_send.at[first + i],
+                gains_recv.at[first + i], partner,
+            )
+            for i, partner in enumerate(gain_steps[step])
+        ]
+        for copy in copies:
+            copy.start()
+        return copies
+
+    def next_gains(step, copies):
+        first = (0, 1, 2, 5)[step]
+        sum_so_far = gains_sent[step]
+        for i, copy in enumerate(copies):
+            copy.wait()
+            sum_so_far = sum_so_far + gains_landed[first + i]
+        if step == 3:
+            gains[...] = sum_so_far
             return None
-        gains_sent[step + 1] = total
+        gains_sent[step + 1] = sum_so_far
         return send_gains(step + 1)
 
-    early.step(3)
     gains_copy = send_gains(0)
-    late = Scatter(
-        late_streams, [normed] * 3, [attended, gate_grad, up_grad], turned,
-        Panels(half, [(wg, 0, hidden), (wg, half, hidden)]),
-        Panels(half, [(wu, 0, hidden), (wu, half, hidden)]),
-        [(early_landed[0], 0)] + [(ref, 0) for ref in late_landed],
-        late_send, late_recv, bits, partners,
-    )
-    for s in range(5):
-        late.open(s)
-    early.step(4)
-    gains_copy = next_gains(0, gains_copy)
-    for step in range(6):
+    early.step(2, streams=range(5))
+    for step in range(3):
+        late.step(step)
+        gains_copy = next_gains(step, gains_copy)
         if step == 1:
-            early.step(5, early_out)
-        late.step(step, late_out)
-        gains_copy = next_gains(step + 1, gains_copy)
-    outward.wait()
-    outward_partial.wait()
+            early.finish(early_out)
+            outward.wait()
+            both = mlp_out[...].astype(jnp.float32) + mlp_other[...].astype(jnp.float32)
+            output[...] = (middle[...] + both).astype(LOW)
+        if step == 2:
+            early.finish(early_out, streams=range(4, 5))
+            wait_all(outward_partial)
+            scaled = (
+                partial[...].astype(jnp.float32) + partial_other[...].astype(jnp.float32)
+            ) * attention_gain[...].astype(jnp.float32)[None, :]
+            across_mean = jnp.mean(scaled * x, axis=-1, keepdims=True)
+            input_grad[...] = (
+                grad_middle[...] + inverse * scaled - x * (inverse * inverse * inverse) * across_mean
+            ).astype(LOW)
+    late.finish(late_out)
+    next_gains(3, gains_copy)
 
 
 def layer(
@@ -680,7 +795,7 @@
     query_gain, key_gain, out_weight, mlp_gain, gate_weight, up_weight, down_weight,
 ):
     rows, features = tokens.shape
-    hd = query_gain.shape[1]
+    hd = query_gain.shape[0]
     heads = key_weight.shape[1] // hd
     half = features // 2
     q_width, k_width, hidden = query_weight.shape[1], key_weight.shape[1], gate_weight.shape[1]
@@ -695,12 +810,8 @@
     far = pl.BlockSpec(memory_space=pl.ANY)
     f32 = jnp.float32
     outs = dict(
-        middle=((rows, features), f32),
-        mlp_out=((rows, features), LOW),
-        mlp_other=((rows, features), LOW),
-        grad_middle=((rows, features), f32),
-        partial=((rows, features), LOW),
-        partial_other=((rows, features), LOW),
+        output=((rows, features), LOW),
+        input_grad=((rows, features), LOW),
         early=((CHUNK, early_width), f32),
         late=((CHUNK, late_width), f32),
         gains=((8, features), f32),
@@ -711,6 +822,9 @@
         in_specs=[vmem] * 9 + [far] * 7,
         out_specs=[vmem] * len(outs),
         scratch_shapes=[
+            pltpu.VMEM((rows, features), f32),
+            pltpu.VMEM((rows, features), f32),
+            pltpu.VMEM((rows, features), LOW),
             pltpu.VMEM((rows, features), LOW),
             pltpu.VMEM((rows, q_width), f32),
             pltpu.VMEM((rows, k_width), f32),
@@ -741,28 +855,29 @@
             pltpu.VMEM((rows, hidden), f32),
             pltpu.VMEM((2, rows, features), LOW),
             pltpu.VMEM((2, rows, features), LOW),
+            pltpu.VMEM((features, rows), LOW),
             pltpu.VMEM((1, features, rows), LOW),
             pltpu.VMEM((half, early_width), LOW),
             pltpu.VMEM((3, rows, 2 * k_width), LOW),
-            pltpu.VMEM((7, 8, features), f32),
-            pltpu.VMEM((7, 8, features), f32),
-            pltpu.SemaphoreType.DMA((7,)),
+            pltpu.VMEM((4, 8, features), f32),
+            pltpu.VMEM((12, 8, features), f32),
+            pltpu.SemaphoreType.DMA((7, 4)),
             pltpu.SemaphoreType.DMA((14,)),
             pltpu.SemaphoreType.DMA((7, 2)),
             pltpu.SemaphoreType.DMA((7,)),
             pltpu.SemaphoreType.DMA((7,)),
-            pltpu.SemaphoreType.DMA((4,)),
-            pltpu.SemaphoreType.DMA((4,)),
-            pltpu.SemaphoreType.DMA((5, 6)),
-            pltpu.SemaphoreType.DMA((5, 6)),
-            pltpu.SemaphoreType.DMA((5, 6)),
-            pltpu.SemaphoreType.DMA((5, 6)),
+            pltpu.SemaphoreType.DMA((4, 2)),
+            pltpu.SemaphoreType.DMA((4, 2)),
+            pltpu.SemaphoreType.DMA((5, 10)),
+            pltpu.SemaphoreType.DMA((5, 10)),
+            pltpu.SemaphoreType.DMA((5, 10)),
+            pltpu.SemaphoreType.DMA((5, 10)),
             pltpu.SemaphoreType.DMA((4,)),
             pltpu.SemaphoreType.DMA((4,)),
             pltpu.SemaphoreType.DMA((3,)),
             pltpu.SemaphoreType.DMA((3,)),
-            pltpu.SemaphoreType.DMA((7,)),
-            pltpu.SemaphoreType.DMA((7,)),
+            pltpu.SemaphoreType.DMA((12,)),
+            pltpu.SemaphoreType.DMA((12,)),
         ]
         + [pltpu.VMEM((half >> step, early_width), LOW) for step in range(6)]
         + [pltpu.VMEM((half >> step, late_width), LOW) for step in range(1, 6)],
@@ -778,28 +893,17 @@
 
 
 def finish_kernel(
-    tokens, attention_gain, middle, mlp_out, mlp_other, grad_middle, partial, partial_other, early,
-    late, gains, output, input_grad, grad_query, grad_key, grad_value, grad_out, grad_gate,
-    grad_up, grad_down, gains_out,
+    output_in, input_grad_in, early, late, gains, output, input_grad, grad_query, grad_key,
+    grad_value, grad_out, grad_gate, grad_up, grad_down, attention_gain, mlp_gain, query_gain,
+    key_gain,
 ):
     hidden, q_width, k_width = grad_gate.shape[1], grad_query.shape[1], grad_key.shape[1]
-    output[...] = (
-        middle[...] + (mlp_out[...].astype(jnp.float32) + mlp_other[...].astype(jnp.float32))
-    ).astype(LOW)
-    x = tokens[...].astype(jnp.float32)
-    inverse = inverse_rms(x)
-    scaled = (
-        partial[...].astype(jnp.float32) + partial_other[...].astype(jnp.float32)
-    ) * attention_gain[...].astype(jnp.float32)
-    input_grad[...] = (
-        grad_middle[...]
-        + inverse * scaled
-        - x * (inverse * inverse * inverse) * jnp.mean(scaled * x, axis=-1, keepdims=True)
-    ).astype(LOW)
+    output[...] = output_in[...]
+    input_grad[...] = input_grad_in[...]
     grad_gate[...] = early[:, :hidden]
     grad_up[...] = early[:, hidden : 2 * hidden]
-    grad_down[...] = early[:, 2 * hidden : 3 * hidden].T
-    grad_out[...] = early[:, 3 * hidden :].T
+    grad_down[...] = early[:, 2 * hidden : 3 * hidden]
+    grad_out[...] = early[:, 3 * hidden :]
     grad_query[...] = late[:, :q_width]
     grad_key[...] = late[:, q_width : q_width + k_width]
     grad_value[...] = late[:, q_width + k_width :]
@@ -807,30 +911,30 @@
     features = gains.shape[1]
     wide = pltpu.roll(gains[0:8, :], lax.rem(features - chunk * CHUNK, features), 1)
     thin = pltpu.roll(gains[0:8, :128], lax.rem(128 - chunk * 2, 128), 1)
-    gains_out[0:2, :] = wide[0:2, :128]
-    gains_out[2:4, :] = thin[2:4, :]
-
-
-def finish(tokens, attention_gain, f, widths):
+    attention_gain[...] = wide[0:1, : attention_gain.shape[1]]
+    mlp_gain[...] = wide[1:2, : mlp_gain.shape[1]]
+    query_gain[...] = thin[2:3, : query_gain.shape[1]]
+    key_gain[...] = thin[3:4, : key_gain.shape[1]]
+
+
+def finish(f, widths):
     q_width, k_width, hidden = widths
-    rows, features = tokens.shape
+    rows, features = f["output"].shape
     f32 = jnp.float32
     vmem = pl.BlockSpec(memory_space=pltpu.VMEM)
     shapes = (
         ((rows, features), LOW), ((rows, features), LOW), ((CHUNK, q_width), f32),
-        ((CHUNK, k_width), f32), ((CHUNK, k_width), f32), ((q_width, CHUNK), f32),
-        ((CHUNK, hidden), f32), ((CHUNK, hidden), f32), ((hidden, CHUNK), f32), ((8, 128), f32),
+        ((CHUNK, k_width), f32), ((CHUNK, k_width), f32), ((CHUNK, q_width), f32),
+        ((CHUNK, hidden), f32), ((CHUNK, hidden), f32), ((CHUNK, hidden), f32),
+        ((1, CHUNK), f32), ((1, CHUNK), f32), ((1, 2), f32), ((1, 2), f32),
     )
     return pl.pallas_call(
         finish_kernel,
         out_shape=[jax.ShapeDtypeStruct(shape, kind) for shape, kind in shapes],
-        in_specs=[vmem] * 11,
+        in_specs=[vmem] * 5,
         out_specs=[vmem] * len(shapes),
         compiler_params=pltpu.CompilerParams(vmem_limit_bytes=60 * 1024 * 1024),
-    )(
-        tokens, attention_gain, f["middle"], f["mlp_out"], f["mlp_other"], f["grad_middle"],
-        f["partial"], f["partial_other"], f["early"], f["late"], f["gains"],
-    )
+    )(f["output"], f["input_grad"], f["early"], f["late"], f["gains"])
 
 
 def shards(
@@ -851,23 +955,25 @@
     down_weight,
 ):
     f = layer(
-        tokens[0], cotangent[0], positions, segments, attention_gain[None], query_weight,
-        key_weight, value_weight, query_gain[None], key_gain[None], out_weight, mlp_gain[None],
+        tokens[0], cotangent[0], positions, segments, attention_gain, query_weight,
+        key_weight, value_weight, query_gain, key_gain, out_weight, mlp_gain,
         gate_weight, up_weight, down_weight,
     )
     results = finish(
-        tokens[0], attention_gain[None], f,
-        (query_weight.shape[1], key_weight.shape[1], gate_weight.shape[1]),
-    )
-    gains = results[-1]
+        f, (query_weight.shape[1], key_weight.shape[1], gate_weight.shape[1])
+    )
+    output, input_grad, query, key, value, out, gate, up, down, *gains = results
     return (
-        results[0][None],
-        results[1][None],
-        *results[2:-1],
-        gains[0, :CHUNK],
-        gains[1, :CHUNK],
-        gains[2, :2],
-        gains[3, :2],
+        output[None],
+        input_grad[None],
+        query,
+        key,
+        value,
+        out.T,
+        gate,
+        up,
+        down.T,
+        *(gain[0] for gain in gains),
     )
 
 

time: 166 us -> 155 us (0.934)
  local copies, waits for them, and re-layouts: 8.97 us -> 0 us
  Pallas kernels: 155 us -> 153 us
    unnamed x2 -> x0, local copies, waits for them, and re-layouts: 3.85 us -> none
    squeeze x2 -> x0, local copies, waits for them, and re-layouts: 2.56 us -> none  [the longest x1 1.28 us: shards(): gains[1, :CHUNK]]
    broadcast_in_dim x2 -> x0, local copies, waits for them, and re-layouts: 2.55 us -> none  [the longest x1 1.28 us: shards(): attention_gain[None]]
    pallas_call x1, Pallas kernels: 4.72 us -> 2.57 us  [finish(): pl.pallas_call(finish_kernel, out_shape=[jax.ShapeDtypeStruct(shape, kind...]
where the time goes in v5:
time: 155 us; the launch traced here: 154 us
  Pallas kernels  153 us (99%)
    pallas_call x1, Pallas kernels, layer(): pl.pallas_call(functools.partial(layer_kernel, early_streams, late_stream...  150 us

profile of v5, /device:TPU:0, one launch (start us, length us, event | category | flops | bytes accessed | tf_op | source)
XLA Modules:
  0.0 154.4 jit_solution(13138593726727030097)
XLA Ops:
  0.7 0.6 maximum_bitcast_fusion.refs_4_
  1.2 150.5 %shard_map.246 = (bf16[256,1024]{1,0:T(8,128)(2,1)}, bf16[256,1024]{1,0:T(8,128)(2,1)}, f32[16,5632]{1,0:T(8,128)}, f32[16,2048]{1,0:T(8,128)}, f32[8,1024]{1,0:T(8,128)}) custom-call(bf16[256,1024]{1,0:T(8,128)(2,1)} %bitcast.12, bf16[256,1024]{1,0:T(8,128)(2,1)} %bitcast.13, s32[1,256]{1,0:T(1,128)} %refs_2_.1, s32[1,256]{1,0:T(1,128)} %refs_3_.1, ...), custom_call_target="tpu_custom_call" | custom-call | tf_op jit(solution)/shard_map/pallas_call | solution.py:819
  151.7 2.6 %shard_map.247 = (bf16[256,1024]{1,0:T(8,128)(2,1)}, bf16[256,1024]{1,0:T(8,128)(2,1)}, f32[16,1024]{1,0:T(8,128)}, f32[16,512]{1,0:T(8,128)}, f32[16,512]{1,0:T...) custom-call(bf16[256,1024]{1,0:T(8,128)(2,1)} %get-tuple-element.31., ...), custom_call_target="tpu_custom_call" | custom-call | tf_op jit(solution)/shard_map/pallas_call | solution.py:931
  (1 shorter events, 0.0 us)

commit v6 on v5

--- a/solution.py
+++ b/solution.py
@@ -65,9 +65,9 @@
 EARLY_ORDERS = (
     ("core", "x3", "x1", "y3", "z", "y1"),
     ("core", "x1", "x3", "y1", "z", "y3"),
-    ("core", "y3", "x3", "x1", "z", "y1"),
+    ("core", "y3", "z", "x3", "x1", "y1"),
     ("core", "y1", "x1", "x3", "z", "y3"),
-    ("core", "z", "y3", "x1", "x3", "y1"),
+    ("core", "z", "x1", "x3", "y3", "y1"),
 )
 LATE_ORDERS = (
     ("core", "x3", "x1", "y3", "y1", "z"),

time: 155 us -> 153 us (0.987)
  Pallas kernels: 153 us -> 151 us
    pallas_call x1, Pallas kernels: 150 us -> 149 us  [layer(): pl.pallas_call(functools.partial(layer_kernel, early_streams, late_stream...]
where the time goes in v6:
time: 153 us; the launch traced here: 152 us
  Pallas kernels  151 us (99%)
    pallas_call x1, Pallas kernels, layer(): pl.pallas_call(functools.partial(layer_kernel, early_streams, late_stream...  149 us

profile of v6, /device:TPU:0, one launch (start us, length us, event | category | flops | bytes accessed | tf_op | source)
XLA Modules:
  0.0 152.5 jit_solution(10716316152513817036)
XLA Ops:
  0.7 0.6 maximum_bitcast_fusion.refs_4_
  1.2 148.5 %shard_map.246 = (bf16[256,1024]{1,0:T(8,128)(2,1)}, bf16[256,1024]{1,0:T(8,128)(2,1)}, f32[16,5632]{1,0:T(8,128)}, f32[16,2048]{1,0:T(8,128)}, f32[8,1024]{1,0:T(8,128)}) custom-call(bf16[256,1024]{1,0:T(8,128)(2,1)} %bitcast.12, bf16[256,1024]{1,0:T(8,128)(2,1)} %bitcast.13, s32[1,256]{1,0:T(1,128)} %refs_2_.1, s32[1,256]{1,0:T(1,128)} %refs_3_.1, ...), custom_call_target="tpu_custom_call" | custom-call | tf_op jit(solution)/shard_map/pallas_call | solution.py:819
  149.8 2.6 %shard_map.247 = (bf16[256,1024]{1,0:T(8,128)(2,1)}, bf16[256,1024]{1,0:T(8,128)(2,1)}, f32[16,1024]{1,0:T(8,128)}, f32[16,512]{1,0:T(8,128)}, f32[16,512]{1,0:T...) custom-call(bf16[256,1024]{1,0:T(8,128)(2,1)} %get-tuple-element.31., ...), custom_call_target="tpu_custom_call" | custom-call | tf_op jit(solution)/shard_map/pallas_call | solution.py:931
  (1 shorter events, 0.0 us)
